TPU v7x, 512 devices: a whole 4x4x16 slice. The times are simulated.
512 devices in a mesh: gx: 32 (over z, core), gy: 16 (over y, x).
Axes of the slice: x: 4, y: 4, z: 16, core: 2. Of those that a mesh axis runs over, the one named last changes fastest.
Arguments:
- load_cases: bfloat16 [32, 16, 1024, 128], P('gx', 'gy')
- schur_blocks: bfloat16 [32, 16, 1024, 1024], P('gx', 'gy'), as said below
- local_inverse: bfloat16 [32, 16, 1024, 1024], P('gx', 'gy'), as said below
- coarse_basis: bfloat16 [32, 16, 8, 1024], P('gx', 'gy'), may hold values from -0.375 to 0.375
- corner_ids: int32 [32, 16, 8], P('gx', 'gy'), may hold values from 0 to 1023, as said below
- coarse_inverse: bfloat16 [1024, 1024], P('gy'), as said below
Outputs:
- solution_field: bfloat16 [32, 16, 1024, 128], P('gx', 'gy')
- residual: bfloat16 [32, 16, 1024, 128], P('gx', 'gy')
Inputs may be any that keep to these rules, and one draw needn't show every extreme that they name: `corner_ids`: coarse unknowns sit at grid vertices, 2 to a vertex, vertices and components numbered by one fixed permutation. Slot k of subdomain (a, b) names component k mod 2 of vertex ((a + c // 2) mod 32, (b + c mod 2) mod 16) with c = k // 2; so every coarse unknown is named by exactly 4 subdomains. `schur_blocks`: every subdomain block is symmetric. `local_inverse`: symmetric per subdomain. `coarse_inverse`: Symmetric.
All inputs are finite; a program needn't handle non-finite values.
Results may differ from a plain program's by a relative error of at most 0.01.
The roundings to bfloat16 on the way count: a program that leaves them out, or rounds other values in their place, can miss the bound.
Values may be sent and summed in bfloat16 or wider, within the bound.
No kernel may reach another device: no remote copies, remote signals or barrier semaphores. Data moves between devices by JAX's collectives and lax.ppermute only.
A program may use at most 64 MiB of HBM per device.

v0:
```python
import jax
import jax.numpy as jnp
from jax import lax
from jax.sharding import PartitionSpec as P

ITERS = 3


def padded(value, sides, width):
    for axis, dim in sides:
        devices, length = (lax.axis_size(axis), value.shape[dim])
        up = [(i, (i + 1) % devices) for i in range(devices - 1)]
        down = [(j, i) for i, j in up]
        last = lax.slice_in_dim(value, length - width, length, axis=dim)
        first = lax.slice_in_dim(value, 0, width, axis=dim)
        before = lax.ppermute(last, axis, up)
        after = lax.ppermute(first, axis, down)
        value = jnp.concatenate([before, value, after], axis=dim)
    return value


def face_weights(rows):
    first = lax.axis_index("gx")
    second = lax.axis_index("gy")
    count_x = lax.axis_size("gx")
    count_y = lax.axis_size("gy")
    values = [
        jnp.where(first > 0, 0.5, 1.0),
        jnp.where(first < count_x - 1, 0.5, 1.0),
        jnp.where(second > 0, 0.5, 1.0),
        jnp.where(second < count_y - 1, 0.5, 1.0),
    ]
    return jnp.concatenate(
        [jnp.ones((rows, 1), jnp.float32) * value.astype(jnp.float32) for value in values], axis=0
    )


def assemble(shares):
    rows = shares.shape[0] // 4
    low_x = shares[:rows]
    high_x = shares[rows : 2 * rows]
    low_y = shares[2 * rows : 3 * rows]
    high_y = shares[3 * rows :]
    padded_x = padded(jnp.stack([low_x, high_x]), (("gx", 0),), 1)
    padded_y = padded(jnp.stack([low_y, high_y]), (("gy", 0),), 1)
    extra = jnp.concatenate([padded_x[0], padded_x[3], padded_y[0], padded_y[3]], axis=0)
    return shares.astype(jnp.float32) + extra.astype(jnp.float32)


def body(load_cases, schur_blocks, local_inverse, coarse_basis, corner_ids, coarse_inverse):
    schur_block = schur_blocks[0, 0]
    inverse_block = local_inverse[0, 0]
    basis = coarse_basis[0, 0]
    corner_rows = corner_ids[0, 0]
    order = schur_block.shape[0]
    weight = face_weights(order // 4)
    coarse_count = coarse_inverse.shape[1]
    onehot = jnp.arange(coarse_count, dtype=jnp.int32)[:, None] == corner_rows[None, :]
    scatter_table = onehot.astype(jnp.float32)
    pick_table = onehot.T.astype(jnp.bfloat16)

    def inner(first, second):
        return lax.psum(jnp.sum(weight * first * second, axis=0), ("gx", "gy"))

    def precondition(remainder):
        scaled = (weight * remainder).astype(jnp.bfloat16)
        local_part = jnp.dot(inverse_block, scaled, preferred_element_type=jnp.float32)
        coarse_terms = jnp.dot(basis, scaled, preferred_element_type=jnp.float32)
        spread_terms = jnp.dot(scatter_table, coarse_terms, precision=lax.Precision.HIGHEST)
        coarse_total = lax.psum(spread_terms, ("gx", "gy"))
        row_solution = jnp.dot(
            coarse_inverse, coarse_total.astype(jnp.bfloat16), preferred_element_type=jnp.float32
        ).astype(jnp.bfloat16)
        coarse_solution = lax.all_gather(row_solution, "gy", axis=0, tiled=True)
        picked = jnp.dot(pick_table, coarse_solution, preferred_element_type=jnp.float32).astype(
            jnp.bfloat16
        )
        coarse_part = lax.dot_general(
            basis, picked, (((0,), (0,)), ((), ())), preferred_element_type=jnp.float32
        )
        blended = (weight * (local_part + coarse_part)).astype(jnp.bfloat16)
        return assemble(blended)

    residual = load_cases[0, 0].astype(jnp.float32)
    solution_field = jnp.zeros_like(residual)
    search = precondition(residual)
    direction = search
    rz_now = inner(residual, search)
    for iteration in range(ITERS):
        schur_part = jnp.dot(
            schur_block, direction.astype(jnp.bfloat16), preferred_element_type=jnp.float32
        )
        product = assemble(schur_part.astype(jnp.bfloat16))
        alpha = rz_now / inner(direction, product)
        solution_field = solution_field + alpha * direction
        residual = residual - alpha * product
        if iteration + 1 < ITERS:
            search = precondition(residual)
            rz_next = inner(residual, search)
            direction = search + rz_next / rz_now * direction
            rz_now = rz_next
    return (
        solution_field.astype(jnp.bfloat16)[None, None],
        residual.astype(jnp.bfloat16)[None, None],
    )


def solution(mesh):
    return jax.shard_map(
        body,
        mesh=mesh,
        in_specs=(
            P("gx", "gy", None, None),
            P("gx", "gy", None, None),
            P("gx", "gy", None, None),
            P("gx", "gy", None, None),
            P("gx", "gy", None),
            P("gy", None),
        ),
        out_specs=(P("gx", "gy", None, None), P("gx", "gy", None, None)),
        check_vma=False,
    )
```

profile of v0, /device:TPU:1, one launch (start us, length us, event | category | flops | bytes accessed | tf_op | source)
XLA Modules:
  0.0 1028.8 jit_solution(18158077037069612653)
XLA Ops:
  0.8 1.2 copy.14
  2.0 0.9 fusion.69
  2.9 1.0 fusion.49
  4.0 113.4 %all-reduce.4 = bf16[1024,128]{1,0:T(8,128)(2,1)S(1)} all-reduce(f32[1024,128]{1,0:T(8,128)S(1)} %fusion.49), channel_id=1, replica_groups=mesh['gx'=32,'gy'=16] {'gx','gy'}, use_global_device_ids=true, to_apply=%region_0.1 | all-reduce | flops 131072 | bytes 786432 | tf_op jit(solution)/shard_map/psum | solution.py:70
  117.6 18.6 %all_gather.9 = bf16[1024,128]{1,0:T(8,128)(2,1)S(1)} all-gather(bf16[64,128]{1,0:T(8,128)(2,1)S(1)} %fusion.39), channel_id=1, replica_groups=mesh['gx'=32,'gy'=16] {'gy'}, dimensions={0}, use_global_device_ids=true | all-gather | bytes 278528 | tf_op jit(solution)/shard_map/all_gather | solution.py:74
  137.0 1.3 fusion.38
  138.3 6.0 collective-permute-start
  144.4 1.3 collective-permute-start.3
  145.7 4.0 collective-permute-start.2
  149.6 1.9 collective-permute-start.1
  151.6 3.6 collective-permute-done.1
  155.2 2.4 fusion.33
  157.7 1.9 collective-permute-start.4
  159.6 1.3 collective-permute-start.7
  160.9 4.0 collective-permute-start.6
  164.9 3.0 collective-permute-start.5
  168.0 2.5 collective-permute-done.5
  171.1 106.8 %all-reduce = (f32[128]{0:T(128)S(1)}, f32[128]{0:T(128)S(1)}) all-reduce(f32[128]{0:T(128)S(1)} %get-tuple-element.9, f32[128]{0:T(128)S(1)} %get-tuple-element.8), channel_id=1, replica_groups=mesh['gx'=32,'gy'=16] {'gx','gy'}, use_global_device_ids=true, to_apply=%region_2.3 | all-reduce | flops 256 | bytes 2048 | tf_op jit(solution)/shard_map/psum | solution.py:63
  278.4 1.1 fusion.42
  279.5 0.9 fusion.72
  280.4 1.6 fusion.8
  282.4 103.7 %all-reduce.5 = bf16[1024,128]{1,0:T(8,128)(2,1)} all-reduce(f32[1024,128]{1,0:T(8,128)S(1)} %fusion.48), channel_id=1, replica_groups=mesh['gx'=32,'gy'=16] {'gx','gy'}, use_global_device_ids=true, to_apply=%region_5.6 | all-reduce | flops 131072 | bytes 786432 | tf_op jit(solution)/shard_map/psum | solution.py:70
  386.1 1.1 fusion.40
  387.3 17.1 %all_gather.10 = bf16[1024,128]{1,0:T(8,128)(2,1)S(1)} all-gather(bf16[64,128]{1,0:T(8,128)(2,1)S(1)} %fusion.40), channel_id=1, replica_groups=mesh['gx'=32,'gy'=16] {'gy'}, dimensions={0}, use_global_device_ids=true | all-gather | bytes 278528 | tf_op jit(solution)/shard_map/all_gather | solution.py:74
  404.4 1.6 fusion.37
  406.0 8.8 collective-permute-start.8
  414.8 1.3 collective-permute-start.11
  416.1 4.0 collective-permute-start.10
  420.1 1.9 collective-permute-start.9
  422.1 3.6 collective-permute-done.9
  425.9 101.5 %psum.67 = f32[128]{0:T(128)S(1)} all-reduce(f32[128]{0:T(128)S(1)} %multiply_reduce_fusion.3), channel_id=1, replica_groups=mesh['gx'=32,'gy'=16] {'gx','gy'}, use_global_device_ids=true, to_apply=%region_7.8 | all-reduce | flops 128 | bytes 1024 | tf_op jit(solution)/shard_map/psum | solution.py:63
  528.6 1.1 multiply_add_fusion.1
  529.6 2.4 fusion.30
  532.1 3.0 collective-permute-start.12
  535.1 1.3 collective-permute-start.15
  536.4 4.0 collective-permute-start.14
  540.4 1.9 collective-permute-start.13
  542.4 3.6 collective-permute-done.13
  546.2 103.3 %psum.68 = f32[128]{0:T(128)S(1)} all-reduce(f32[128]{0:T(128)S(1)} %multiply_reduce_fusion.2), channel_id=1, replica_groups=mesh['gx'=32,'gy'=16] {'gx','gy'}, use_global_device_ids=true, to_apply=%region_9.10 | all-reduce | flops 128 | bytes 1024 | tf_op jit(solution)/shard_map/psum | solution.py:63
  650.2 1.2 multiply_subtract_fusion
  651.3 0.9 fusion.73
  652.2 1.6 fusion.6
  653.9 1.2 fusion.47
  655.1 102.7 %all-reduce.6 = bf16[1024,128]{1,0:T(8,128)(2,1)S(1)} all-reduce(f32[1024,128]{1,0:T(8,128)} %fusion.47), channel_id=1, replica_groups=mesh['gx'=32,'gy'=16] {'gx','gy'}, use_global_device_ids=true, to_apply=%region_10.11 | all-reduce | flops 131072 | bytes 786432 | tf_op jit(solution)/shard_map/psum | solution.py:70
  757.9 19.4 %all_gather.11 = bf16[1024,128]{1,0:T(8,128)(2,1)} all-gather(bf16[64,128]{1,0:T(8,128)(2,1)S(1)} %fusion.41), channel_id=1, replica_groups=mesh['gx'=32,'gy'=16] {'gy'}, dimensions={0}, use_global_device_ids=true | all-gather | bytes 278528 | tf_op jit(solution)/shard_map/all_gather | solution.py:74
  777.3 1.7 fusion.36
  779.0 8.4 collective-permute-start.16
  787.5 1.3 collective-permute-start.19
  788.8 4.0 collective-permute-start.18
  792.8 1.9 collective-permute-start.17
  794.8 3.6 collective-permute-done.17
  799.2 101.5 %psum.70 = f32[128]{0:T(128)} all-reduce(f32[128]{0:T(128)S(1)} %multiply_reduce_fusion.1), channel_id=1, replica_groups=mesh['gx'=32,'gy'=16] {'gx','gy'}, use_global_device_ids=true, to_apply=%region_12.13 | all-reduce | flops 128 | bytes 1024 | tf_op jit(solution)/shard_map/psum | solution.py:63
  901.4 2.5 fusion.27
  904.0 3.0 collective-permute-start.20
  906.9 1.3 collective-permute-start.23
  908.2 4.0 collective-permute-start.22
  912.2 1.9 collective-permute-start.21
  914.2 3.6 collective-permute-done.21
  918.5 0.9 multiply_reduce_fusion
  919.3 103.0 %psum.71 = f32[128]{0:T(128)} all-reduce(f32[128]{0:T(128)} %multiply_reduce_fusion), channel_id=1, replica_groups=mesh['gx'=32,'gy'=16] {'gx','gy'}, use_global_device_ids=true, to_apply=%region_14.15 | all-reduce | flops 128 | bytes 1024 | tf_op jit(solution)/shard_map/psum | solution.py:63
  1023.0 2.0 fusion.52
  1025.1 1.1 fusion.53
  1026.2 0.8 copy.16
  1027.0 1.8 copy.15
  (102 shorter events, 7.9 us)
Async XLA Ops:
  0.6 135.6 %copy-start = (bf16[1,1,1024,1024]{3,2,1,0:T(8,128)(2,1)S(1)}, bf16[1,1,1024,1024]{3,2,1,0:T(8,128)(2,1)}, u32[]{:S(2)}) copy-start(bf16[1,1,1024,1024]{3,2,1,0:T(8,128)(2,1)} %param.8) | copy-start | bytes 6291460
  0.6 116.8 %copy-start.4 = (bf16[64,1024]{1,0:T(8,128)(2,1)S(1)}, bf16[64,1024]{1,0:T(8,128)(2,1)}, u32[]{:S(2)}) copy-start(bf16[64,1024]{1,0:T(8,128)(2,1)} %param.11) | copy-start | bytes 393220
  4.0 133.1 %copy-start.25 = (s32[1,1,8]{2,1,0:T(1,128)S(1)}, s32[1,1,8]{2,1,0:T(1,128)}, u32[]{:S(2)}) copy-start(s32[1,1,8]{2,1,0:T(1,128)} %param.10) | copy-start | bytes 100
  138.3 390.2 %copy-start.2 = (bf16[1024,128]{0,1:T(8,128)(2,1)}, bf16[1024,128]{0,1:T(8,128)(2,1)S(1)}, u32[]{:S(2)}) copy-start(bf16[1024,128]{0,1:T(8,128)(2,1)S(1)} %fusion.38) | copy-start | bytes 786436
  138.3 13.2 %collective-permute-start = (bf16[1,256,128]{1,2,0:T(8,128)(2,1)S(1)}, bf16[1,256,128]{1,2,0:T(8,128)(2,1)S(1)}, u32[]{:S(2)}, u32[]{:S(2)}) collective-permute-start(bf16[1,256,128]{1,2,0:T(8,128)(2,1)S(1)} %get-tuple-element.32), channel_id=1, source_target_pairs={{0,16},{16,32},{32,48},{48,64},{64,80},{80,96},{96,112},{112,128},... | collective-permute-start | bytes 196616 | tf_op jit(solution)/shard_map/ppermute | solution.py:16
  144.4 7.2 collective-permute-start.3
  145.7 6.0 collective-permute-start.2
  149.6 5.6 collective-permute-start.1
  151.6 19.3 %copy-start.9 = (bf16[1,256,128]{1,2,0:T(8,128)(2,1)}, bf16[1,256,128]{1,2,0:T(8,128)(2,1)S(1)}, u32[]{:S(2)}) copy-start(bf16[1,256,128]{1,2,0:T(8,128)(2,1)S(1)} %collective-permute-done) | copy-start | bytes 196612
  151.6 19.2 %copy-start.10 = (bf16[1,256,128]{1,2,0:T(8,128)(2,1)}, bf16[1,256,128]{1,2,0:T(8,128)(2,1)S(1)}, u32[]{:S(2)}) copy-start(bf16[1,256,128]{1,2,0:T(8,128)(2,1)S(1)} %collective-permute-done.3) | copy-start | bytes 196612
  151.6 19.2 %copy-start.11 = (bf16[1,256,128]{1,2,0:T(8,128)(2,1)}, bf16[1,256,128]{1,2,0:T(8,128)(2,1)S(1)}, u32[]{:S(2)}) copy-start(bf16[1,256,128]{1,2,0:T(8,128)(2,1)S(1)} %collective-permute-done.2) | copy-start | bytes 196612
  155.2 15.6 %copy-start.12 = (bf16[1,256,128]{1,2,0:T(8,128)(2,1)}, bf16[1,256,128]{1,2,0:T(8,128)(2,1)S(1)}, u32[]{:S(2)}) copy-start(bf16[1,256,128]{1,2,0:T(8,128)(2,1)S(1)} %collective-permute-done.1) | copy-start | bytes 196612
  157.7 10.2 collective-permute-start.4
  159.6 8.3 collective-permute-start.7
  160.9 7.0 collective-permute-start.6
  164.9 5.6 collective-permute-start.5
  167.9 2.9 copy-start.13
  167.9 2.9 copy-start.14
  168.0 2.9 copy-start.15
  170.5 0.6 copy-start.16
  277.9 0.5 copy-start.27
  279.5 146.3 %copy-start.1 = (f32[1024,128]{0,1:T(8,128)}, f32[1024,128]{0,1:T(8,128)S(1)}, u32[]{:S(2)}) copy-start(f32[1024,128]{0,1:T(8,128)S(1)} %fusion.42) | copy-start | bytes 1572868
  406.0 16.0 %collective-permute-start.8 = (bf16[1,256,128]{1,2,0:T(8,128)(2,1)S(1)}, bf16[1,256,128]{1,2,0:T(8,128)(2,1)S(1)}, u32[]{:S(2)}, u32[]{:S(2)}) collective-permute-start(bf16[1,256,128]{1,2,0:T(8,128)(2,1)S(1)} %get-tuple-element.24), channel_id=1, source_target_pairs={{0,16},{16,32},{32,48},{48,64},{64,80},{80,96},{96,112},{112,128},... | collective-permute-start | bytes 196616 | tf_op jit(solution)/shard_map/ppermute | solution.py:16
  414.8 7.2 collective-permute-start.11
  416.1 5.9 collective-permute-start.10
  420.1 5.6 collective-permute-start.9
  527.4 0.6 copy-start.26
  532.1 10.3 collective-permute-start.12
  535.1 7.2 collective-permute-start.15
  536.4 6.0 collective-permute-start.14
  540.4 5.6 collective-permute-start.13
  542.4 107.1 %copy-start.21 = (bf16[1,256,128]{1,2,0:T(8,128)(2,1)}, bf16[1,256,128]{1,2,0:T(8,128)(2,1)S(1)}, u32[]{:S(2)}) copy-start(bf16[1,256,128]{1,2,0:T(8,128)(2,1)S(1)} %collective-permute-done.12) | copy-start | bytes 196612
  542.4 107.1 %copy-start.22 = (bf16[1,256,128]{1,2,0:T(8,128)(2,1)}, bf16[1,256,128]{1,2,0:T(8,128)(2,1)S(1)}, u32[]{:S(2)}) copy-start(bf16[1,256,128]{1,2,0:T(8,128)(2,1)S(1)} %collective-permute-done.15) | copy-start | bytes 196612
  542.4 107.1 %copy-start.23 = (bf16[1,256,128]{1,2,0:T(8,128)(2,1)}, bf16[1,256,128]{1,2,0:T(8,128)(2,1)S(1)}, u32[]{:S(2)}) copy-start(bf16[1,256,128]{1,2,0:T(8,128)(2,1)S(1)} %collective-permute-done.14) | copy-start | bytes 196612
  546.0 103.5 %copy-start.24 = (bf16[1,256,128]{1,2,0:T(8,128)(2,1)}, bf16[1,256,128]{1,2,0:T(8,128)(2,1)S(1)}, u32[]{:S(2)}) copy-start(bf16[1,256,128]{1,2,0:T(8,128)(2,1)S(1)} %collective-permute-done.13) | copy-start | bytes 196612
  779.0 15.7 %collective-permute-start.16 = (bf16[1,256,128]{1,2,0:T(8,128)(2,1)S(1)}, bf16[1,256,128]{1,2,0:T(8,128)(2,1)S(1)}, u32[]{:S(2)}, u32[]{:S(2)}) collective-permute-start(bf16[1,256,128]{1,2,0:T(8,128)(2,1)S(1)} %get-tuple-element.16), channel_id=1, source_target_pairs={{0,16},{16,32},{32,48},{48,64},{64,80},{80,96},{96,112},{112,128},... | collective-permute-start | bytes 196616 | tf_op jit(solution)/shard_map/ppermute | solution.py:16
  787.5 7.2 collective-permute-start.19
  788.8 5.9 collective-permute-start.18
  792.8 5.6 collective-permute-start.17
  794.7 3.6 copy-start.5
  798.4 0.6 copy-start.7
  900.7 17.8 %copy-start.6 = (bf16[1,256,128]{1,2,0:T(8,128)(2,1)S(1)}, bf16[1,256,128]{1,2,0:T(8,128)(2,1)}, u32[]{:S(2)}) copy-start(bf16[1,256,128]{1,2,0:T(8,128)(2,1)} %copy-done.5) | copy-start | bytes 196612
  900.7 17.8 %copy-start.8 = (bf16[1,256,128]{1,2,0:T(8,128)(2,1)S(1)}, bf16[1,256,128]{1,2,0:T(8,128)(2,1)}, u32[]{:S(2)}) copy-start(bf16[1,256,128]{1,2,0:T(8,128)(2,1)} %copy-done.7) | copy-start | bytes 196612
  903.9 13.9 %copy-start.3 = (bf16[1024,128]{0,1:T(8,128)(2,1)}, bf16[1024,128]{0,1:T(8,128)(2,1)S(1)}, u32[]{:S(2)}) copy-start(bf16[1024,128]{0,1:T(8,128)(2,1)S(1)} %fusion.27) | copy-start | bytes 786436
  904.0 10.2 collective-permute-start.20
  906.9 7.3 collective-permute-start.23
  908.2 6.0 collective-permute-start.22
  912.2 5.6 collective-permute-start.21
  914.2 3.6 copy-start.17
  914.2 3.6 copy-start.18
  914.2 3.6 copy-start.19
  917.8 0.6 copy-start.20
where the time goes:
time: 1030 us
  blocking collectives  891 us (87%)
  starting transfers between devices  75.4 us (7%)
  matrix products  22.8 us (2%)
  waiting for transfers between devices  20.6 us (2%)
  other arithmetic  10.9 us (1%)
    psum x5, blocking collectives, inner(): return lax.psum(jnp.sum(weight * first * second, axis=0), ('gx', 'gy'))  516 us
    psum x3, blocking collectives, precondition(): coarse_total = lax.psum(spread_terms, ('gx', 'gy'))  320 us
    all_gather x3, blocking collectives, precondition(): coarse_solution = lax.all_gather(row_solution, 'gy', axis=0, tiled=True)  55.1 us
    ppermute x12, starting transfers between devices, padded(): before = lax.ppermute(last, axis, up)  55.1 us
  transfers between devices with their start and end apart: 24, of which 6 were waited for; matrix products, arithmetic and copies ran while one was open for 0% of the time, Pallas kernels for 0%

commit v1 on v0

v1 whole, which is shorter than its diff:
```python
import jax
import jax.numpy as jnp
from jax import lax
from jax.experimental import pallas as pl
from jax.experimental.pallas import tpu as pltpu
from jax.sharding import PartitionSpec as P

F32 = jnp.float32
BF16 = jnp.bfloat16
NI = 1024
FACE = 256
R = 128
NX = 32
NY = 16
SL = R // NY
NCG = 1024
WIN = 32

VMEM = pl.BlockSpec(memory_space=pltpu.VMEM)
SMEM = pl.BlockSpec(memory_space=pltpu.SMEM)


def call(kernel, args, outs, scratch=(), smem=0, flops=0):
    size = sum(a.size * a.dtype.itemsize for a in args)
    return pl.pallas_call(
        kernel,
        out_shape=tuple(jax.ShapeDtypeStruct(s, d) for s, d in outs),
        in_specs=[SMEM] * smem + [VMEM] * (len(args) - smem),
        out_specs=tuple(VMEM for _ in outs),
        scratch_shapes=list(scratch),
        compiler_params=pltpu.CompilerParams(vmem_limit_bytes=32 * 1024 * 1024),
        cost_estimate=pl.CostEstimate(flops=flops, bytes_accessed=size, transcendentals=0),
    )(*args)


def rows(i):
    return slice(FACE * i, FACE * (i + 1))


def dot(a, b):
    return jnp.dot(a, b, preferred_element_type=F32)


def lanes(shape):
    return lax.broadcasted_iota(jnp.int32, shape, len(shape) - 1)


def rolled(value, shift):
    shift = shift % 128
    return value if shift == 0 else pltpu.roll(value, shift, value.ndim - 1)


def total(value):
    return jnp.sum(value, axis=0, keepdims=True)


def start_kernel(wt, ids, load, inverse, basis, own, l_out, f0, f1, f2, f3, msg_out, table):
    scaled = [(load[rows(i)].astype(F32) * wt[i]).astype(BF16) for i in range(4)]
    scaled = jnp.concatenate(scaled, axis=0)
    for i, face in enumerate((f0, f1, f2, f3)):
        local = wt[i] * dot(inverse[rows(i)], scaled)
        l_out[rows(i)] = local
        face[0:FACE] = local
        face[FACE : FACE + 8] = basis[:, FACE * i : FACE * i + 128].astype(F32)
        face[FACE + 8 : FACE + 16] = basis[:, FACE * i + 128 : FACE * (i + 1)].astype(F32)
    table[...] = jnp.zeros((128, 128), F32)
    table[0:WIN] = dot(own[...], scaled)
    for c in range(2):
        table[64 + c : 65 + c] = jnp.full((1, 128), ids[c].astype(F32))
    msg_out[...] = jnp.transpose(table[...]).reshape(NY, SL, 128)


def place(out, base, column, piece, dx0, dy0):
    width = piece.shape[1]
    for cx in range(2):
        for cy in range(2):
            row = base + (dy0 + cy) * 8 + (dx0 + cx) * 2
            slot = 4 * cx + 2 * cy
            out[row : row + 2, column : column + width] = piece[slot : slot + 2]


def window_kernel(basis, f0, f1, f2, f3, b_out, bt_out, table):
    table[...] = jnp.zeros((2 * WIN, NI), F32)
    place(table, 0, 0, basis[...].astype(F32), 1, 1)
    for i, (face, dx0, dy0) in enumerate(((f0, 0, 1), (f1, 2, 1), (f2, 1, 0), (f3, 1, 2))):
        for h in range(2):
            piece = face[FACE + 8 * h : FACE + 8 * h + 8]
            place(table, WIN, FACE * i + 128 * h, piece, dx0, dy0)
    b_out[...] = table[...].astype(BF16)
    bt_out[...] = jnp.transpose(table[...]).astype(BF16)


def local_kernel(wt, s, f0, f1, f2, f3, inverse, q_out, l_out, g0, g1, g2, g3):
    parts = []
    for i, face in enumerate((f0, f1, f2, f3)):
        q = s[rows(i)].astype(F32) + face[...].astype(F32)
        q_out[rows(i)] = q
        parts.append((wt[i] * q).astype(BF16))
    scaled = jnp.concatenate(parts, axis=0)
    for i, face in enumerate((g0, g1, g2, g3)):
        local = wt[i] * dot(inverse[rows(i)], scaled)
        l_out[rows(i)] = local
        face[...] = local


def arrived(m):
    return jnp.transpose(m[...].reshape(R, 128))


def blended(wt, i, window_t, y, mine, facing):
    y = y[0:WIN].astype(BF16)
    mine = mine + wt[i] * dot(window_t[rows(i), 0:WIN], y)
    facing = facing + wt[i] * dot(window_t[rows(i), WIN:], y)
    return mine.astype(BF16).astype(F32) + facing.astype(BF16).astype(F32)


def split(value):
    high = value.astype(BF16)
    return jnp.concatenate([high, (value - high.astype(F32)).astype(BF16)], axis=1)


def joined(value):
    return value[:, 0:R] + value[:, R:]


def apply_schur(schur, zb, s_out, faces):
    for i, face in enumerate(faces):
        s = joined(dot(schur[rows(i)], zb[...]))
        s_out[rows(i)] = s
        face[...] = s


def window_terms(wt, window, s):
    terms = jnp.zeros((2 * WIN, 2 * R), F32)
    for i in range(4):
        terms += dot(window[:, rows(i)], split(s[rows(i)].astype(F32) * wt[i]))
    return joined(terms[0:WIN] + terms[WIN:])


def send_table(table, msg_out, terms, inner):
    table[...] = jnp.zeros((128, 128), F32)
    table[0:WIN] = terms
    for j, value in enumerate(inner):
        table[WIN + j : WIN + j + 1] = value
    msg_out[...] = jnp.transpose(table[...]).reshape(NY, SL, 128)


def first_kernel(
    wt, m, l0, f0, f1, f2, f3, window_t, window, schur, load,
    z_out, s_out, g0, g1, g2, g3, msg_out, table, zb,
):
    y = arrived(m)
    for i, face in enumerate((f0, f1, f2, f3)):
        z = blended(wt, i, window_t, y, l0[rows(i)], face[0:FACE])
        z_out[rows(i)] = z
        zb[rows(i)] = z.astype(BF16)
    for i, face in enumerate((g0, g1, g2, g3)):
        s = dot(schur[rows(i)], zb[...]).astype(BF16)
        s_out[rows(i)] = s
        face[...] = s
    rz = jnp.zeros((1, R), F32)
    pq = jnp.zeros((1, R), F32)
    for i in range(4):
        z = z_out[rows(i)]
        rz += total(wt[i] * load[rows(i)].astype(F32) * z)
        pq += total(z * s_out[rows(i)].astype(F32))
    send_table(table, msg_out, window_terms(wt, window, s_out), (rz, pq))


def second_kernel(
    wt, m, l0, e0, e1, e2, e3, l1, f0, f1, f2, f3, q0, s0, window_t, window, schur, load,
    z_out, l_out, h0, h1, h2, h3, r_out, s_out, g0, g1, g2, g3, msg_out, got_out, table, zb,
):
    got = arrived(m)
    got_out[...] = got[WIN : WIN + 8]
    alpha = got[WIN : WIN + 1]
    faces = ((e0, f0, h0), (e1, f1, h1), (e2, f2, h2), (e3, f3, h3))
    for i, (before, face, after) in enumerate(faces):
        mine = l0[rows(i)] - alpha * l1[rows(i)]
        facing = before[0:FACE] - alpha * face[...]
        z = blended(wt, i, window_t, got, mine, facing)
        l_out[rows(i)] = mine
        after[...] = facing
        z_out[rows(i)] = z
        zb[rows(i)] = split(z)
        r_out[rows(i)] = load[rows(i)].astype(F32) - alpha * q0[rows(i)]
    apply_schur(schur, zb, s_out, (g0, g1, g2, g3))
    rz = jnp.zeros((1, R), F32)
    zz = jnp.zeros((1, R), F32)
    zq = jnp.zeros((1, R), F32)
    for i in range(4):
        z = z_out[rows(i)]
        rz += total(wt[i] * r_out[rows(i)] * z)
        zz += total(z * s_out[rows(i)])
        zq += total(z * s0[rows(i)].astype(F32))
    send_table(table, msg_out, window_terms(wt, window, s_out), (rz, zz, zq))


def third_kernel(
    wt, m, got0, lm, d0, d1, d2, d3, l1, e0, e1, e2, e3, l2, f0, f1, f2, f3,
    q0, q1, s0, s1, z0, z1, r1, window_t, schur,
    z_out, x_out, p_out, q_out, r_out, s_out, g0, g1, g2, g3, msg_out, got_out, zb,
):
    got = arrived(m)
    got_out[...] = got[WIN : WIN + 8]
    alpha0 = got0[0:1]
    alpha = got[WIN : WIN + 1]
    beta = got[WIN + 1 : WIN + 2]
    faces = ((d0, e0, f0), (d1, e1, f1), (d2, e2, f2), (d3, e3, f3))
    for i, (before, first, second) in enumerate(faces):
        mine = lm[rows(i)] - alpha * (l2[rows(i)] + beta * l1[rows(i)])
        facing = before[...] - alpha * (second[...] + beta * first[...])
        z = blended(wt, i, window_t, got, mine, facing)
        z_out[rows(i)] = z
        zb[rows(i)] = split(z)
        p = z1[rows(i)] + beta * z0[rows(i)]
        q = q1[rows(i)] + beta * q0[rows(i)]
        p_out[rows(i)] = p
        q_out[rows(i)] = q
        x_out[rows(i)] = alpha0 * z0[rows(i)] + alpha * p
        r_out[rows(i)] = r1[rows(i)] - alpha * q
    apply_schur(schur, zb, s_out, (g0, g1, g2, g3))
    rz = jnp.zeros((1, R), F32)
    zz = jnp.zeros((1, R), F32)
    zq = jnp.zeros((1, R), F32)
    for i in range(4):
        z = z_out[rows(i)]
        s = s1[rows(i)] + beta * s0[rows(i)].astype(F32)
        rz += total(wt[i] * r_out[rows(i)] * z)
        zz += total(z * s_out[rows(i)])
        zq += total(z * s)
    inner = jnp.concatenate([rz, zz, zq, jnp.zeros((5, R), F32)], axis=0)
    msg_out[...] = jnp.broadcast_to(inner[None], (NY, 8, R))


def last_kernel(m, got, s, f0, f1, f2, f3, z, p, q, x, r, x_out, r_out):
    inner = jnp.sum(m[...], axis=0)
    rz1 = got[2:3]
    pq1 = got[3:4]
    rz = inner[0:1]
    beta = rz / rz1
    pq = inner[1:2] + 2.0 * beta * inner[2:3] + beta * beta * pq1
    alpha = rz / pq
    for i, face in enumerate((f0, f1, f2, f3)):
        product = s[rows(i)] + face[...] + beta * q[rows(i)]
        direction = z[rows(i)] + beta * p[rows(i)]
        x_out[rows(i)] = (x[rows(i)] + alpha * direction).astype(BF16)
        r_out[rows(i)] = (r[rows(i)] - alpha * product).astype(BF16)


def column_kernel(m, out):
    where = lanes((SL, 128))
    column = jnp.zeros((SL, 128), F32)
    other = jnp.zeros((SL, 128), F32)
    for b in range(NY):
        value = m[b]
        column += rolled(jnp.where(where < WIN, value, 0.0), 8 * (b - 1))
        other += jnp.where((where >= WIN) & (where < 64), value, 0.0)
    both = jnp.concatenate([column, other], axis=0)
    out[...] = jnp.broadcast_to(both[None], (NX, 2 * SL, 128))


def first_column_kernel(m, out):
    where = lanes((SL, 128))
    column = jnp.zeros((SL, 128), F32)
    other = jnp.zeros((SL, 128), F32)
    for b in range(NY):
        value = m[b]
        column += rolled(jnp.where(where < WIN, value, 0.0), 8 * (b - 1))
        named = jnp.where((where >= 64) & (where < 66), value, 0.0)
        other += rolled(named, 8 * b - 64)
    both = jnp.concatenate([column, other], axis=0)
    out[...] = jnp.broadcast_to(both[None], (NX, 2 * SL, 128))


def vertex_sums(m, group):
    place_of = lanes((SL, 128)) % 8 // 2
    result = jnp.zeros((SL, 128), F32)
    for k in range(4):
        value = jnp.zeros((SL, 128), F32)
        for j in range(4):
            value += rolled(m[(4 * group + k - j + 1) % NX, 0:SL], 2 * (k - j))
        result += jnp.where(place_of == k, value, 0.0)
    return result


def reply(out, y, scalars):
    where = lanes((SL, 128))
    rest = jnp.zeros((SL, 128), F32)
    for j, value in enumerate(scalars):
        rest += jnp.where(where == WIN + j, value, 0.0)
    for b in range(NY):
        out[b] = jnp.where(where < WIN, rolled(y, -8 * (b - 1)), rest)


def solve(sums, table, out, scalars):
    y = dot(sums[...].astype(BF16), table[...])
    reply(out, y.astype(BF16).astype(F32), scalars)


def first_solve_kernel(ax, m, inverse, sums, table, out, picked, spread):
    for group in range(8):
        sums[:, 128 * group : 128 * (group + 1)] = vertex_sums(m, group)
    own = jnp.zeros((SL, 128), F32)
    for j in range(4):
        own += rolled(m[(ax[0] + j - 1 + NX) % NX, SL : 2 * SL], 2 * j)
    for i in range(4):
        number = lax.broadcasted_iota(jnp.int32, (FACE, 128), 0).astype(F32) + float(FACE * i)
        spread[rows(i), 0:128] = jnp.where(number == own[0:1], 1.0, 0.0).astype(BF16)
    for i in range(4):
        picked[rows(i)] = dot(inverse[rows(i)], spread[:, 0:128]).astype(BF16)
    lane = lanes((128, 128)).astype(F32)
    for group in range(8):
        named = jnp.zeros((SL, 128), F32)
        for k in range(4):
            named += rolled(m[4 * group + k, SL : 2 * SL], 2 * k)
        named = jnp.transpose(jnp.broadcast_to(named[0:1], (128, 128)))
        for part in range(8):
            spread[128 * group : 128 * (group + 1), 128 * part : 128 * (part + 1)] = jnp.where(
                named == lane + float(128 * part), 1.0, 0.0
            ).astype(BF16)
    for i in range(4):
        table[rows(i)] = dot(spread[rows(i)], picked[...]).astype(BF16)
    solve(sums, table, out, ())


def scalar(value, j):
    where = lanes((SL, 128))
    return jnp.sum(jnp.where(where == WIN + j, value, 0.0), axis=1, keepdims=True)


def second_solve_kernel(m, sums0, table, change, sums, kept, out):
    inner = jnp.sum(m[:, SL : 2 * SL], axis=0)
    rz, pq = (scalar(inner, 0), scalar(inner, 1))
    alpha = rz / pq
    for group in range(8):
        part = slice(128 * group, 128 * (group + 1))
        value = vertex_sums(m, group)
        change[:, part] = value
        sums[:, part] = sums0[:, part] - alpha * value
    kept[...] = jnp.where(lanes((SL, 128)) == 0, rz, pq)
    solve(sums, table, out, (alpha,))


def third_solve_kernel(m, sums1, table, change0, kept, out, sums):
    inner = jnp.sum(m[:, SL : 2 * SL], axis=0)
    rz, zz, zq = (scalar(inner, 0), scalar(inner, 1), scalar(inner, 2))
    beta = rz / kept[:, 0:1]
    pq = zz + 2.0 * beta * zq + beta * beta * kept[:, 1:2]
    alpha = rz / pq
    for group in range(8):
        part = slice(128 * group, 128 * (group + 1))
        value = vertex_sums(m, group) + beta * change0[:, part]
        sums[:, part] = sums1[:, part] - alpha * value
    solve(sums, table, out, (alpha, beta, rz, pq))


def last_column_kernel(m, out):
    out[...] = jnp.broadcast_to(jnp.sum(m[...], axis=0)[None], (NX, 8, R))


def across(faces):
    low_x, high_x, low_y, high_y = faces
    result = []
    for axis, size, low, high in (("gx", NX, low_x, high_x), ("gy", NY, low_y, high_y)):
        up = [(i, i + 1) for i in range(size - 1)]
        down = [(j, i) for i, j in up]
        result.append(lax.ppermute(high, axis, up))
        result.append(lax.ppermute(low, axis, down))
    return result


def swap(value, axis):
    return lax.all_to_all(value, axis, 0, 0, tiled=True)


def body(load_cases, schur_blocks, local_inverse, coarse_basis, corner_ids, coarse_inverse):
    load = load_cases[0, 0]
    schur = schur_blocks[0, 0]
    inverse = local_inverse[0, 0]
    basis = coarse_basis[0, 0]
    ids = corner_ids[0, 0]
    ax = lax.axis_index("gx")
    ay = lax.axis_index("gy")
    shared = jnp.stack([ax > 0, ax < NX - 1, ay > 0, ay < NY - 1])
    wt = jnp.where(shared, 0.5, 1.0).astype(F32)
    gap = jnp.zeros((10, NI), BF16)
    own = jnp.concatenate(
        [gap, basis[0:2], basis[4:6], gap[0:4], basis[2:4], basis[6:8], gap], axis=0
    )
    copies = jnp.broadcast_to(coarse_inverse[None], (NY, NCG // NY, NCG))
    whole = swap(copies, "gy").reshape(NCG, NCG)

    tall = (NI, R)
    msg = ((NY, SL, 128), F32)
    wide = ((NX, 2 * SL, 128), F32)
    block = 2 * NI * NI * R
    table = pltpu.VMEM((128, 128), F32)
    zb = pltpu.VMEM((NI, 2 * R), BF16)
    face = ((FACE, R), F32)
    l0, f0, f1, f2, f3, m = call(
        start_kernel,
        (wt, ids, load, inverse, basis, own),
        [(tall, F32)] + [((FACE + 16, R), F32)] * 4 + [msg],
        [table],
        smem=2,
        flops=block,
    )
    m = swap(m, "gy")
    faces = across((f0, f1, f2, f3))
    (m,) = call(first_column_kernel, (m,), [wide])
    m = swap(m, "gx")
    window, window_t = call(
        window_kernel,
        (basis, *faces),
        [((2 * WIN, NI), BF16), ((NI, 2 * WIN), BF16)],
        [pltpu.VMEM((2 * WIN, NI), F32)],
    )
    sums0, picked, m = call(
        first_solve_kernel,
        (ax.astype(jnp.int32).reshape(1), m, whole),
        [((SL, NCG), F32), ((NCG, 128), BF16), msg],
        [pltpu.VMEM((NCG, 128), BF16), pltpu.VMEM((NCG, NCG), BF16)],
        smem=1,
        flops=2 * block,
    )
    m = swap(m, "gy")
    z0, s0, g0, g1, g2, g3, m = call(
        first_kernel,
        (wt, m, l0, *faces, window_t, window, schur, load),
        [(tall, F32), (tall, BF16)] + [((FACE, R), BF16)] * 4 + [msg],
        [table, pltpu.VMEM(tall, BF16)],
        smem=1,
        flops=block,
    )

    def local(s, sent):
        q, l, h0, h1, h2, h3 = call(
            local_kernel,
            (wt, s, *across(sent), inverse),
            [(tall, F32), (tall, F32)] + [face] * 4,
            smem=1,
            flops=block,
        )
        return q, l, across((h0, h1, h2, h3))

    m = swap(m, "gy")
    q0, l1, faces1 = local(s0, (g0, g1, g2, g3))
    (m,) = call(column_kernel, (m,), [wide])
    m = swap(m, "gx")
    change0, sums1, kept, m = call(
        second_solve_kernel,
        (m, sums0, picked),
        [((SL, NCG), F32), ((SL, NCG), F32), ((SL, 128), F32), msg],
    )
    m = swap(m, "gy")
    z1, lm, d0, d1, d2, d3, r1, s1, g0, g1, g2, g3, m, got0 = call(
        second_kernel,
        (wt, m, l0, *faces, l1, *faces1, q0, s0, window_t, window, schur, load),
        [(tall, F32)] * 2 + [face] * 4 + [(tall, F32)] * 2 + [face] * 4 + [msg, ((8, R), F32)],
        [table, zb],
        smem=1,
        flops=block,
    )

    m = swap(m, "gy")
    q1, l2, faces2 = local(s1, (g0, g1, g2, g3))
    (m,) = call(column_kernel, (m,), [wide])
    m = swap(m, "gx")
    (m,) = call(
        third_solve_kernel,
        (m, sums1, picked, change0, kept),
        [msg],
        [pltpu.VMEM((SL, NCG), F32)],
    )
    m = swap(m, "gy")
    z2, x2, p1, q1, r2, s2, g0, g1, g2, g3, m, got1 = call(
        third_kernel,
        (
            wt, m, got0, lm, d0, d1, d2, d3, l1, *faces1, l2, *faces2,
            q0, q1, s0, s1, z0, z1, r1, window_t, schur,
        ),
        [(tall, F32)] * 6 + [face] * 4 + [((NY, 8, R), F32), ((8, R), F32)],
        [zb],
        smem=1,
        flops=block,
    )

    m = swap(m, "gy")
    faces = across((g0, g1, g2, g3))
    (m,) = call(last_column_kernel, (m,), [((NX, 8, R), F32)])
    m = swap(m, "gx")
    x, r = call(
        last_kernel,
        (m, got1, s2, *faces, z2, p1, q1, x2, r2),
        [(tall, BF16), (tall, BF16)],
    )
    return x[None, None], r[None, None]


def solution(mesh):
    return jax.shard_map(
        body,
        mesh=mesh,
        in_specs=(
            P("gx", "gy", None, None),
            P("gx", "gy", None, None),
            P("gx", "gy", None, None),
            P("gx", "gy", None, None),
            P("gx", "gy", None),
            P("gy", None),
        ),
        out_specs=(P("gx", "gy", None, None), P("gx", "gy", None, None)),
        check_vma=False,
    )
```

time: 1030 us -> 358 us (0.35)
  blocking collectives: 891 us -> 82.4 us
  local copies, waits for them, and re-layouts: 6.66 us -> 66.8 us
  starting transfers between devices: 75.4 us -> 129 us
  waiting for transfers between devices: 20.6 us -> 51.8 us
  Pallas kernels: 0 us -> 23.5 us
  matrix products: 22.8 us -> 0 us
  other arithmetic: 10.9 us -> 0.08 us
    psum x8 -> x0, blocking collectives: 836 us -> none  [the longest x5 516 us: inner(): return lax.psum(jnp.sum(weight * first * second, axis=0), ('gx', 'gy'))]
    all_to_all x0 -> x5, blocking collectives: none -> 82.4 us  [swap(): return lax.all_to_all(value, axis, 0, 0, tiled=True)]
    all_to_all x0 -> x7, starting transfers between devices: none -> 72.6 us  [swap(): return lax.all_to_all(value, axis, 0, 0, tiled=True)]
    unnamed x59 -> x182, local copies, waits for them, and re-layouts: 6.5 us -> 64 us
    all_gather x3 -> x0, blocking collectives: 55.1 us -> none  [precondition(): coarse_solution = lax.all_gather(row_solution, 'gy', axis=0, tiled=True)]
    all_to_all x0 -> x7, waiting for transfers between devices: none -> 36.3 us  [swap(): return lax.all_to_all(value, axis, 0, 0, tiled=True)]
    pallas_call x0 -> x15, Pallas kernels: none -> 23.5 us  [call(): pl.pallas_call(kernel, out_shape=tuple((jax.ShapeDtypeStruct(s, d) for s,...]
    dot_general x18 -> x0, matrix products: 22.8 us -> none  [the longest x3 7.37 us: body(): jnp.dot(schur_block, direction.astype(jnp.bfloat16), preferred_element_ty...]
  transfers between devices with their start and end apart: 24 -> 31, of which waited for: 6 -> 10; matrix products, arithmetic and copies ran while one was open for 0% -> 0% of each run, Pallas kernels for 0% -> 3%
where the time goes in v1:
time: 358 us; the launch traced here: 355 us
  starting transfers between devices  129 us (36%)
  blocking collectives  82.4 us (23%)
  local copies, waits for them, and re-layouts  66.8 us (19%)
  waiting for transfers between devices  51.8 us (14%)
  Pallas kernels  23.5 us (7%)
    all_to_all x5, blocking collectives, swap(): return lax.all_to_all(value, axis, 0, 0, tiled=True)  82.4 us
    all_to_all x7, starting transfers between devices, swap(): return lax.all_to_all(value, axis, 0, 0, tiled=True)  72.6 us
    unnamed x182, local copies, waits for them, and re-layouts  64 us
    ppermute x12, starting transfers between devices, across(): result.append(lax.ppermute(high, axis, up))  37 us
    all_to_all x7, waiting for transfers between devices, swap(): return lax.all_to_all(value, axis, 0, 0, tiled=True)  36.3 us
    pallas_call x15, Pallas kernels, call(): pl.pallas_call(kernel, out_shape=tuple((jax.ShapeDtypeStruct(s, d) for s,...  23.5 us
    ppermute x12, starting transfers between devices, across(): result.append(lax.ppermute(low, axis, down))  19.4 us
    ppermute x12, waiting for transfers between devices, across(): result.append(lax.ppermute(low, axis, down))  13.3 us
  transfers between devices with their start and end apart: 31, of which 10 were waited for; matrix products, arithmetic and copies ran while one was open for 0% of the time, Pallas kernels for 3%

profile of v1, /device:TPU:1, one launch (start us, length us, event | category | flops | bytes accessed | tf_op | source)
XLA Modules:
  0.0 355.0 jit_solution(13953854627483539301)
XLA Ops:
  2.0 1.6 copy-done
  5.9 1.9 shard_map.77
  7.8 13.9 %all_to_all.60.m = f32[16,8,128]{2,1,0:T(8,128)S(1)} all-to-all(f32[16,8,128]{2,1,0:T(8,128)S(1)} %get-tuple-element.64), channel_id=1, replica_groups=mesh['gx'=32,'gy'=16] {'gy'}, dimensions={0} | all-to-all | bytes 131072 | tf_op jit(solution)/shard_map/all_to_all | solution.py:374
  21.8 39.3 %all_to_all.61.m = f32[32,16,128]{2,1,0:T(8,128)} all-to-all(f32[32,16,128]{2,1,0:T(8,128)S(1)} %shard_map.78), channel_id=1, replica_groups=mesh['gx'=32,'gy'=16] {'gx'}, dimensions={0} | all-to-all | bytes 524288 | tf_op jit(solution)/shard_map/all_to_all | solution.py:374
  61.1 1.6 broadcast_in_dim.26
  62.7 3.8 %all-to-all-start.2 = ((bf16[16,64,1024]{2,1,0:T(8,128)(2,1)}), bf16[16,64,1024]{2,1,0:T(8,128)(2,1)S(1)}, u32[]{:S(2)}, u32[]{:S(2)}) async-start(bf16[16,64,1024]{2,1,0:T(8,128)(2,1)} %broadcast_in_dim.26), calls=%async_computation.2 | async-start | bytes 4194304 | tf_op jit(solution)/shard_map/all_to_all | solution.py:374
  66.5 2.6 collective-permute-start
  69.2 1.9 collective-permute-start.1
  71.1 3.4 collective-permute-start.2
  74.6 1.3 collective-permute-start.3
  75.9 21.2 %all-to-all-done.2 = bf16[16,64,1024]{2,1,0:T(8,128)(2,1)S(1)} async-done(((bf16[16,64,1024]{2,1,0:T(8,128)(2,1)}), bf16[16,64,1024]{2,1,0:T(8,128)(2,1)S(1)}, u32[]{:S(2)}, u32[]{:S(2)}) %all-to-all-start.2) | async-done | bytes 2097184 | tf_op jit(solution)/shard_map/all_to_all | solution.py:374
  98.0 2.6 shard_map.79
  101.4 3.5 all-to-all-start.3
  106.5 1.1 shard_map.80
  108.2 3.1 all-to-all-done.3.m
  112.0 1.6 copy-done.2
  117.1 2.4 shard_map.81
  121.6 9.8 %all_to_all.62.m = f32[16,8,128]{2,1,0:T(8,128)S(1)} all-to-all(f32[16,8,128]{2,1,0:T(8,128)S(1)} %get-tuple-element.73), channel_id=1, replica_groups=mesh['gx'=32,'gy'=16] {'gy'}, dimensions={0} | all-to-all | bytes 131072 | tf_op jit(solution)/shard_map/all_to_all | solution.py:374
  132.2 12.0 %all-to-all-start.5 = ((f32[32,16,128]{2,1,0:T(8,128)}), f32[32,16,128]{2,1,0:T(8,128)}, u32[]{:S(2)}, u32[]{:S(2)}) async-start(f32[32,16,128]{2,1,0:T(8,128)} %shard_map.82), calls=%async_computation.5 | async-start | bytes 524288 | tf_op jit(solution)/shard_map/all_to_all | solution.py:374
  144.2 3.5 collective-permute-start.4
  147.8 1.9 collective-permute-start.5
  149.7 2.2 collective-permute-start.6
  151.9 1.3 collective-permute-start.7
  153.2 4.7 %collective-permute-done.5.f1 = bf16[256,128]{1,0:T(8,128)(2,1)S(1)} collective-permute-done((bf16[256,128]{1,0:T(8,128)(2,1)}, bf16[256,128]{1,0:T(8,128)(2,1)S(1)}, u32[]{:S(2)}, u32[]{:S(2)}) %collective-permute-start.5) | collective-permute-done | bytes 65568 | tf_op jit(solution)/shard_map/ppermute | solution.py:369
  157.9 1.9 shard_map.84
  160.7 4.2 %collective-permute-start.8 = (f32[256,128]{1,0:T(8,128)}, f32[256,128]{1,0:T(8,128)}, u32[]{:S(2)}, u32[]{:S(2)}) collective-permute-start(f32[256,128]{1,0:T(8,128)} %get-tuple-element.83), channel_id=1, source_target_pairs={{0,16},{16,32},{32,48},{48,64},{64,80},{80,96},{96,112},{112,128},... | collective-permute-start | bytes 393224 | tf_op jit(solution)/shard_map/ppermute | solution.py:368
  164.9 1.9 collective-permute-start.9
  166.8 3.0 collective-permute-start.10
  169.8 1.3 collective-permute-start.11
  172.8 1.3 shard_map.83
  176.6 8.4 %all-to-all-start.6 = ((f32[16,8,128]{2,1,0:T(8,128)}), f32[16,8,128]{2,1,0:T(8,128)}, u32[]{:S(2)}, u32[]{:S(2)}) async-start(f32[16,8,128]{2,1,0:T(8,128)} %copy-done.65), calls=%async_computation.6 | async-start | bytes 131072 | tf_op jit(solution)/shard_map/all_to_all | solution.py:374
  185.0 6.5 %all-to-all-done.6.m = f32[16,8,128]{2,1,0:T(8,128)} async-done(((f32[16,8,128]{2,1,0:T(8,128)}), f32[16,8,128]{2,1,0:T(8,128)}, u32[]{:S(2)}, u32[]{:S(2)}) %all-to-all-start.6) | async-done | bytes 65568 | tf_op jit(solution)/shard_map/all_to_all | solution.py:374
  191.6 1.6 copy-done.3
  194.2 1.0 copy-done.11
  198.0 2.6 shard_map.85
  208.3 9.8 %all_to_all.63.m = f32[16,8,128]{2,1,0:T(8,128)S(1)} all-to-all(f32[16,8,128]{2,1,0:T(8,128)S(1)} %get-tuple-element.88), channel_id=1, replica_groups=mesh['gx'=32,'gy'=16] {'gy'}, dimensions={0} | all-to-all | bytes 131072 | tf_op jit(solution)/shard_map/all_to_all | solution.py:374
  218.9 18.0 %all-to-all-start.8 = ((f32[32,16,128]{2,1,0:T(8,128)}), f32[32,16,128]{2,1,0:T(8,128)}, u32[]{:S(2)}, u32[]{:S(2)}) async-start(f32[32,16,128]{2,1,0:T(8,128)} %shard_map.86), calls=%async_computation.8 | async-start | bytes 524288 | tf_op jit(solution)/shard_map/all_to_all | solution.py:374
  236.9 3.5 collective-permute-start.12
  240.5 1.9 collective-permute-start.13
  242.4 2.2 collective-permute-start.14
  244.6 1.3 collective-permute-start.15
  245.9 2.2 collective-permute-done.12.f0
  248.1 3.3 collective-permute-done.13.f1
  251.4 1.0 copy-done.13
  252.5 1.9 shard_map.88
  256.0 4.1 %collective-permute-start.16 = (f32[256,128]{1,0:T(8,128)}, f32[256,128]{1,0:T(8,128)S(1)}, u32[]{:S(2)}, u32[]{:S(2)}) collective-permute-start(f32[256,128]{1,0:T(8,128)} %get-tuple-element.104), channel_id=1, source_target_pairs={{0,16},{16,32},{32,48},{48,64},{64,80},{80,96},{96,112},{112,128},... | collective-permute-start | bytes 393224 | tf_op jit(solution)/shard_map/ppermute | solution.py:368
  260.2 1.9 collective-permute-start.17
  262.1 2.3 collective-permute-start.18
  264.4 1.5 collective-permute-start.19
  268.1 2.0 shard_map.87
  270.1 9.0 %all-to-all-start.9 = ((f32[16,8,128]{2,1,0:T(8,128)}), f32[16,8,128]{2,1,0:T(8,128)S(1)}, u32[]{:S(2)}, u32[]{:S(2)}) async-start(f32[16,8,128]{2,1,0:T(8,128)} %shard_map.87), calls=%async_computation.9 | async-start | bytes 131072 | tf_op jit(solution)/shard_map/all_to_all | solution.py:374
  281.8 3.9 %all-to-all-done.9.m = f32[16,8,128]{2,1,0:T(8,128)S(1)} async-done(((f32[16,8,128]{2,1,0:T(8,128)}), f32[16,8,128]{2,1,0:T(8,128)S(1)}, u32[]{:S(2)}, u32[]{:S(2)}) %all-to-all-start.9) | async-done | bytes 65568 | tf_op jit(solution)/shard_map/all_to_all | solution.py:374
  285.7 1.6 copy-done.4
  301.9 2.4 shard_map.89
  307.9 9.7 %all_to_all.64.m = f32[16,8,128]{2,1,0:T(8,128)S(1)} all-to-all(f32[16,8,128]{2,1,0:T(8,128)S(1)} %get-tuple-element.112), channel_id=1, replica_groups=mesh['gx'=32,'gy'=16] {'gy'}, dimensions={0} | all-to-all | bytes 131072 | tf_op jit(solution)/shard_map/all_to_all | solution.py:374
  318.3 17.8 %all-to-all-start.11 = ((f32[32,8,128]{2,1,0:T(8,128)}), f32[32,8,128]{2,1,0:T(8,128)S(1)}, u32[]{:S(2)}, u32[]{:S(2)}) async-start(f32[32,8,128]{2,1,0:T(8,128)} %shard_map.90), calls=%async_computation.11 | async-start | bytes 262144 | tf_op jit(solution)/shard_map/all_to_all | solution.py:374
  336.0 3.5 collective-permute-start.20
  339.6 1.9 collective-permute-start.21
  341.5 2.2 collective-permute-start.22
  343.7 1.3 collective-permute-start.23
  345.0 2.2 collective-permute-done.21.f1
  347.2 3.1 collective-permute-done.23.f3
  350.3 1.5 all-to-all-done.11.m
  351.9 1.0 copy-done.42
  (206 shorter events, 59.3 us)
Async XLA Ops:
  2.0 1.6 copy-start
  5.9 55.2 %copy-start.90 = (bf16[64,1024]{1,0:T(8,128)(2,1)S(1)}, bf16[64,1024]{1,0:T(8,128)(2,1)}, u32[]{:S(2)}) copy-start(bf16[64,1024]{1,0:T(8,128)(2,1)} %param.11) | copy-start | bytes 393220
  7.8 53.3 %copy-start.75 = (f32[272,128]{1,0:T(8,128)}, f32[272,128]{1,0:T(8,128)S(1)}, u32[]{:S(2)}) copy-start(f32[272,128]{1,0:T(8,128)S(1)} %get-tuple-element.70) | copy-start | bytes 417796
  7.8 53.3 %copy-start.76 = (f32[272,128]{1,0:T(8,128)}, f32[272,128]{1,0:T(8,128)S(1)}, u32[]{:S(2)}) copy-start(f32[272,128]{1,0:T(8,128)S(1)} %get-tuple-element.69) | copy-start | bytes 417796
  7.8 54.9 %copy-start.77 = (f32[272,128]{1,0:T(8,128)}, f32[272,128]{1,0:T(8,128)S(1)}, u32[]{:S(2)}) copy-start(f32[272,128]{1,0:T(8,128)S(1)} %get-tuple-element.68) | copy-start | bytes 417796
  7.8 104.2 %copy-start.10 = (f32[1024,128]{1,0:T(8,128)}, f32[1024,128]{1,0:T(8,128)S(1)}, u32[]{:S(2)}) copy-start(f32[1024,128]{1,0:T(8,128)S(1)} %get-tuple-element.66.l0) | copy-start | bytes 1572868
  62.7 42.9 %copy-start.48 = (bf16[1,1,8,1024]{3,2,1,0:T(8,128)(2,1)S(1)}, bf16[1,1,8,1024]{3,2,1,0:T(8,128)(2,1)}, u32[]{:S(2)}) copy-start(bf16[1,1,8,1024]{3,2,1,0:T(8,128)(2,1)} %param.9) | copy-start | bytes 49156
  62.7 34.4 %all-to-all-start.2 = ((bf16[16,64,1024]{2,1,0:T(8,128)(2,1)}), bf16[16,64,1024]{2,1,0:T(8,128)(2,1)S(1)}, u32[]{:S(2)}, u32[]{:S(2)}) async-start(bf16[16,64,1024]{2,1,0:T(8,128)(2,1)} %broadcast_in_dim.26), calls=%async_computation.2 | async-start | bytes 4194304 | tf_op jit(solution)/shard_map/all_to_all | solution.py:374
  66.5 45.5 %copy-start.6 = (bf16[1,1,1024,128]{3,2,1,0:T(8,128)(2,1)S(1)}, bf16[1,1,1024,128]{3,2,1,0:T(8,128)(2,1)}, u32[]{:S(2)}) copy-start(bf16[1,1,1024,128]{3,2,1,0:T(8,128)(2,1)} %param.6) | copy-start | bytes 786436
  66.5 38.3 %collective-permute-start = (f32[272,128]{1,0:T(8,128)}, f32[272,128]{1,0:T(8,128)S(1)}, u32[]{:S(2)}, u32[]{:S(2)}) collective-permute-start(f32[272,128]{1,0:T(8,128)} %get-tuple-element.67), channel_id=1, source_target_pairs={{0,16},{16,32},{32,48},{48,64},{64,80},{80,96},{96,112},{112,128},... | collective-permute-start | bytes 417800 | tf_op jit(solution)/shard_map/ppermute | solution.py:368
  69.2 35.7 %collective-permute-start.1 = (f32[272,128]{1,0:T(8,128)}, f32[272,128]{1,0:T(8,128)S(1)}, u32[]{:S(2)}, u32[]{:S(2)}) collective-permute-start(f32[272,128]{1,0:T(8,128)} %copy-done.77), channel_id=1, source_target_pairs={{16,0},{32,16},{48,32},{64,48},{80,64},{96,80},{112,96},{128,112},... | collective-permute-start | bytes 417800 | tf_op jit(solution)/shard_map/ppermute | solution.py:369
  71.1 33.8 %collective-permute-start.2 = (f32[272,128]{1,0:T(8,128)}, f32[272,128]{1,0:T(8,128)S(1)}, u32[]{:S(2)}, u32[]{:S(2)}) collective-permute-start(f32[272,128]{1,0:T(8,128)} %copy-done.76), channel_id=1, source_target_pairs={{0,1},{1,2},{2,3},{3,4},{4,5},{5,6},{6,7},{7,8},{8,9},{9,10},{10,1... | collective-permute-start | bytes 417800 | tf_op jit(solution)/shard_map/ppermute | solution.py:368
  74.6 31.0 %collective-permute-start.3 = (f32[272,128]{1,0:T(8,128)}, f32[272,128]{1,0:T(8,128)}, u32[]{:S(2)}, u32[]{:S(2)}) collective-permute-start(f32[272,128]{1,0:T(8,128)} %copy-done.75), channel_id=1, source_target_pairs={{1,0},{2,1},{3,2},{4,3},{5,4},{6,5},{7,6},{8,7},{9,8},{10,9},{11,1... | collective-permute-start | bytes 417800 | tf_op jit(solution)/shard_map/ppermute | solution.py:369
  101.4 10.6 %copy-start.70 = (f32[8,1024]{1,0:T(8,128)}, f32[8,1024]{1,0:T(8,128)S(1)}, u32[]{:S(2)}) copy-start(f32[8,1024]{1,0:T(8,128)S(1)} %get-tuple-element.74.sums0) | copy-start | bytes 98308
  101.4 10.0 %all-to-all-start.3 = ((f32[16,8,128]{2,1,0:T(8,128)}), f32[16,8,128]{2,1,0:T(8,128)S(1)}, u32[]{:S(2)}, u32[]{:S(2)}) async-start(f32[16,8,128]{2,1,0:T(8,128)} %get-tuple-element.65), calls=%async_computation.3 | async-start | bytes 131072 | tf_op jit(solution)/shard_map/all_to_all | solution.py:374
  104.9 7.1 %copy-start.15 = (f32[272,128]{1,0:T(8,128)}, f32[272,128]{1,0:T(8,128)S(1)}, u32[]{:S(2)}) copy-start(f32[272,128]{1,0:T(8,128)S(1)} %collective-permute-done.1.f1.e1) | copy-start | bytes 417796
  112.0 1.6 copy-start.2
  117.1 40.8 %copy-start.1 = (bf16[1,1,1024,1024]{3,2,1,0:T(8,128)(2,1)S(1)}, bf16[1,1,1024,1024]{3,2,1,0:T(8,128)(2,1)}, u32[]{:S(2)}) copy-start(bf16[1,1,1024,1024]{3,2,1,0:T(8,128)(2,1)} %param.8) | copy-start | bytes 6291460
  121.6 9.8 %copy-start.86 = (bf16[256,128]{1,0:T(8,128)(2,1)}, bf16[256,128]{1,0:T(8,128)(2,1)S(1)}, u32[]{:S(2)}) copy-start(bf16[256,128]{1,0:T(8,128)(2,1)S(1)} %get-tuple-element.81) | copy-start | bytes 196612
  121.6 9.8 %copy-start.87 = (bf16[256,128]{1,0:T(8,128)(2,1)}, bf16[256,128]{1,0:T(8,128)(2,1)S(1)}, u32[]{:S(2)}) copy-start(bf16[256,128]{1,0:T(8,128)(2,1)S(1)} %get-tuple-element.80) | copy-start | bytes 196612
  132.2 38.9 %all-to-all-start.5 = ((f32[32,16,128]{2,1,0:T(8,128)}), f32[32,16,128]{2,1,0:T(8,128)}, u32[]{:S(2)}, u32[]{:S(2)}) async-start(f32[32,16,128]{2,1,0:T(8,128)} %shard_map.82), calls=%async_computation.5 | async-start | bytes 524288 | tf_op jit(solution)/shard_map/all_to_all | solution.py:374
  144.2 9.0 %collective-permute-start.4 = (bf16[256,128]{1,0:T(8,128)(2,1)}, bf16[256,128]{1,0:T(8,128)(2,1)S(1)}, u32[]{:S(2)}, u32[]{:S(2)}) collective-permute-start(bf16[256,128]{1,0:T(8,128)(2,1)} %copy-done.89), channel_id=1, source_target_pairs={{0,16},{16,32},{32,48},{48,64},{64,80},{80,96},{96,112},{112,128},... | collective-permute-start | bytes 196616 | tf_op jit(solution)/shard_map/ppermute | solution.py:368
  147.8 10.1 %collective-permute-start.5 = (bf16[256,128]{1,0:T(8,128)(2,1)}, bf16[256,128]{1,0:T(8,128)(2,1)S(1)}, u32[]{:S(2)}, u32[]{:S(2)}) collective-permute-start(bf16[256,128]{1,0:T(8,128)(2,1)} %copy-done.88), channel_id=1, source_target_pairs={{16,0},{32,16},{48,32},{64,48},{80,64},{96,80},{112,96},{128,112},... | collective-permute-start | bytes 196616 | tf_op jit(solution)/shard_map/ppermute | solution.py:369
  149.7 8.2 %collective-permute-start.6 = (bf16[256,128]{1,0:T(8,128)(2,1)}, bf16[256,128]{1,0:T(8,128)(2,1)S(1)}, u32[]{:S(2)}, u32[]{:S(2)}) collective-permute-start(bf16[256,128]{1,0:T(8,128)(2,1)} %copy-done.87), channel_id=1, source_target_pairs={{0,1},{1,2},{2,3},{3,4},{4,5},{5,6},{6,7},{7,8},{8,9},{9,10},{10,1... | collective-permute-start | bytes 196616 | tf_op jit(solution)/shard_map/ppermute | solution.py:368
  151.9 6.0 %collective-permute-start.7 = (bf16[256,128]{1,0:T(8,128)(2,1)}, bf16[256,128]{1,0:T(8,128)(2,1)S(1)}, u32[]{:S(2)}, u32[]{:S(2)}) collective-permute-start(bf16[256,128]{1,0:T(8,128)(2,1)} %copy-done.86), channel_id=1, source_target_pairs={{1,0},{2,1},{3,2},{4,3},{5,4},{6,5},{7,6},{8,7},{9,8},{10,9},{11,1... | collective-permute-start | bytes 196616 | tf_op jit(solution)/shard_map/ppermute | solution.py:369
  160.7 24.3 %collective-permute-start.8 = (f32[256,128]{1,0:T(8,128)}, f32[256,128]{1,0:T(8,128)}, u32[]{:S(2)}, u32[]{:S(2)}) collective-permute-start(f32[256,128]{1,0:T(8,128)} %get-tuple-element.83), channel_id=1, source_target_pairs={{0,16},{16,32},{32,48},{48,64},{64,80},{80,96},{96,112},{112,128},... | collective-permute-start | bytes 393224 | tf_op jit(solution)/shard_map/ppermute | solution.py:368
  164.9 20.1 %collective-permute-start.9 = (f32[256,128]{1,0:T(8,128)}, f32[256,128]{1,0:T(8,128)}, u32[]{:S(2)}, u32[]{:S(2)}) collective-permute-start(f32[256,128]{1,0:T(8,128)} %get-tuple-element.84), channel_id=1, source_target_pairs={{16,0},{32,16},{48,32},{64,48},{80,64},{96,80},{112,96},{128,112},... | collective-permute-start | bytes 393224 | tf_op jit(solution)/shard_map/ppermute | solution.py:369
  166.8 18.2 %collective-permute-start.10 = (f32[256,128]{1,0:T(8,128)}, f32[256,128]{1,0:T(8,128)}, u32[]{:S(2)}, u32[]{:S(2)}) collective-permute-start(f32[256,128]{1,0:T(8,128)} %get-tuple-element.85), channel_id=1, source_target_pairs={{0,1},{1,2},{2,3},{3,4},{4,5},{5,6},{6,7},{7,8},{8,9},{9,10},{10,1... | collective-permute-start | bytes 393224 | tf_op jit(solution)/shard_map/ppermute | solution.py:368
  169.8 15.2 %collective-permute-start.11 = (f32[256,128]{1,0:T(8,128)}, f32[256,128]{1,0:T(8,128)}, u32[]{:S(2)}, u32[]{:S(2)}) collective-permute-start(f32[256,128]{1,0:T(8,128)} %get-tuple-element.86), channel_id=1, source_target_pairs={{1,0},{2,1},{3,2},{4,3},{5,4},{6,5},{7,6},{8,7},{9,8},{10,9},{11,1... | collective-permute-start | bytes 393224 | tf_op jit(solution)/shard_map/ppermute | solution.py:369
  176.6 15.0 %all-to-all-start.6 = ((f32[16,8,128]{2,1,0:T(8,128)}), f32[16,8,128]{2,1,0:T(8,128)}, u32[]{:S(2)}, u32[]{:S(2)}) async-start(f32[16,8,128]{2,1,0:T(8,128)} %copy-done.65), calls=%async_computation.6 | async-start | bytes 131072 | tf_op jit(solution)/shard_map/all_to_all | solution.py:374
  191.6 1.6 copy-start.3
  193.2 1.0 copy-start.8
  194.2 1.0 copy-start.11
  208.3 9.8 %copy-start.51 = (f32[256,128]{1,0:T(8,128)}, f32[256,128]{1,0:T(8,128)S(1)}, u32[]{:S(2)}) copy-start(f32[256,128]{1,0:T(8,128)S(1)} %get-tuple-element.95.d1) | copy-start | bytes 393220
  208.3 57.6 %copy-start.25 = (bf16[1024,128]{1,0:T(8,128)(2,1)S(1)}, bf16[1024,128]{1,0:T(8,128)(2,1)}, u32[]{:S(2)}) copy-start(bf16[1024,128]{1,0:T(8,128)(2,1)} %copy-done.23) | copy-start | bytes 786436
  218.9 66.8 %copy-start.50 = (f32[256,128]{1,0:T(8,128)S(1)}, f32[256,128]{1,0:T(8,128)}, u32[]{:S(2)}) copy-start(f32[256,128]{1,0:T(8,128)} %copy-done.49) | copy-start | bytes 393220
  218.9 47.0 %all-to-all-start.8 = ((f32[32,16,128]{2,1,0:T(8,128)}), f32[32,16,128]{2,1,0:T(8,128)}, u32[]{:S(2)}, u32[]{:S(2)}) async-start(f32[32,16,128]{2,1,0:T(8,128)} %shard_map.86), calls=%async_computation.8 | async-start | bytes 524288 | tf_op jit(solution)/shard_map/all_to_all | solution.py:374
  236.9 11.2 %collective-permute-start.12 = (f32[256,128]{1,0:T(8,128)}, f32[256,128]{1,0:T(8,128)S(1)}, u32[]{:S(2)}, u32[]{:S(2)}) collective-permute-start(f32[256,128]{1,0:T(8,128)} %copy-done.85), channel_id=1, source_target_pairs={{0,16},{16,32},{32,48},{48,64},{64,80},{80,96},{96,112},{112,128},... | collective-permute-start | bytes 393224 | tf_op jit(solution)/shard_map/ppermute | solution.py:368
  240.5 11.0 %collective-permute-start.13 = (f32[256,128]{1,0:T(8,128)}, f32[256,128]{1,0:T(8,128)S(1)}, u32[]{:S(2)}, u32[]{:S(2)}) collective-permute-start(f32[256,128]{1,0:T(8,128)} %copy-done.84), channel_id=1, source_target_pairs={{16,0},{32,16},{48,32},{64,48},{80,64},{96,80},{112,96},{128,112},... | collective-permute-start | bytes 393224 | tf_op jit(solution)/shard_map/ppermute | solution.py:369
  242.4 9.0 %collective-permute-start.14 = (f32[256,128]{1,0:T(8,128)}, f32[256,128]{1,0:T(8,128)S(1)}, u32[]{:S(2)}, u32[]{:S(2)}) collective-permute-start(f32[256,128]{1,0:T(8,128)} %copy-done.83), channel_id=1, source_target_pairs={{0,1},{1,2},{2,3},{3,4},{4,5},{5,6},{6,7},{7,8},{8,9},{9,10},{10,1... | collective-permute-start | bytes 393224 | tf_op jit(solution)/shard_map/ppermute | solution.py:368
  244.6 6.8 %collective-permute-start.15 = (f32[256,128]{1,0:T(8,128)}, f32[256,128]{1,0:T(8,128)S(1)}, u32[]{:S(2)}, u32[]{:S(2)}) collective-permute-start(f32[256,128]{1,0:T(8,128)} %copy-done.82), channel_id=1, source_target_pairs={{1,0},{2,1},{3,2},{4,3},{5,4},{6,5},{7,6},{8,7},{9,8},{10,9},{11,1... | collective-permute-start | bytes 393224 | tf_op jit(solution)/shard_map/ppermute | solution.py:369
  251.4 1.0 copy-start.13
  256.0 23.1 %collective-permute-start.16 = (f32[256,128]{1,0:T(8,128)}, f32[256,128]{1,0:T(8,128)S(1)}, u32[]{:S(2)}, u32[]{:S(2)}) collective-permute-start(f32[256,128]{1,0:T(8,128)} %get-tuple-element.104), channel_id=1, source_target_pairs={{0,16},{16,32},{32,48},{48,64},{64,80},{80,96},{96,112},{112,128},... | collective-permute-start | bytes 393224 | tf_op jit(solution)/shard_map/ppermute | solution.py:368
  260.2 19.6 %collective-permute-start.17 = (f32[256,128]{1,0:T(8,128)}, f32[256,128]{1,0:T(8,128)S(1)}, u32[]{:S(2)}, u32[]{:S(2)}) collective-permute-start(f32[256,128]{1,0:T(8,128)} %get-tuple-element.105), channel_id=1, source_target_pairs={{16,0},{32,16},{48,32},{64,48},{80,64},{96,80},{112,96},{128,112},... | collective-permute-start | bytes 393224 | tf_op jit(solution)/shard_map/ppermute | solution.py:369
  262.1 18.4 %collective-permute-start.18 = (f32[256,128]{1,0:T(8,128)}, f32[256,128]{1,0:T(8,128)S(1)}, u32[]{:S(2)}, u32[]{:S(2)}) collective-permute-start(f32[256,128]{1,0:T(8,128)} %get-tuple-element.106), channel_id=1, source_target_pairs={{0,1},{1,2},{2,3},{3,4},{4,5},{5,6},{6,7},{7,8},{8,9},{9,10},{10,1... | collective-permute-start | bytes 393224 | tf_op jit(solution)/shard_map/ppermute | solution.py:368
  264.4 16.7 %collective-permute-start.19 = (f32[256,128]{1,0:T(8,128)}, f32[256,128]{1,0:T(8,128)S(1)}, u32[]{:S(2)}, u32[]{:S(2)}) collective-permute-start(f32[256,128]{1,0:T(8,128)} %get-tuple-element.107), channel_id=1, source_target_pairs={{1,0},{2,1},{3,2},{4,3},{5,4},{6,5},{7,6},{8,7},{9,8},{10,9},{11,1... | collective-permute-start | bytes 393224 | tf_op jit(solution)/shard_map/ppermute | solution.py:369
  270.1 15.5 %all-to-all-start.9 = ((f32[16,8,128]{2,1,0:T(8,128)}), f32[16,8,128]{2,1,0:T(8,128)S(1)}, u32[]{:S(2)}, u32[]{:S(2)}) async-start(f32[16,8,128]{2,1,0:T(8,128)} %shard_map.87), calls=%async_computation.9 | async-start | bytes 131072 | tf_op jit(solution)/shard_map/all_to_all | solution.py:374
  285.7 1.6 copy-start.4
  287.3 1.0 copy-start.9
  288.3 1.0 copy-start.14
  289.3 1.0 copy-start.27
  290.4 1.0 copy-start.29
  291.4 1.0 copy-start.31
  292.5 1.0 copy-start.33
  293.5 1.0 copy-start.35
  294.5 1.0 copy-start.37
  307.9 9.7 %copy-start.78 = (f32[256,128]{1,0:T(8,128)}, f32[256,128]{1,0:T(8,128)S(1)}, u32[]{:S(2)}) copy-start(f32[256,128]{1,0:T(8,128)S(1)} %get-tuple-element.118) | copy-start | bytes 393220
  318.3 33.6 %all-to-all-start.11 = ((f32[32,8,128]{2,1,0:T(8,128)}), f32[32,8,128]{2,1,0:T(8,128)S(1)}, u32[]{:S(2)}, u32[]{:S(2)}) async-start(f32[32,8,128]{2,1,0:T(8,128)} %shard_map.90), calls=%async_computation.11 | async-start | bytes 262144 | tf_op jit(solution)/shard_map/all_to_all | solution.py:374
  336.0 9.0 %collective-permute-start.20 = (f32[256,128]{1,0:T(8,128)}, f32[256,128]{1,0:T(8,128)S(1)}, u32[]{:S(2)}, u32[]{:S(2)}) collective-permute-start(f32[256,128]{1,0:T(8,128)} %copy-done.81), channel_id=1, source_target_pairs={{0,16},{16,32},{32,48},{48,64},{64,80},{80,96},{96,112},{112,128},... | collective-permute-start | bytes 393224 | tf_op jit(solution)/shard_map/ppermute | solution.py:368
  339.6 7.6 %collective-permute-start.21 = (f32[256,128]{1,0:T(8,128)}, f32[256,128]{1,0:T(8,128)S(1)}, u32[]{:S(2)}, u32[]{:S(2)}) collective-permute-start(f32[256,128]{1,0:T(8,128)} %copy-done.80), channel_id=1, source_target_pairs={{16,0},{32,16},{48,32},{64,48},{80,64},{96,80},{112,96},{128,112},... | collective-permute-start | bytes 393224 | tf_op jit(solution)/shard_map/ppermute | solution.py:369
  341.5 5.7 %collective-permute-start.22 = (f32[256,128]{1,0:T(8,128)}, f32[256,128]{1,0:T(8,128)S(1)}, u32[]{:S(2)}, u32[]{:S(2)}) collective-permute-start(f32[256,128]{1,0:T(8,128)} %copy-done.79), channel_id=1, source_target_pairs={{0,1},{1,2},{2,3},{3,4},{4,5},{5,6},{6,7},{7,8},{8,9},{9,10},{10,1... | collective-permute-start | bytes 393224 | tf_op jit(solution)/shard_map/ppermute | solution.py:368
  343.7 6.6 %collective-permute-start.23 = (f32[256,128]{1,0:T(8,128)}, f32[256,128]{1,0:T(8,128)S(1)}, u32[]{:S(2)}, u32[]{:S(2)}) collective-permute-start(f32[256,128]{1,0:T(8,128)} %copy-done.78), channel_id=1, source_target_pairs={{1,0},{2,1},{3,2},{4,3},{5,4},{6,5},{7,6},{8,7},{9,8},{10,9},{11,1... | collective-permute-start | bytes 393224 | tf_op jit(solution)/shard_map/ppermute | solution.py:369
  351.9 1.0 copy-start.42
  352.9 1.0 copy-start.44
  (58 other events, 44.2 us)

commit v2 on v1

v2 whole, which is shorter than its diff:
```python
from typing import NamedTuple

import jax
import jax.numpy as jnp
from jax import lax
from jax.experimental import pallas as pl
from jax.experimental.pallas import tpu as pltpu
from jax.sharding import PartitionSpec as P

F32 = jnp.float32
BF16 = jnp.bfloat16
NI = 1024
FACE = 256
R = 128
NX = 32
NY = 16
SL = R // NY
NCG = 1024
VMEM_BYTES = 60 * 1024 * 1024
PAD = 32
LONG = SL * 128 + 128
WIN = 32

ANY = pl.BlockSpec(memory_space=pl.ANY)
SMEM = pl.BlockSpec(memory_space=pltpu.SMEM)


class Taken:
    def __init__(self, source, buffer, semaphore):
        self.buffer = buffer
        self.copy = pltpu.make_async_copy(source, buffer, semaphore)
        self.copy.start()
        self.here = False

    def wait(self):
        if not self.here:
            self.copy.wait()
            self.here = True

    def __getitem__(self, index):
        self.wait()
        return self.buffer[index]

    def rows(self, first, size):
        self.wait()
        return self.buffer[pl.ds(pl.multiple_of(first, size), size)]


class Given:
    def __init__(self, target, buffer, semaphore):
        self.buffer = buffer
        self.copy = pltpu.make_async_copy(buffer, target, semaphore)
        self.sent = False

    def send(self):
        if not self.sent:
            self.copy.start()
            self.sent = True

    def __getitem__(self, index):
        return self.buffer[index]

    def __setitem__(self, index, value):
        self.buffer[index] = value


class Part(NamedTuple):
    array: jax.Array
    first: int
    size: int

    def shape(self):
        *blocks, _, width = self.array.shape
        return (*blocks, self.size, width)

    def of(self, ref):
        rows = pl.ds(self.first, self.size)
        return ref.at[rows] if self.array.ndim == 2 else ref.at[:, rows]


def call(kernel, args, outs, scratch=(), smem=0, flops=0):
    inputs = args[smem:]
    count = len(inputs)
    parts = [a if isinstance(a, Part) else None for a in inputs]
    args = [a.array if isinstance(a, Part) else a for a in args]
    size = sum(a.size * a.dtype.itemsize for a in args)
    shapes = [
        a.shape if part is None else part.shape() for a, part in zip(args[smem:], parts)
    ]
    whole = count + len(outs)

    def moved(*refs):
        scalars, refs = refs[:smem], refs[smem:]
        outside, buffers = refs[:whole], refs[whole : 2 * whole]
        semaphores, rest = refs[2 * whole], refs[2 * whole + 1 :]
        sources = [
            ref if part is None else part.of(ref) for ref, part in zip(outside, parts)
        ]
        taken = [Taken(sources[i], buffers[i], semaphores.at[i]) for i in range(count)]
        given = [Given(outside[i], buffers[i], semaphores.at[i]) for i in range(count, whole)]
        kernel(*scalars, *taken, *given, *rest)
        for value in given:
            value.send()
        for value in taken:
            value.wait()
        for value in given:
            value.copy.wait()

    return pl.pallas_call(
        moved,
        out_shape=tuple(jax.ShapeDtypeStruct(s, d) for s, d in outs),
        in_specs=[SMEM] * smem + [ANY] * count,
        out_specs=tuple(ANY for _ in outs),
        scratch_shapes=[pltpu.VMEM(t, a.dtype) for t, a in zip(shapes, args[smem:])]
        + [pltpu.VMEM(s, d) for s, d in outs]
        + [pltpu.SemaphoreType.DMA((whole,))]
        + list(scratch),
        compiler_params=pltpu.CompilerParams(vmem_limit_bytes=VMEM_BYTES),
        cost_estimate=pl.CostEstimate(flops=flops, bytes_accessed=size, transcendentals=0),
    )(*args)


def rows(i):
    return slice(FACE * i, FACE * (i + 1))


def dot(a, b):
    return jnp.dot(a, b, preferred_element_type=F32)


def lanes(shape):
    return lax.broadcasted_iota(jnp.int32, shape, len(shape) - 1)


def rolled(value, shift):
    shift = shift % 128
    return value if shift == 0 else pltpu.roll(value, shift, value.ndim - 1)


def total(value):
    return jnp.sum(value, axis=0, keepdims=True)


def place(out, base, column, piece, dx0, dy0):
    width = piece.shape[1]
    for cx in range(2):
        for cy in range(2):
            row = base + (dy0 + cy) * 8 + (dx0 + cx) * 2
            slot = 4 * cx + 2 * cy
            out[row : row + 2, column : column + width] = piece[slot : slot + 2]


def weights(ax, ay):
    shared = (ax[0] > 0, ax[0] < NX - 1, ay[0] > 0, ay[0] < NY - 1)
    return [jnp.where(face, 0.5, 1.0).astype(F32) for face in shared]


def thirds(value):
    high = value.astype(BF16).astype(F32)
    middle = (value - high).astype(BF16).astype(F32)
    return high, middle, value - high - middle


def start_kernel(ax, ay, ids, load, basis, inverse, coarse, l_out, msg_out, table, own):
    wt = weights(ax, ay)
    piece = coarse.rows(32 * (ax[0] % 2), 32)
    for k in range(8):
        column = piece[:, 128 * k : 128 * (k + 1)]
        msg_out[:, 32 * k : 32 * (k + 1)] = jnp.broadcast_to(column[None], (NY, 32, 128))
    scaled = [(load[rows(i)].astype(F32) * wt[i]).astype(BF16) for i in range(4)]
    scaled = jnp.concatenate(scaled, axis=0)
    own[...] = jnp.zeros((WIN, NI), F32)
    place(own, 0, 0, basis[...].astype(F32), 1, 1)
    table[...] = jnp.zeros((128, 128), F32)
    table[0:WIN] = dot(own[...].astype(BF16), scaled)
    for c in range(2):
        table[64 + c : 65 + c] = jnp.full((1, 128), ids[c].astype(F32))
    terms = thirds(jnp.transpose(table[...]).reshape(NY, SL, 128))
    terms = jnp.concatenate([*terms, jnp.zeros((NY, SL, 128), F32)], axis=1)
    msg_out[:, FACE : FACE + 32] = terms.astype(BF16)
    msg_out.send()
    for i in range(4):
        l_out[rows(i)] = wt[i] * dot(inverse[rows(i)], scaled)


def first_faces_kernel(l, basis, f0, f1, f2, f3):
    for i, face in enumerate((f0, f1, f2, f3)):
        face[0:FACE] = l[rows(i)]
        face[FACE : FACE + 8] = basis[:, FACE * i : FACE * i + 128].astype(F32)
        face[FACE + 8 : FACE + 16] = basis[:, FACE * i + 128 : FACE * (i + 1)].astype(F32)


def faces_kernel(s, f0, f1, f2, f3):
    for i, face in enumerate((f0, f1, f2, f3)):
        face[...] = s[rows(i)]
        face.send()


def window_kernel(basis, f0, f1, f2, f3, b_out, bt_out, table):
    table[...] = jnp.zeros((2 * WIN, NI), F32)
    place(table, 0, 0, basis[...].astype(F32), 1, 1)
    for i, (face, dx0, dy0) in enumerate(((f0, 0, 1), (f1, 2, 1), (f2, 1, 0), (f3, 1, 2))):
        for h in range(2):
            piece = face[FACE + 8 * h : FACE + 8 * h + 8]
            place(table, WIN, FACE * i + 128 * h, piece, dx0, dy0)
    b_out[...] = table[...].astype(BF16)
    bt_out[...] = jnp.transpose(table[...]).astype(BF16)


def local_kernel(ax, ay, s, f0, f1, f2, f3, inverse, q_out, l_out, g0, g1, g2, g3):
    wt = weights(ax, ay)
    parts = []
    for i, face in enumerate((f0, f1, f2, f3)):
        q = s[rows(i)].astype(F32) + face[...].astype(F32)
        q_out[rows(i)] = q
        parts.append((wt[i] * q).astype(BF16))
    q_out.send()
    scaled = jnp.concatenate(parts, axis=0)
    for i, face in enumerate((g0, g1, g2, g3)):
        local = wt[i] * dot(inverse[rows(i)], scaled)
        l_out[rows(i)] = local
        face[...] = local
        face.send()


def arrived(m):
    return jnp.transpose(m[...].reshape(R, 128))


def blended(wt, i, window_t, y, mine, facing):
    y = y[0:WIN].astype(BF16)
    mine = mine + wt[i] * dot(window_t[rows(i), 0:WIN], y)
    facing = facing + wt[i] * dot(window_t[rows(i), WIN:], y)
    return mine.astype(BF16).astype(F32) + facing.astype(BF16).astype(F32)


def split(value):
    high = value.astype(BF16)
    return jnp.concatenate([high, (value - high.astype(F32)).astype(BF16)], axis=1)


def joined(value):
    return value[:, 0:R] + value[:, R:]


def apply_schur(schur, zb, s_out, faces):
    for i in range(4):
        s = joined(dot(schur[rows(i)], zb[...]))
        s_out[rows(i)] = s
        if faces:
            faces[i][...] = s
            faces[i].send()
    s_out.send()


def window_terms(wt, window, s):
    terms = jnp.zeros((2 * WIN, 2 * R), F32)
    for i in range(4):
        terms += dot(window[:, rows(i)], split(s[rows(i)].astype(F32) * wt[i]))
    return joined(terms[0:WIN] + terms[WIN:])


def send_table(table, msg_out, terms, inner):
    table[...] = jnp.zeros((128, 128), F32)
    table[0:WIN] = terms
    for j, value in enumerate(inner):
        table[WIN + j : WIN + j + 1] = value
    msg_out[:, 0:SL] = jnp.transpose(table[...]).reshape(NY, SL, 128)
    msg_out[:, SL:] = jnp.zeros((NY, PAD - SL, 128), F32)


def first_kernel(
    ax, ay, m, window_t, l0, f0, f1, f2, f3, schur, window, load,
    z_out, s_out, g0, g1, g2, g3, msg_out, table, zb,
):
    wt = weights(ax, ay)
    y = arrived(m)
    for i, face in enumerate((f0, f1, f2, f3)):
        z = blended(wt, i, window_t, y, l0[rows(i)], face[0:FACE])
        z_out[rows(i)] = z
        zb[rows(i)] = z.astype(BF16)
    z_out.send()
    for i, face in enumerate((g0, g1, g2, g3)):
        s = dot(schur[rows(i)], zb[...]).astype(BF16)
        s_out[rows(i)] = s
        face[...] = s
        face.send()
    s_out.send()
    rz = jnp.zeros((1, R), F32)
    pq = jnp.zeros((1, R), F32)
    for i in range(4):
        z = z_out[rows(i)]
        rz += total(wt[i] * load[rows(i)].astype(F32) * z)
        pq += total(z * s_out[rows(i)].astype(F32))
    send_table(table, msg_out, window_terms(wt, window, s_out), (rz, pq))


def second_kernel(
    ax, ay, m, window_t, l0, e0, e1, e2, e3, l1, f0, f1, f2, f3, schur, window, q0, s0, load,
    z_out, s_out, g0, g1, g2, g3, msg_out, got_out, table, zb,
):
    wt = weights(ax, ay)
    got = arrived(m)
    got_out[...] = got[WIN : WIN + 8]
    alpha = got[WIN : WIN + 1]
    for i, (before, face) in enumerate(((e0, f0), (e1, f1), (e2, f2), (e3, f3))):
        mine = l0[rows(i)] - alpha * l1[rows(i)]
        facing = before[0:FACE] - alpha * face[...]
        z = blended(wt, i, window_t, got, mine, facing)
        z_out[rows(i)] = z
        zb[rows(i)] = split(z)
    z_out.send()
    apply_schur(schur, zb, s_out, (g0, g1, g2, g3))
    rz = jnp.zeros((1, R), F32)
    zz = jnp.zeros((1, R), F32)
    zq = jnp.zeros((1, R), F32)
    for i in range(4):
        z = z_out[rows(i)]
        r = load[rows(i)].astype(F32) - alpha * q0[rows(i)]
        rz += total(wt[i] * r * z)
        zz += total(z * s_out[rows(i)])
        zq += total(z * s0[rows(i)].astype(F32))
    send_table(table, msg_out, window_terms(wt, window, s_out), (rz, zz, zq))


def third_kernel(
    ax, ay, m, got0, window_t, l0, d0, d1, d2, d3, l1, e0, e1, e2, e3, l2, f0, f1, f2, f3,
    schur, q0, q1, s0, s1, load,
    z_out, s_out, msg_out, got_out, zb,
):
    wt = weights(ax, ay)
    got = arrived(m)
    got_out[...] = got[WIN : WIN + 8]
    alpha0 = got0[0:1]
    alpha = got[WIN : WIN + 1]
    beta = got[WIN + 1 : WIN + 2]
    scale = alpha0 + alpha * beta
    faces = ((d0, e0, f0), (d1, e1, f1), (d2, e2, f2), (d3, e3, f3))
    for i, (before, first, second) in enumerate(faces):
        mine = l0[rows(i)] - scale * l1[rows(i)] - alpha * l2[rows(i)]
        facing = before[0:FACE] - scale * first[...] - alpha * second[...]
        z = blended(wt, i, window_t, got, mine, facing)
        z_out[rows(i)] = z
        zb[rows(i)] = split(z)
    z_out.send()
    apply_schur(schur, zb, s_out, ())
    rz = jnp.zeros((1, R), F32)
    zz = jnp.zeros((1, R), F32)
    zq = jnp.zeros((1, R), F32)
    for i in range(4):
        z = z_out[rows(i)]
        s = s1[rows(i)] + beta * s0[rows(i)].astype(F32)
        r = load[rows(i)].astype(F32) - scale * q0[rows(i)] - alpha * q1[rows(i)]
        rz += total(wt[i] * r * z)
        zz += total(z * s_out[rows(i)])
        zq += total(z * s)
    inner = jnp.concatenate([rz, zz, zq, jnp.zeros((5, R), F32)], axis=0)
    msg_out[...] = jnp.broadcast_to(inner[None], (NY, 8, R))


def update_kernel(got0, got1, z0, z1, q0, q1, load, x_out, p_out, q_out, r_out):
    alpha0 = got0[0:1]
    alpha = got1[0:1]
    beta = got1[1:2]
    for i in range(4):
        p = z1[rows(i)] + beta * z0[rows(i)]
        q = q1[rows(i)] + beta * q0[rows(i)]
        p_out[rows(i)] = p
        q_out[rows(i)] = q
        x_out[rows(i)] = alpha0 * z0[rows(i)] + alpha * p
        r_out[rows(i)] = load[rows(i)].astype(F32) - alpha0 * q0[rows(i)] - alpha * q


def last_kernel(m, got, s, f0, f1, f2, f3, z, p, q, x, r, x_out, r_out):
    inner = jnp.sum(m[...], axis=0)
    rz1 = got[2:3]
    pq1 = got[3:4]
    rz = inner[0:1]
    beta = rz / rz1
    pq = inner[1:2] + 2.0 * beta * inner[2:3] + beta * beta * pq1
    alpha = rz / pq
    for i, face in enumerate((f0, f1, f2, f3)):
        product = s[rows(i)] + face[...] + beta * q[rows(i)]
        direction = z[rows(i)] + beta * p[rows(i)]
        x_out[rows(i)] = (x[rows(i)] + alpha * direction).astype(BF16)
        r_out[rows(i)] = (r[rows(i)] - alpha * product).astype(BF16)


def send_column(out, column, other):
    for r in range(SL):
        out[:, :, 128 * r : 128 * (r + 1)] = jnp.broadcast_to(column[r : r + 1][None], (NX, 1, 128))
    out[:, :, 128 * SL :] = jnp.broadcast_to(other[None], (NX, 1, 128))


def column_kernel(m, out):
    where = lanes((SL, 128))
    column = jnp.zeros((SL, 128), F32)
    inner = jnp.zeros((SL, 128), F32)
    for b in range(NY):
        value = m[b]
        column += rolled(jnp.where(where < WIN, value, 0.0), 8 * (b - 1))
        inner += jnp.where((where >= WIN) & (where < WIN + 16), value, 0.0)
    other = jnp.zeros((1, 128), F32)
    for r in range(SL):
        other += rolled(inner[r : r + 1], 16 * r - WIN)
    send_column(out, column, other)


def first_column_kernel(m, out):
    where = lanes((SL, 128))
    column = jnp.zeros((SL, 128), F32)
    other = jnp.zeros((SL, 128), F32)
    for b in range(NY):
        value = m[b].astype(F32)
        value = value[0:SL] + value[SL : 2 * SL] + value[2 * SL : 3 * SL]
        column += rolled(jnp.where(where < WIN, value, 0.0), 8 * (b - 1))
        named = jnp.where((where >= 64) & (where < 66), value, 0.0)
        other += rolled(named, 8 * b - 64)
    send_column(out, column, other[0:1])


def unpacked(m, columns):
    for r in range(SL):
        columns[:, r : r + 1] = m[:, :, 128 * r : 128 * (r + 1)]


def vertex_sums(columns, group):
    place_of = lanes((SL, 128)) % 8 // 2
    result = jnp.zeros((SL, 128), F32)
    for k in range(4):
        value = jnp.zeros((SL, 128), F32)
        for j in range(4):
            value += rolled(columns[(4 * group + k - j + 1) % NX], 2 * (k - j))
        result += jnp.where(place_of == k, value, 0.0)
    return result


def reply(out, y, scalars):
    where = lanes((SL, 128))
    rest = jnp.zeros((SL, 128), F32)
    for j, value in enumerate(scalars):
        rest += jnp.where(where == WIN + j, value, 0.0)
    for b in range(NY):
        out[b] = jnp.where(where < WIN, rolled(y, -8 * (b - 1)), rest)


def solve(sums, table, out, scalars):
    y = dot(sums[...].astype(BF16), table[...])
    reply(out, y.astype(BF16).astype(F32), scalars)


def first_solve_kernel(ax, m, mine, other, sums, table, out, columns, picked, spread):
    unpacked(m, columns)
    for group in range(8):
        sums[:, 128 * group : 128 * (group + 1)] = vertex_sums(columns, group)
    own = jnp.zeros((1, 128), F32)
    for j in range(4):
        own += rolled(m[(ax[0] + j - 1 + NX) % NX, :, 128 * SL :], 2 * j)
    for i in range(4):
        number = lax.broadcasted_iota(jnp.int32, (FACE, 128), 0).astype(F32) + float(FACE * i)
        spread[rows(i), 0:128] = jnp.where(number == own, 1.0, 0.0).astype(BF16)
    for half, inverse in enumerate((mine, other)):
        value = jnp.zeros((NCG // 2, 128), F32)
        for k in range(8):
            block = inverse[:, 32 * k : 32 * (k + 1)].reshape(NCG // 2, 128)
            value += dot(block, spread[128 * k : 128 * (k + 1), 0:128])
        picked[NCG // 2 * half : NCG // 2 * (half + 1)] = value.astype(BF16)
    core = ax[0] % 2
    lane = lanes((128, 128))
    for group in range(8):
        named = jnp.zeros((1, 128), F32)
        for k in range(4):
            named += rolled(m[4 * group + k, :, 128 * SL :], 2 * k)
        named = jnp.transpose(jnp.broadcast_to(named, (128, 128))).astype(jnp.int32)
        far = jnp.where(((named >> 5) & 1) != core, NCG // 2, 0)
        named = ((named >> 6) << 5) + (named & 31) + far
        for part in range(8):
            spread[128 * group : 128 * (group + 1), 128 * part : 128 * (part + 1)] = jnp.where(
                named == lane + 128 * part, 1.0, 0.0
            ).astype(BF16)
    for i in range(4):
        table[rows(i)] = dot(spread[rows(i)], picked[...]).astype(BF16)
    solve(sums, table, out, ())


def inner_sums(m, count):
    inner = jnp.sum(m[:, :, 128 * SL :], axis=0)
    offset = lanes((SL, 128)) - 16 * lax.broadcasted_iota(jnp.int32, (SL, 128), 0)
    return [
        jnp.sum(jnp.where(offset == j, inner, 0.0), axis=1, keepdims=True) for j in range(count)
    ]


def second_solve_kernel(m, sums0, table, change, sums, kept, out, columns):
    rz, pq = inner_sums(m, 2)
    alpha = rz / pq
    unpacked(m, columns)
    for group in range(8):
        part = slice(128 * group, 128 * (group + 1))
        value = vertex_sums(columns, group)
        change[:, part] = value
        sums[:, part] = sums0[:, part] - alpha * value
    kept[...] = jnp.where(lanes((SL, 128)) == 0, rz, pq)
    solve(sums, table, out, (alpha,))


def third_solve_kernel(m, sums1, table, change0, kept, out, columns, sums):
    rz, zz, zq = inner_sums(m, 3)
    beta = rz / kept[:, 0:1]
    pq = zz + 2.0 * beta * zq + beta * beta * kept[:, 1:2]
    alpha = rz / pq
    unpacked(m, columns)
    for group in range(8):
        part = slice(128 * group, 128 * (group + 1))
        value = vertex_sums(columns, group) + beta * change0[:, part]
        sums[:, part] = sums1[:, part] - alpha * value
    solve(sums, table, out, (alpha, beta, rz, pq))


def last_column_kernel(m, out):
    out[...] = jnp.broadcast_to(jnp.sum(m[...], axis=0)[None], (NX, 8, R))


def across(faces):
    low_x, high_x, low_y, high_y = faces
    result = []
    for axis, size, low, high in (("gx", NX, low_x, high_x), ("gy", NY, low_y, high_y)):
        up = [(i, i + 1) for i in range(size - 1)]
        down = [(j, i) for i, j in up]
        result.append(lax.ppermute(high, axis, up))
        result.append(lax.ppermute(low, axis, down))
    return result


def swap(value, axis):
    return lax.all_to_all(value, axis, 0, 0, tiled=True)


def after(value, *others):
    return lax.optimization_barrier((value, *others))[0]


def body(load_cases, schur_blocks, local_inverse, coarse_basis, corner_ids, coarse_inverse):
    load = load_cases[0, 0]
    schur = schur_blocks[0, 0]
    inverse = local_inverse[0, 0]
    basis = coarse_basis[0, 0]
    ids = corner_ids[0, 0]
    here = [lax.axis_index(axis).astype(jnp.int32).reshape(1) for axis in ("gx", "gy")]

    tall = (NI, R)
    msg = ((NY, SL, 128), F32)
    wide = ((NX, 1, LONG), F32)
    columns = pltpu.VMEM((NX, SL, 128), F32)
    block = 2 * NI * NI * R
    table = pltpu.VMEM((128, 128), F32)
    zb = pltpu.VMEM((NI, 2 * R), BF16)
    face = ((FACE, R), F32)

    l0, m = call(
        start_kernel,
        (*here, ids, load, basis, inverse, coarse_inverse),
        [(tall, F32), ((NY, FACE + 32, 128), BF16)],
        [table, pltpu.VMEM((WIN, NI), F32)],
        smem=3,
        flops=block,
    )
    f0, f1, f2, f3 = call(
        first_faces_kernel,
        (l0, basis),
        [((FACE + 16, R), F32)] * 4,
        flops=block,
    )
    faces0 = across((f0, f1, f2, f3))
    mine, *faces0 = lax.optimization_barrier((swap(m, "gy"), *faces0))
    other = lax.ppermute(mine, "gx", [(i, i ^ 1) for i in range(NX)])
    (m,) = call(first_column_kernel, (Part(mine, FACE, 32),), [wide])
    m = swap(m, "gx")
    window, window_t = call(
        window_kernel,
        (basis, *faces0),
        [((2 * WIN, NI), BF16), ((NI, 2 * WIN), BF16)],
        [pltpu.VMEM((2 * WIN, NI), F32)],
    )
    sums0, picked, m = call(
        first_solve_kernel,
        (here[0], after(m, window), Part(mine, 0, FACE), Part(other, 0, FACE)),
        [((SL, NCG), F32), ((NCG, 128), BF16), msg],
        [columns, pltpu.VMEM((NCG, 128), BF16), pltpu.VMEM((NCG, NCG), BF16)],
        smem=1,
        flops=2 * block,
    )
    m = swap(m, "gy")
    z0, s0, g0, g1, g2, g3, m = call(
        first_kernel,
        (*here, m, window_t, l0, *faces0, schur, window, load),
        [(tall, F32), (tall, BF16)] + [((FACE, R), BF16)] * 4 + [((NY, PAD, 128), F32)],
        [table, pltpu.VMEM(tall, BF16)],
        smem=2,
        flops=block,
    )

    def stage(s, faces, m):
        m, *faces = lax.optimization_barrier((swap(m, "gy"), *across(faces)))
        (m,) = call(column_kernel, (Part(m, 0, SL),), [wide])
        q, l, *faces = call(
            local_kernel,
            (*here, s, *faces, inverse),
            [(tall, F32), (tall, F32)] + [face] * 4,
            smem=2,
            flops=block,
        )
        m, *faces = lax.optimization_barrier((swap(m, "gx"), *across(faces)))
        return m, q, l, faces

    m, q0, l1, faces1 = stage(s0, (g0, g1, g2, g3), m)
    change0, sums1, kept, m = call(
        second_solve_kernel,
        (m, sums0, picked),
        [((SL, NCG), F32), ((SL, NCG), F32), ((SL, 128), F32), msg],
        [columns],
    )
    m = swap(m, "gy")
    z1, s1, g0, g1, g2, g3, m, got0 = call(
        second_kernel,
        (*here, m, window_t, l0, *faces0, l1, *faces1, schur, window, q0, s0, load),
        [(tall, F32), (tall, F32)] + [face] * 4 + [((NY, PAD, 128), F32), ((8, R), F32)],
        [table, zb],
        smem=2,
        flops=block,
    )

    m, q1, l2, faces2 = stage(s1, (g0, g1, g2, g3), m)
    (m,) = call(
        third_solve_kernel,
        (m, sums1, picked, change0, kept),
        [msg],
        [columns, pltpu.VMEM((SL, NCG), F32)],
    )
    m = swap(m, "gy")
    z2, s2, m, got1 = call(
        third_kernel,
        (
            *here, m, got0, window_t, l0, *faces0, l1, *faces1, l2, *faces2,
            schur, q0, q1, s0, s1, load,
        ),
        [(tall, F32), (tall, F32), ((NY, 8, R), F32), ((8, R), F32)],
        [zb],
        smem=2,
        flops=block,
    )

    m = swap(m, "gy")
    (sums,) = call(last_column_kernel, (m,), [((NX, 8, R), F32)])
    faces = across(call(faces_kernel, (after(s2, m),), [face] * 4, flops=block))
    x2, p1, q1, r2 = call(
        update_kernel,
        (got0, got1, after(z0, m), z1, q0, q1, load),
        [(tall, F32)] * 4,
        flops=block,
    )
    m = swap(sums, "gx")
    x, r = call(
        last_kernel,
        (m, got1, s2, *faces, z2, p1, q1, x2, r2),
        [(tall, BF16), (tall, BF16)],
    )
    return x[None, None], r[None, None]


def solution(mesh):
    return jax.shard_map(
        body,
        mesh=mesh,
        in_specs=(
            P("gx", "gy", None, None),
            P("gx", "gy", None, None),
            P("gx", "gy", None, None),
            P("gx", "gy", None, None),
            P("gx", "gy", None),
            P("gy", None),
        ),
        out_specs=(P("gx", "gy", None, None), P("gx", "gy", None, None)),
        check_vma=False,
    )
```

time: 358 us -> 298 us (0.83)
  local copies, waits for them, and re-layouts: 66.8 us -> 5.29 us
  Pallas kernels: 23.5 us -> 52.8 us
  blocking collectives: 82.4 us -> 56.4 us
  waiting for transfers between devices: 51.8 us -> 41.8 us
  starting transfers between devices: 129 us -> 136 us
    unnamed x182 -> x64, local copies, waits for them, and re-layouts: 64 us -> 5.29 us
    pallas_call x15 -> x18, Pallas kernels: 23.5 us -> 52.8 us  [call(): pl.pallas_call(moved, out_shape=tuple((jax.ShapeDtypeStruct(s, d) for s,...]
    all_to_all x5 -> x4, blocking collectives: 82.4 us -> 56.4 us  [swap(): return lax.all_to_all(value, axis, 0, 0, tiled=True)]
    all_to_all x7, waiting for transfers between devices: 36.3 us -> 14.4 us  [swap(): return lax.all_to_all(value, axis, 0, 0, tiled=True)]
    ppermute x12, waiting for transfers between devices: 13.3 us -> 22.7 us  [across(): result.append(lax.ppermute(low, axis, down))]
    ppermute x12, starting transfers between devices: 37 us -> 44.7 us  [across(): result.append(lax.ppermute(high, axis, up))]
    all_to_all x7, starting transfers between devices: 72.6 us -> 68.7 us  [swap(): return lax.all_to_all(value, axis, 0, 0, tiled=True)]
  transfers between devices with their start and end apart: 31 -> 32, of which waited for: 10 -> 16; matrix products, arithmetic and copies ran while one was open for 0% -> 0% of each run, Pallas kernels for 3% -> 6%
where the time goes in v2:
time: 298 us; the launch traced here: 294 us
  starting transfers between devices  136 us (46%)
  blocking collectives  56.4 us (19%)
  Pallas kernels  52.8 us (18%)
  waiting for transfers between devices  41.8 us (14%)
  local copies, waits for them, and re-layouts  5.29 us (2%)
    all_to_all x7, starting transfers between devices, swap(): return lax.all_to_all(value, axis, 0, 0, tiled=True)  68.7 us
    all_to_all x4, blocking collectives, swap(): return lax.all_to_all(value, axis, 0, 0, tiled=True)  56.4 us
    pallas_call x18, Pallas kernels, call(): pl.pallas_call(moved, out_shape=tuple((jax.ShapeDtypeStruct(s, d) for s,...  52.8 us
    ppermute x12, starting transfers between devices, across(): result.append(lax.ppermute(high, axis, up))  44.7 us
    ppermute x12, waiting for transfers between devices, across(): result.append(lax.ppermute(low, axis, down))  22.7 us
    ppermute x12, starting transfers between devices, across(): result.append(lax.ppermute(low, axis, down))  19.3 us
    all_to_all x7, waiting for transfers between devices, swap(): return lax.all_to_all(value, axis, 0, 0, tiled=True)  14.4 us
  transfers between devices with their start and end apart: 32, of which 16 were waited for; matrix products, arithmetic and copies ran while one was open for 0% of the time, Pallas kernels for 6%

profile of v2, /device:TPU:1, one launch (start us, length us, event | category | flops | bytes accessed | tf_op | source)
XLA Modules:
  0.0 293.8 jit_solution(13437554428359343690)
XLA Ops:
  0.6 4.3 %shard_map.77 = (f32[1024,128]{1,0:T(8,128)}, bf16[16,288,128]{2,1,0:T(8,128)(2,1)}) custom-call(s32[1]{0:T(128)} %bitcast.refs_0_, s32[1]{0:T(128)} %bitcast.1.refs_1_, s32[8]{0:T(128)} %bitcast.23, bf16[1024,128]{1,0:T(8,128)(2,1)} %bitcast.15, bf16[8,1024]{1,0:T(8,128)(2,1)} %bitcast.20, bf16[1024,1024]{1,0:T(8,128)(2,1)} %bitcast.12, ...), custom_call_target="tpu_custom_call" | custom-call | flops 268435456 | bytes 2506792 | tf_op jit(solution)/shard_map/pallas_call | solution.py:109
  4.9 7.6 %all-to-all-start = ((bf16[16,288,128]{2,1,0:T(8,128)(2,1)}), bf16[16,288,128]{2,1,0:T(8,128)(2,1)S(1)}, u32[]{:S(2)}, u32[]{:S(2)}) async-start(bf16[16,288,128]{2,1,0:T(8,128)(2,1)} %get-tuple-element.86), calls=%async_computation | async-start | bytes 2359296 | tf_op jit(solution)/shard_map/all_to_all | solution.py:536
  12.5 1.9 shard_map.78
  14.4 4.4 %collective-permute-start = (f32[272,128]{1,0:T(8,128)}, f32[272,128]{1,0:T(8,128)S(1)}, u32[]{:S(2)}, u32[]{:S(2)}) collective-permute-start(f32[272,128]{1,0:T(8,128)} %get-tuple-element.88), channel_id=1, source_target_pairs={{0,16},{16,32},{32,48},{48,64},{64,80},{80,96},{96,112},{112,128},... | collective-permute-start | bytes 417800 | tf_op jit(solution)/shard_map/ppermute | solution.py:530
  18.8 1.9 collective-permute-start.1
  20.8 3.6 %collective-permute-start.2 = (f32[272,128]{1,0:T(8,128)}, f32[272,128]{1,0:T(8,128)S(1)}, u32[]{:S(2)}, u32[]{:S(2)}) collective-permute-start(f32[272,128]{1,0:T(8,128)} %get-tuple-element.90), channel_id=1, source_target_pairs={{0,1},{1,2},{2,3},{3,4},{4,5},{5,6},{6,7},{7,8},{8,9},{9,10},{10,1... | collective-permute-start | bytes 417800 | tf_op jit(solution)/shard_map/ppermute | solution.py:530
  24.3 1.3 collective-permute-start.3
  25.7 2.5 collective-permute-done.2.refs_3_.refs_7_.refs_8_
  28.2 3.9 %collective-permute-done.3.refs_4_.refs_8_.refs_9_ = f32[272,128]{1,0:T(8,128)S(1)} collective-permute-done((f32[272,128]{1,0:T(8,128)}, f32[272,128]{1,0:T(8,128)S(1)}, u32[]{:S(2)}, u32[]{:S(2)}) %collective-permute-start.3) | collective-permute-done | bytes 139296 | tf_op jit(solution)/shard_map/ppermute | solution.py:531
  32.0 3.3 %collective-permute-start.4 = (bf16[16,288,128]{2,1,0:T(8,128)(2,1)S(1)}, bf16[16,288,128]{2,1,0:T(8,128)(2,1)S(1)}, u32[]{:S(2)}, u32[]{:S(2)}) collective-permute-start(bf16[16,288,128]{2,1,0:T(8,128)(2,1)S(1)} %all-to-all-done.refs_0_.refs_2_), channel_id=1, source_target_pairs={{0,16},{16,0},{32,48},{48,32},{64,80},{80,64},{96,112},{112,96},{1... | collective-permute-start | bytes 3538952 | tf_op jit(solution)/shard_map/ppermute | solution.py:576
  35.3 1.8 shard_map.79
  37.1 15.5 %all-to-all-start.1 = ((f32[32,1,1152]{2,1,0:T(1,128)}), f32[32,1,1152]{2,1,0:T(1,128)S(1)}, u32[]{:S(2)}, u32[]{:S(2)}) async-start(f32[32,1,1152]{2,1,0:T(1,128)} %shard_map.79), calls=%async_computation.1 | async-start | bytes 294912 | tf_op jit(solution)/shard_map/all_to_all | solution.py:536
  52.6 2.0 shard_map.80
  54.6 14.4 %all-to-all-done.1.refs_1_ = f32[32,1,1152]{2,1,0:T(1,128)S(1)} async-done(((f32[32,1,1152]{2,1,0:T(1,128)}), f32[32,1,1152]{2,1,0:T(1,128)S(1)}, u32[]{:S(2)}, u32[]{:S(2)}) %all-to-all-start.1) | async-done | bytes 147488 | tf_op jit(solution)/shard_map/all_to_all | solution.py:536
  69.7 1.0 copy-done.5
  70.7 4.6 %shard_map.81 = (f32[8,1024]{1,0:T(8,128)}, bf16[1024,128]{1,0:T(8,128)(2,1)}, f32[16,8,128]{2,1,0:T(8,128)}) custom-call(s32[1]{0:T(128)} %bitcast.refs_0_, f32[32,1,1152]{2,1,0:T(1,128)} %copy-done.10, bf16[16,288,128]{2,1,0:T(8,128)(2,1)} %copy-done, bf16[16,288,128]{2,1,0:T(8,128)(2,1)} %copy-done.5), custom_call_target="tpu_custom_call" | custom-call | flops 536870912 | bytes 2506756 | tf_op jit(solution)/shard_map/pallas_call | solution.py:109
  75.3 14.3 %all_to_all.55.refs_2_ = f32[16,8,128]{2,1,0:T(8,128)} all-to-all(f32[16,8,128]{2,1,0:T(8,128)} %get-tuple-element.99), channel_id=1, replica_groups=mesh['gx'=32,'gy'=16] {'gy'}, dimensions={0} | all-to-all | bytes 131072 | tf_op jit(solution)/shard_map/all_to_all | solution.py:536
  89.6 4.2 %shard_map.82 = (f32[1024,128]{1,0:T(8,128)}, bf16[1024,128]{1,0:T(8,128)(2,1)}, bf16[256,128]{1,0:T(8,128)(2,1)}, bf16[256,128]{1,0:T(8,128)(2,1)}, bf16[256,12...) custom-call(s32[1]{0:T(128)} %bitcast.refs_0_, s32[1]{0:T(128)} %bitcast.1.refs_1_, ...), custom_call_target="tpu_custom_call" | custom-call | flops 268435456 | bytes 3768328 | tf_op jit(solution)/shard_map/pallas_call | solution.py:109
  93.9 3.5 %all-to-all-start.3 = ((f32[16,32,128]{2,1,0:T(8,128)}), f32[16,32,128]{2,1,0:T(8,128)S(1)}, u32[]{:S(2)}, u32[]{:S(2)}) async-start(f32[16,32,128]{2,1,0:T(8,128)} %get-tuple-element.101), calls=%async_computation.3 | async-start | bytes 524288 | tf_op jit(solution)/shard_map/all_to_all | solution.py:536
  97.4 4.9 %collective-permute-start.5 = (bf16[256,128]{1,0:T(8,128)(2,1)}, bf16[256,128]{1,0:T(8,128)(2,1)S(1)}, u32[]{:S(2)}, u32[]{:S(2)}) collective-permute-start(bf16[256,128]{1,0:T(8,128)(2,1)} %get-tuple-element.102), channel_id=1, source_target_pairs={{0,16},{16,32},{32,48},{48,64},{64,80},{80,96},{96,112},{112,128},... | collective-permute-start | bytes 196616 | tf_op jit(solution)/shard_map/ppermute | solution.py:530
  102.3 1.9 collective-permute-start.6
  104.3 3.4 %collective-permute-start.7 = (bf16[256,128]{1,0:T(8,128)(2,1)}, bf16[256,128]{1,0:T(8,128)(2,1)S(1)}, u32[]{:S(2)}, u32[]{:S(2)}) collective-permute-start(bf16[256,128]{1,0:T(8,128)(2,1)} %get-tuple-element.104), channel_id=1, source_target_pairs={{0,1},{1,2},{2,3},{3,4},{4,5},{5,6},{6,7},{7,8},{8,9},{9,10},{10,1... | collective-permute-start | bytes 196616 | tf_op jit(solution)/shard_map/ppermute | solution.py:530
  107.7 1.3 collective-permute-start.8
  109.3 3.9 %collective-permute-done.8.refs_6_ = bf16[256,128]{1,0:T(8,128)(2,1)S(1)} collective-permute-done((bf16[256,128]{1,0:T(8,128)(2,1)}, bf16[256,128]{1,0:T(8,128)(2,1)S(1)}, u32[]{:S(2)}, u32[]{:S(2)}) %collective-permute-start.8) | collective-permute-done | bytes 65568 | tf_op jit(solution)/shard_map/ppermute | solution.py:531
  113.9 1.7 shard_map.83
  115.6 6.0 %all-to-all-start.4 = ((f32[32,1,1152]{2,1,0:T(1,128)}), f32[32,1,1152]{2,1,0:T(1,128)S(1)}, u32[]{:S(2)}, u32[]{:S(2)}) async-start(f32[32,1,1152]{2,1,0:T(1,128)} %shard_map.83), calls=%async_computation.4 | async-start | bytes 294912 | tf_op jit(solution)/shard_map/all_to_all | solution.py:536
  121.6 3.5 %shard_map.84 = (f32[1024,128]{1,0:T(8,128)}, f32[1024,128]{1,0:T(8,128)}, f32[256,128]{1,0:T(8,128)}, f32[256,128]{1,0:T(8,128)}, f32[256,128]{1,0:T(8,128)}, /*index=5*/f32[256,128]{1,0:T(8,128)}) custom-call(s32[1]{0:T(128)} %bitcast.refs_0_, s32[1]{0:T(128)} %bitcast.1.refs_1_, bf16[1024,128]{1,0:T(8,128)(2,1)} %get-tuple-element.107.refs_2_.refs_17_.refs_23_, ...), custom_call_target="tpu_custom_call" | custom-call | flops 268435456 | bytes 2621448 | tf_op jit(solution)/shard_map/pallas_call | solution.py:109
  125.2 3.5 %collective-permute-start.9 = (f32[256,128]{1,0:T(8,128)}, f32[256,128]{1,0:T(8,128)S(1)}, u32[]{:S(2)}, u32[]{:S(2)}) collective-permute-start(f32[256,128]{1,0:T(8,128)} %get-tuple-element.112), channel_id=1, source_target_pairs={{0,16},{16,32},{32,48},{48,64},{64,80},{80,96},{96,112},{112,128},... | collective-permute-start | bytes 393224 | tf_op jit(solution)/shard_map/ppermute | solution.py:530
  128.7 1.9 collective-permute-start.10
  130.6 3.1 %collective-permute-start.11 = (f32[256,128]{1,0:T(8,128)}, f32[256,128]{1,0:T(8,128)S(1)}, u32[]{:S(2)}, u32[]{:S(2)}) collective-permute-start(f32[256,128]{1,0:T(8,128)} %get-tuple-element.114), channel_id=1, source_target_pairs={{0,1},{1,2},{2,3},{3,4},{4,5},{5,6},{6,7},{7,8},{8,9},{9,10},{10,1... | collective-permute-start | bytes 393224 | tf_op jit(solution)/shard_map/ppermute | solution.py:530
  133.7 1.3 collective-permute-start.12
  136.1 4.0 %collective-permute-done.12.refs_13_.refs_14_ = f32[256,128]{1,0:T(8,128)S(1)} collective-permute-done((f32[256,128]{1,0:T(8,128)}, f32[256,128]{1,0:T(8,128)S(1)}, u32[]{:S(2)}, u32[]{:S(2)}) %collective-permute-start.12) | collective-permute-done | bytes 131104 | tf_op jit(solution)/shard_map/ppermute | solution.py:531
  140.8 2.1 shard_map.85
  142.9 15.7 %all_to_all.56.refs_2_ = f32[16,8,128]{2,1,0:T(8,128)} all-to-all(f32[16,8,128]{2,1,0:T(8,128)} %get-tuple-element.119), channel_id=1, replica_groups=mesh['gx'=32,'gy'=16] {'gy'}, dimensions={0} | all-to-all | bytes 131072 | tf_op jit(solution)/shard_map/all_to_all | solution.py:536
  158.6 4.8 %shard_map.86 = (f32[1024,128]{1,0:T(8,128)}, f32[1024,128]{1,0:T(8,128)}, f32[256,128]{1,0:T(8,128)}, f32[256,128]{1,0:T(8,128)}, f32[256,128]{1,0:T(8,128)}, /...) custom-call(s32[1]{0:T(128)} %bitcast.refs_0_, s32[1]{0:T(128)} %bitcast.1.refs_1_, ...), custom_call_target="tpu_custom_call" | custom-call | flops 268435456 | bytes 5603336 | tf_op jit(solution)/shard_map/pallas_call | solution.py:109
  163.5 3.5 %all-to-all-start.6 = ((f32[16,32,128]{2,1,0:T(8,128)}), f32[16,32,128]{2,1,0:T(8,128)S(1)}, u32[]{:S(2)}, u32[]{:S(2)}) async-start(f32[16,32,128]{2,1,0:T(8,128)} %get-tuple-element.126), calls=%async_computation.6 | async-start | bytes 524288 | tf_op jit(solution)/shard_map/all_to_all | solution.py:536
  167.0 6.0 %collective-permute-start.13 = (f32[256,128]{1,0:T(8,128)}, f32[256,128]{1,0:T(8,128)S(1)}, u32[]{:S(2)}, u32[]{:S(2)}) collective-permute-start(f32[256,128]{1,0:T(8,128)} %get-tuple-element.127), channel_id=1, source_target_pairs={{0,16},{16,32},{32,48},{48,64},{64,80},{80,96},{96,112},{112,128},... | collective-permute-start | bytes 393224 | tf_op jit(solution)/shard_map/ppermute | solution.py:530
  173.0 1.9 collective-permute-start.14
  175.0 3.4 %collective-permute-start.15 = (f32[256,128]{1,0:T(8,128)}, f32[256,128]{1,0:T(8,128)S(1)}, u32[]{:S(2)}, u32[]{:S(2)}) collective-permute-start(f32[256,128]{1,0:T(8,128)} %get-tuple-element.129), channel_id=1, source_target_pairs={{0,1},{1,2},{2,3},{3,4},{4,5},{5,6},{6,7},{7,8},{8,9},{9,10},{10,1... | collective-permute-start | bytes 393224 | tf_op jit(solution)/shard_map/ppermute | solution.py:530
  178.4 1.3 collective-permute-start.16
  179.8 0.8 collective-permute-done.15.refs_5_
  180.6 3.7 %collective-permute-done.16.refs_6_ = f32[256,128]{1,0:T(8,128)S(1)} collective-permute-done((f32[256,128]{1,0:T(8,128)}, f32[256,128]{1,0:T(8,128)S(1)}, u32[]{:S(2)}, u32[]{:S(2)}) %collective-permute-start.16) | collective-permute-done | bytes 131104 | tf_op jit(solution)/shard_map/ppermute | solution.py:531
  185.1 1.7 shard_map.87
  186.7 15.9 %all-to-all-start.7 = ((f32[32,1,1152]{2,1,0:T(1,128)}), f32[32,1,1152]{2,1,0:T(1,128)S(1)}, u32[]{:S(2)}, u32[]{:S(2)}) async-start(f32[32,1,1152]{2,1,0:T(1,128)} %shard_map.87), calls=%async_computation.7 | async-start | bytes 294912 | tf_op jit(solution)/shard_map/all_to_all | solution.py:536
  202.7 3.6 %shard_map.88 = (f32[1024,128]{1,0:T(8,128)}, f32[1024,128]{1,0:T(8,128)}, f32[256,128]{1,0:T(8,128)}, f32[256,128]{1,0:T(8,128)}, f32[256,128]{1,0:T(8,128)}, /*index=5*/f32[256,128]{1,0:T(8,128)}) custom-call(s32[1]{0:T(128)} %bitcast.refs_0_, s32[1]{0:T(128)} %bitcast.1.refs_1_, f32[1024,128]{1,0:T(8,128)} %get-tuple-element.132.refs_2_.refs_24_, ...), custom_call_target="tpu_custom_call" | custom-call | flops 268435456 | bytes 3145736 | tf_op jit(solution)/shard_map/pallas_call | solution.py:109
  206.3 3.5 %collective-permute-start.17 = (f32[256,128]{1,0:T(8,128)}, f32[256,128]{1,0:T(8,128)S(1)}, u32[]{:S(2)}, u32[]{:S(2)}) collective-permute-start(f32[256,128]{1,0:T(8,128)} %get-tuple-element.137), channel_id=1, source_target_pairs={{0,16},{16,32},{32,48},{48,64},{64,80},{80,96},{96,112},{112,128},... | collective-permute-start | bytes 393224 | tf_op jit(solution)/shard_map/ppermute | solution.py:530
  209.8 1.9 collective-permute-start.18
  211.8 3.1 %collective-permute-start.19 = (f32[256,128]{1,0:T(8,128)}, f32[256,128]{1,0:T(8,128)S(1)}, u32[]{:S(2)}, u32[]{:S(2)}) collective-permute-start(f32[256,128]{1,0:T(8,128)} %get-tuple-element.139), channel_id=1, source_target_pairs={{0,1},{1,2},{2,3},{3,4},{4,5},{5,6},{6,7},{7,8},{8,9},{9,10},{10,1... | collective-permute-start | bytes 393224 | tf_op jit(solution)/shard_map/ppermute | solution.py:530
  214.9 1.3 collective-permute-start.20
  217.2 4.0 %collective-permute-done.20.refs_19_ = f32[256,128]{1,0:T(8,128)S(1)} collective-permute-done((f32[256,128]{1,0:T(8,128)}, f32[256,128]{1,0:T(8,128)S(1)}, u32[]{:S(2)}, u32[]{:S(2)}) %collective-permute-start.20) | collective-permute-done | bytes 131104 | tf_op jit(solution)/shard_map/ppermute | solution.py:531
  221.9 2.2 shard_map.89
  224.1 15.7 %all_to_all.57.refs_2_ = f32[16,8,128]{2,1,0:T(8,128)} all-to-all(f32[16,8,128]{2,1,0:T(8,128)} %shard_map.89), channel_id=1, replica_groups=mesh['gx'=32,'gy'=16] {'gy'}, dimensions={0} | all-to-all | bytes 131072 | tf_op jit(solution)/shard_map/all_to_all | solution.py:536
  239.9 4.8 %shard_map.90 = (f32[1024,128]{1,0:T(8,128)}, f32[1024,128]{1,0:T(8,128)}, f32[16,8,128]{2,1,0:T(8,128)}, f32[8,128]{1,0:T(8,128)}) custom-call(s32[1]{0:T(128)} %bitcast.refs_0_, s32[1]{0:T(128)} %bitcast.1.refs_1_, f32[16,8,128]{2,1,0:T(8,128)} %all_to_all.57.refs_2_, f32[8,128]{1,0:T(8,128)} %get-tuple-element.145.refs_3_.refs_0_, ...), custom_call_target="tpu_custom_call" | custom-call | flops 268435456 | bytes 7573512 | tf_op jit(solution)/shard_map/pallas_call | solution.py:109
  244.7 10.6 %all_to_all.58.refs_0_ = f32[16,8,128]{2,1,0:T(8,128)} all-to-all(f32[16,8,128]{2,1,0:T(8,128)} %get-tuple-element.152), channel_id=1, replica_groups=mesh['gx'=32,'gy'=16] {'gy'}, dimensions={0} | all-to-all | bytes 131072 | tf_op jit(solution)/shard_map/all_to_all | solution.py:536
  255.3 1.5 shard_map.91
  256.9 16.7 %all-to-all-start.10 = ((f32[32,8,128]{2,1,0:T(8,128)}), f32[32,8,128]{2,1,0:T(8,128)S(1)}, u32[]{:S(2)}, u32[]{:S(2)}) async-start(f32[32,8,128]{2,1,0:T(8,128)} %shard_map.91), calls=%async_computation.10 | async-start | bytes 262144 | tf_op jit(solution)/shard_map/all_to_all | solution.py:536
  273.6 1.9 shard_map.92
  275.5 3.5 %collective-permute-start.21 = (f32[256,128]{1,0:T(8,128)}, f32[256,128]{1,0:T(8,128)S(1)}, u32[]{:S(2)}, u32[]{:S(2)}) collective-permute-start(f32[256,128]{1,0:T(8,128)} %get-tuple-element.156), channel_id=1, source_target_pairs={{0,16},{16,32},{32,48},{48,64},{64,80},{80,96},{96,112},{112,128},... | collective-permute-start | bytes 393224 | tf_op jit(solution)/shard_map/ppermute | solution.py:530
  279.0 1.9 collective-permute-start.22
  281.0 2.2 collective-permute-start.23
  283.2 1.3 collective-permute-start.24
  284.5 3.1 %shard_map.93 = (f32[1024,128]{1,0:T(8,128)}, f32[1024,128]{1,0:T(8,128)}, f32[1024,128]{1,0:T(8,128)}, f32[1024,128]{1,0:T(8,128)}) custom-call(f32[8,128]{1,0:T(8,128)} %get-tuple-element.145.refs_3_.refs_0_, f32[8,128]{1,0:T(8,128)} %get-tuple-element.153.refs_1_, f32[1024,128]{1,0:T(8,128)} %get-tuple-element.162.refs_2_, ...), custom_call_target="tpu_custom_call" | custom-call | flops 268435456 | bytes 2367488 | tf_op jit(solution)/shard_map/pallas_call | solution.py:109
  287.6 2.2 collective-permute-done.24.refs_6_
  290.5 3.1 %shard_map.94 = (bf16[1024,128]{1,0:T(8,128)(2,1)}, bf16[1024,128]{1,0:T(8,128)(2,1)}) custom-call(f32[32,8,128]{2,1,0:T(8,128)} %copy-done.15, f32[8,128]{1,0:T(8,128)} %get-tuple-element.153.refs_1_, f32[1024,128]{1,0:T(8,128)} %get-tuple-element.155.refs_0_.refs_2_, f32[256,128]{1,0:T(8,128)} %copy-done.20, f32[256,128]{1,0:T(8,128)} %copy-done.21, ...), custom_call_target="tpu_custom_call" | custom-call | bytes 3805184 | tf_op jit(solution)/shard_map/pallas_call | solution.py:109
  (86 shorter events, 6.8 us)
Async XLA Ops:
  4.9 27.1 %all-to-all-start = ((bf16[16,288,128]{2,1,0:T(8,128)(2,1)}), bf16[16,288,128]{2,1,0:T(8,128)(2,1)S(1)}, u32[]{:S(2)}, u32[]{:S(2)}) async-start(bf16[16,288,128]{2,1,0:T(8,128)(2,1)} %get-tuple-element.86), calls=%async_computation | async-start | bytes 2359296 | tf_op jit(solution)/shard_map/all_to_all | solution.py:536
  14.4 11.2 %collective-permute-start = (f32[272,128]{1,0:T(8,128)}, f32[272,128]{1,0:T(8,128)S(1)}, u32[]{:S(2)}, u32[]{:S(2)}) collective-permute-start(f32[272,128]{1,0:T(8,128)} %get-tuple-element.88), channel_id=1, source_target_pairs={{0,16},{16,32},{32,48},{48,64},{64,80},{80,96},{96,112},{112,128},... | collective-permute-start | bytes 417800 | tf_op jit(solution)/shard_map/ppermute | solution.py:530
  18.8 6.9 %collective-permute-start.1 = (f32[272,128]{1,0:T(8,128)}, f32[272,128]{1,0:T(8,128)S(1)}, u32[]{:S(2)}, u32[]{:S(2)}) collective-permute-start(f32[272,128]{1,0:T(8,128)} %get-tuple-element.89), channel_id=1, source_target_pairs={{16,0},{32,16},{48,32},{64,48},{80,64},{96,80},{112,96},{128,112},... | collective-permute-start | bytes 417800 | tf_op jit(solution)/shard_map/ppermute | solution.py:531
  20.8 7.4 %collective-permute-start.2 = (f32[272,128]{1,0:T(8,128)}, f32[272,128]{1,0:T(8,128)S(1)}, u32[]{:S(2)}, u32[]{:S(2)}) collective-permute-start(f32[272,128]{1,0:T(8,128)} %get-tuple-element.90), channel_id=1, source_target_pairs={{0,1},{1,2},{2,3},{3,4},{4,5},{5,6},{6,7},{7,8},{8,9},{9,10},{10,1... | collective-permute-start | bytes 417800 | tf_op jit(solution)/shard_map/ppermute | solution.py:530
  24.3 7.7 %collective-permute-start.3 = (f32[272,128]{1,0:T(8,128)}, f32[272,128]{1,0:T(8,128)S(1)}, u32[]{:S(2)}, u32[]{:S(2)}) collective-permute-start(f32[272,128]{1,0:T(8,128)} %get-tuple-element.91), channel_id=1, source_target_pairs={{1,0},{2,1},{3,2},{4,3},{5,4},{6,5},{7,6},{8,7},{9,8},{10,9},{11,1... | collective-permute-start | bytes 417800 | tf_op jit(solution)/shard_map/ppermute | solution.py:531
  25.6 26.9 %copy-start.1 = (f32[272,128]{1,0:T(8,128)}, f32[272,128]{1,0:T(8,128)S(1)}, u32[]{:S(2)}) copy-start(f32[272,128]{1,0:T(8,128)S(1)} %collective-permute-done.refs_1_.refs_5_.refs_6_) | copy-start | bytes 417796
  25.7 26.9 %copy-start.2 = (f32[272,128]{1,0:T(8,128)}, f32[272,128]{1,0:T(8,128)S(1)}, u32[]{:S(2)}) copy-start(f32[272,128]{1,0:T(8,128)S(1)} %collective-permute-done.1.refs_2_.refs_6_.refs_7_) | copy-start | bytes 417796
  28.2 24.4 %copy-start.3 = (f32[272,128]{1,0:T(8,128)}, f32[272,128]{1,0:T(8,128)S(1)}, u32[]{:S(2)}) copy-start(f32[272,128]{1,0:T(8,128)S(1)} %collective-permute-done.2.refs_3_.refs_7_.refs_8_) | copy-start | bytes 417796
  32.0 20.6 %copy-start.4 = (f32[272,128]{1,0:T(8,128)}, f32[272,128]{1,0:T(8,128)S(1)}, u32[]{:S(2)}) copy-start(f32[272,128]{1,0:T(8,128)S(1)} %collective-permute-done.3.refs_4_.refs_8_.refs_9_) | copy-start | bytes 417796
  32.0 3.3 %copy-start = (bf16[16,288,128]{2,1,0:T(8,128)(2,1)}, bf16[16,288,128]{2,1,0:T(8,128)(2,1)S(1)}, u32[]{:S(2)}) copy-start(bf16[16,288,128]{2,1,0:T(8,128)(2,1)S(1)} %all-to-all-done.refs_0_.refs_2_) | copy-start | bytes 3538948
  32.0 37.0 %collective-permute-start.4 = (bf16[16,288,128]{2,1,0:T(8,128)(2,1)S(1)}, bf16[16,288,128]{2,1,0:T(8,128)(2,1)S(1)}, u32[]{:S(2)}, u32[]{:S(2)}) collective-permute-start(bf16[16,288,128]{2,1,0:T(8,128)(2,1)S(1)} %all-to-all-done.refs_0_.refs_2_), channel_id=1, source_target_pairs={{0,16},{16,0},{32,48},{48,32},{64,80},{80,64},{96,112},{112,96},{1... | collective-permute-start | bytes 3538952 | tf_op jit(solution)/shard_map/ppermute | solution.py:576
  37.1 31.9 %all-to-all-start.1 = ((f32[32,1,1152]{2,1,0:T(1,128)}), f32[32,1,1152]{2,1,0:T(1,128)S(1)}, u32[]{:S(2)}, u32[]{:S(2)}) async-start(f32[32,1,1152]{2,1,0:T(1,128)} %shard_map.79), calls=%async_computation.1 | async-start | bytes 294912 | tf_op jit(solution)/shard_map/all_to_all | solution.py:536
  69.0 0.6 copy-start.10
  69.7 1.0 copy-start.5
  93.9 19.4 %all-to-all-start.3 = ((f32[16,32,128]{2,1,0:T(8,128)}), f32[16,32,128]{2,1,0:T(8,128)S(1)}, u32[]{:S(2)}, u32[]{:S(2)}) async-start(f32[16,32,128]{2,1,0:T(8,128)} %get-tuple-element.101), calls=%async_computation.3 | async-start | bytes 524288 | tf_op jit(solution)/shard_map/all_to_all | solution.py:536
  97.4 11.6 %collective-permute-start.5 = (bf16[256,128]{1,0:T(8,128)(2,1)}, bf16[256,128]{1,0:T(8,128)(2,1)S(1)}, u32[]{:S(2)}, u32[]{:S(2)}) collective-permute-start(bf16[256,128]{1,0:T(8,128)(2,1)} %get-tuple-element.102), channel_id=1, source_target_pairs={{0,16},{16,32},{32,48},{48,64},{64,80},{80,96},{96,112},{112,128},... | collective-permute-start | bytes 196616 | tf_op jit(solution)/shard_map/ppermute | solution.py:530
  102.3 6.7 %collective-permute-start.6 = (bf16[256,128]{1,0:T(8,128)(2,1)}, bf16[256,128]{1,0:T(8,128)(2,1)S(1)}, u32[]{:S(2)}, u32[]{:S(2)}) collective-permute-start(bf16[256,128]{1,0:T(8,128)(2,1)} %get-tuple-element.103), channel_id=1, source_target_pairs={{16,0},{32,16},{48,32},{64,48},{80,64},{96,80},{112,96},{128,112},... | collective-permute-start | bytes 196616 | tf_op jit(solution)/shard_map/ppermute | solution.py:531
  104.3 5.1 %collective-permute-start.7 = (bf16[256,128]{1,0:T(8,128)(2,1)}, bf16[256,128]{1,0:T(8,128)(2,1)S(1)}, u32[]{:S(2)}, u32[]{:S(2)}) collective-permute-start(bf16[256,128]{1,0:T(8,128)(2,1)} %get-tuple-element.104), channel_id=1, source_target_pairs={{0,1},{1,2},{2,3},{3,4},{4,5},{5,6},{6,7},{7,8},{8,9},{9,10},{10,1... | collective-permute-start | bytes 196616 | tf_op jit(solution)/shard_map/ppermute | solution.py:530
  107.7 5.5 %collective-permute-start.8 = (bf16[256,128]{1,0:T(8,128)(2,1)}, bf16[256,128]{1,0:T(8,128)(2,1)S(1)}, u32[]{:S(2)}, u32[]{:S(2)}) collective-permute-start(bf16[256,128]{1,0:T(8,128)(2,1)} %get-tuple-element.105), channel_id=1, source_target_pairs={{1,0},{2,1},{3,2},{4,3},{5,4},{6,5},{7,6},{8,7},{9,8},{10,9},{11,1... | collective-permute-start | bytes 196616 | tf_op jit(solution)/shard_map/ppermute | solution.py:531
  109.0 12.6 %copy-start.28 = (bf16[256,128]{1,0:T(8,128)(2,1)}, bf16[256,128]{1,0:T(8,128)(2,1)S(1)}, u32[]{:S(2)}) copy-start(bf16[256,128]{1,0:T(8,128)(2,1)S(1)} %collective-permute-done.5.refs_3_) | copy-start | bytes 196612
  109.0 12.6 %copy-start.29 = (bf16[256,128]{1,0:T(8,128)(2,1)}, bf16[256,128]{1,0:T(8,128)(2,1)S(1)}, u32[]{:S(2)}) copy-start(bf16[256,128]{1,0:T(8,128)(2,1)S(1)} %collective-permute-done.6.refs_4_) | copy-start | bytes 196612
  109.3 12.3 %copy-start.30 = (bf16[256,128]{1,0:T(8,128)(2,1)}, bf16[256,128]{1,0:T(8,128)(2,1)S(1)}, u32[]{:S(2)}) copy-start(bf16[256,128]{1,0:T(8,128)(2,1)S(1)} %collective-permute-done.7.refs_5_) | copy-start | bytes 196612
  113.2 8.4 %copy-start.31 = (bf16[256,128]{1,0:T(8,128)(2,1)}, bf16[256,128]{1,0:T(8,128)(2,1)S(1)}, u32[]{:S(2)}) copy-start(bf16[256,128]{1,0:T(8,128)(2,1)S(1)} %collective-permute-done.8.refs_6_) | copy-start | bytes 196612
  113.2 0.7 copy-start.6
  115.6 24.5 %all-to-all-start.4 = ((f32[32,1,1152]{2,1,0:T(1,128)}), f32[32,1,1152]{2,1,0:T(1,128)S(1)}, u32[]{:S(2)}, u32[]{:S(2)}) async-start(f32[32,1,1152]{2,1,0:T(1,128)} %shard_map.83), calls=%async_computation.4 | async-start | bytes 294912 | tf_op jit(solution)/shard_map/all_to_all | solution.py:536
  125.2 9.9 %collective-permute-start.9 = (f32[256,128]{1,0:T(8,128)}, f32[256,128]{1,0:T(8,128)S(1)}, u32[]{:S(2)}, u32[]{:S(2)}) collective-permute-start(f32[256,128]{1,0:T(8,128)} %get-tuple-element.112), channel_id=1, source_target_pairs={{0,16},{16,32},{32,48},{48,64},{64,80},{80,96},{96,112},{112,128},... | collective-permute-start | bytes 393224 | tf_op jit(solution)/shard_map/ppermute | solution.py:530
  128.7 6.8 %collective-permute-start.10 = (f32[256,128]{1,0:T(8,128)}, f32[256,128]{1,0:T(8,128)S(1)}, u32[]{:S(2)}, u32[]{:S(2)}) collective-permute-start(f32[256,128]{1,0:T(8,128)} %get-tuple-element.113), channel_id=1, source_target_pairs={{16,0},{32,16},{48,32},{64,48},{80,64},{96,80},{112,96},{128,112},... | collective-permute-start | bytes 393224 | tf_op jit(solution)/shard_map/ppermute | solution.py:531
  130.6 5.4 %collective-permute-start.11 = (f32[256,128]{1,0:T(8,128)}, f32[256,128]{1,0:T(8,128)S(1)}, u32[]{:S(2)}, u32[]{:S(2)}) collective-permute-start(f32[256,128]{1,0:T(8,128)} %get-tuple-element.114), channel_id=1, source_target_pairs={{0,1},{1,2},{2,3},{3,4},{4,5},{5,6},{6,7},{7,8},{8,9},{9,10},{10,1... | collective-permute-start | bytes 393224 | tf_op jit(solution)/shard_map/ppermute | solution.py:530
  133.7 6.3 %collective-permute-start.12 = (f32[256,128]{1,0:T(8,128)}, f32[256,128]{1,0:T(8,128)S(1)}, u32[]{:S(2)}, u32[]{:S(2)}) collective-permute-start(f32[256,128]{1,0:T(8,128)} %get-tuple-element.115), channel_id=1, source_target_pairs={{1,0},{2,1},{3,2},{4,3},{5,4},{6,5},{7,6},{8,7},{9,8},{10,9},{11,1... | collective-permute-start | bytes 393224 | tf_op jit(solution)/shard_map/ppermute | solution.py:531
  135.0 23.6 %copy-start.11 = (f32[256,128]{1,0:T(8,128)}, f32[256,128]{1,0:T(8,128)S(1)}, u32[]{:S(2)}) copy-start(f32[256,128]{1,0:T(8,128)S(1)} %collective-permute-done.9.refs_10_.refs_11_) | copy-start | bytes 393220
  135.5 23.1 %copy-start.12 = (f32[256,128]{1,0:T(8,128)}, f32[256,128]{1,0:T(8,128)S(1)}, u32[]{:S(2)}) copy-start(f32[256,128]{1,0:T(8,128)S(1)} %collective-permute-done.10.refs_11_.refs_12_) | copy-start | bytes 393220
  136.1 22.6 %copy-start.13 = (f32[256,128]{1,0:T(8,128)}, f32[256,128]{1,0:T(8,128)S(1)}, u32[]{:S(2)}) copy-start(f32[256,128]{1,0:T(8,128)S(1)} %collective-permute-done.11.refs_12_.refs_13_) | copy-start | bytes 393220
  140.1 18.6 %copy-start.14 = (f32[256,128]{1,0:T(8,128)}, f32[256,128]{1,0:T(8,128)S(1)}, u32[]{:S(2)}) copy-start(f32[256,128]{1,0:T(8,128)S(1)} %collective-permute-done.12.refs_13_.refs_14_) | copy-start | bytes 393220
  140.1 0.7 copy-start.8
  163.5 20.8 %all-to-all-start.6 = ((f32[16,32,128]{2,1,0:T(8,128)}), f32[16,32,128]{2,1,0:T(8,128)S(1)}, u32[]{:S(2)}, u32[]{:S(2)}) async-start(f32[16,32,128]{2,1,0:T(8,128)} %get-tuple-element.126), calls=%async_computation.6 | async-start | bytes 524288 | tf_op jit(solution)/shard_map/all_to_all | solution.py:536
  167.0 12.7 %collective-permute-start.13 = (f32[256,128]{1,0:T(8,128)}, f32[256,128]{1,0:T(8,128)S(1)}, u32[]{:S(2)}, u32[]{:S(2)}) collective-permute-start(f32[256,128]{1,0:T(8,128)} %get-tuple-element.127), channel_id=1, source_target_pairs={{0,16},{16,32},{32,48},{48,64},{64,80},{80,96},{96,112},{112,128},... | collective-permute-start | bytes 393224 | tf_op jit(solution)/shard_map/ppermute | solution.py:530
  173.0 6.8 %collective-permute-start.14 = (f32[256,128]{1,0:T(8,128)}, f32[256,128]{1,0:T(8,128)S(1)}, u32[]{:S(2)}, u32[]{:S(2)}) collective-permute-start(f32[256,128]{1,0:T(8,128)} %get-tuple-element.128), channel_id=1, source_target_pairs={{16,0},{32,16},{48,32},{64,48},{80,64},{96,80},{112,96},{128,112},... | collective-permute-start | bytes 393224 | tf_op jit(solution)/shard_map/ppermute | solution.py:531
  175.0 5.7 %collective-permute-start.15 = (f32[256,128]{1,0:T(8,128)}, f32[256,128]{1,0:T(8,128)S(1)}, u32[]{:S(2)}, u32[]{:S(2)}) collective-permute-start(f32[256,128]{1,0:T(8,128)} %get-tuple-element.129), channel_id=1, source_target_pairs={{0,1},{1,2},{2,3},{3,4},{4,5},{5,6},{6,7},{7,8},{8,9},{9,10},{10,1... | collective-permute-start | bytes 393224 | tf_op jit(solution)/shard_map/ppermute | solution.py:530
  178.4 5.9 %collective-permute-start.16 = (f32[256,128]{1,0:T(8,128)}, f32[256,128]{1,0:T(8,128)S(1)}, u32[]{:S(2)}, u32[]{:S(2)}) collective-permute-start(f32[256,128]{1,0:T(8,128)} %get-tuple-element.130), channel_id=1, source_target_pairs={{1,0},{2,1},{3,2},{4,3},{5,4},{6,5},{7,6},{8,7},{9,8},{10,9},{11,1... | collective-permute-start | bytes 393224 | tf_op jit(solution)/shard_map/ppermute | solution.py:531
  179.7 22.9 %copy-start.23 = (f32[256,128]{1,0:T(8,128)}, f32[256,128]{1,0:T(8,128)S(1)}, u32[]{:S(2)}) copy-start(f32[256,128]{1,0:T(8,128)S(1)} %collective-permute-done.13.refs_3_) | copy-start | bytes 393220
  179.8 22.8 %copy-start.25 = (f32[256,128]{1,0:T(8,128)}, f32[256,128]{1,0:T(8,128)S(1)}, u32[]{:S(2)}) copy-start(f32[256,128]{1,0:T(8,128)S(1)} %collective-permute-done.14.refs_4_) | copy-start | bytes 393220
  180.6 22.0 %copy-start.26 = (f32[256,128]{1,0:T(8,128)}, f32[256,128]{1,0:T(8,128)S(1)}, u32[]{:S(2)}) copy-start(f32[256,128]{1,0:T(8,128)S(1)} %collective-permute-done.15.refs_5_) | copy-start | bytes 393220
  184.3 18.3 %copy-start.27 = (f32[256,128]{1,0:T(8,128)}, f32[256,128]{1,0:T(8,128)S(1)}, u32[]{:S(2)}) copy-start(f32[256,128]{1,0:T(8,128)S(1)} %collective-permute-done.16.refs_6_) | copy-start | bytes 393220
  184.3 0.7 copy-start.7
  186.7 34.4 %all-to-all-start.7 = ((f32[32,1,1152]{2,1,0:T(1,128)}), f32[32,1,1152]{2,1,0:T(1,128)S(1)}, u32[]{:S(2)}, u32[]{:S(2)}) async-start(f32[32,1,1152]{2,1,0:T(1,128)} %shard_map.87), calls=%async_computation.7 | async-start | bytes 294912 | tf_op jit(solution)/shard_map/all_to_all | solution.py:536
  206.3 9.9 %collective-permute-start.17 = (f32[256,128]{1,0:T(8,128)}, f32[256,128]{1,0:T(8,128)S(1)}, u32[]{:S(2)}, u32[]{:S(2)}) collective-permute-start(f32[256,128]{1,0:T(8,128)} %get-tuple-element.137), channel_id=1, source_target_pairs={{0,16},{16,32},{32,48},{48,64},{64,80},{80,96},{96,112},{112,128},... | collective-permute-start | bytes 393224 | tf_op jit(solution)/shard_map/ppermute | solution.py:530
  209.8 6.8 %collective-permute-start.18 = (f32[256,128]{1,0:T(8,128)}, f32[256,128]{1,0:T(8,128)S(1)}, u32[]{:S(2)}, u32[]{:S(2)}) collective-permute-start(f32[256,128]{1,0:T(8,128)} %get-tuple-element.138), channel_id=1, source_target_pairs={{16,0},{32,16},{48,32},{64,48},{80,64},{96,80},{112,96},{128,112},... | collective-permute-start | bytes 393224 | tf_op jit(solution)/shard_map/ppermute | solution.py:531
  211.8 5.4 %collective-permute-start.19 = (f32[256,128]{1,0:T(8,128)}, f32[256,128]{1,0:T(8,128)S(1)}, u32[]{:S(2)}, u32[]{:S(2)}) collective-permute-start(f32[256,128]{1,0:T(8,128)} %get-tuple-element.139), channel_id=1, source_target_pairs={{0,1},{1,2},{2,3},{3,4},{4,5},{5,6},{6,7},{7,8},{8,9},{9,10},{10,1... | collective-permute-start | bytes 393224 | tf_op jit(solution)/shard_map/ppermute | solution.py:530
  214.9 6.3 %collective-permute-start.20 = (f32[256,128]{1,0:T(8,128)}, f32[256,128]{1,0:T(8,128)S(1)}, u32[]{:S(2)}, u32[]{:S(2)}) collective-permute-start(f32[256,128]{1,0:T(8,128)} %get-tuple-element.140), channel_id=1, source_target_pairs={{1,0},{2,1},{3,2},{4,3},{5,4},{6,5},{7,6},{8,7},{9,8},{10,9},{11,1... | collective-permute-start | bytes 393224 | tf_op jit(solution)/shard_map/ppermute | solution.py:531
  216.2 23.7 %copy-start.16 = (f32[256,128]{1,0:T(8,128)}, f32[256,128]{1,0:T(8,128)S(1)}, u32[]{:S(2)}) copy-start(f32[256,128]{1,0:T(8,128)S(1)} %collective-permute-done.17.refs_16_) | copy-start | bytes 393220
  216.6 23.2 %copy-start.17 = (f32[256,128]{1,0:T(8,128)}, f32[256,128]{1,0:T(8,128)S(1)}, u32[]{:S(2)}) copy-start(f32[256,128]{1,0:T(8,128)S(1)} %collective-permute-done.18.refs_17_) | copy-start | bytes 393220
  217.2 22.7 %copy-start.18 = (f32[256,128]{1,0:T(8,128)}, f32[256,128]{1,0:T(8,128)S(1)}, u32[]{:S(2)}) copy-start(f32[256,128]{1,0:T(8,128)S(1)} %collective-permute-done.19.refs_18_) | copy-start | bytes 393220
  221.2 18.7 %copy-start.19 = (f32[256,128]{1,0:T(8,128)}, f32[256,128]{1,0:T(8,128)S(1)}, u32[]{:S(2)}) copy-start(f32[256,128]{1,0:T(8,128)S(1)} %collective-permute-done.20.refs_19_) | copy-start | bytes 393220
  221.2 0.7 copy-start.9
  256.9 32.9 %all-to-all-start.10 = ((f32[32,8,128]{2,1,0:T(8,128)}), f32[32,8,128]{2,1,0:T(8,128)S(1)}, u32[]{:S(2)}, u32[]{:S(2)}) async-start(f32[32,8,128]{2,1,0:T(8,128)} %shard_map.91), calls=%async_computation.10 | async-start | bytes 262144 | tf_op jit(solution)/shard_map/all_to_all | solution.py:536
  275.5 12.1 %collective-permute-start.21 = (f32[256,128]{1,0:T(8,128)}, f32[256,128]{1,0:T(8,128)S(1)}, u32[]{:S(2)}, u32[]{:S(2)}) collective-permute-start(f32[256,128]{1,0:T(8,128)} %get-tuple-element.156), channel_id=1, source_target_pairs={{0,16},{16,32},{32,48},{48,64},{64,80},{80,96},{96,112},{112,128},... | collective-permute-start | bytes 393224 | tf_op jit(solution)/shard_map/ppermute | solution.py:530
  279.0 8.5 %collective-permute-start.22 = (f32[256,128]{1,0:T(8,128)}, f32[256,128]{1,0:T(8,128)S(1)}, u32[]{:S(2)}, u32[]{:S(2)}) collective-permute-start(f32[256,128]{1,0:T(8,128)} %get-tuple-element.157), channel_id=1, source_target_pairs={{16,0},{32,16},{48,32},{64,48},{80,64},{96,80},{112,96},{128,112},... | collective-permute-start | bytes 393224 | tf_op jit(solution)/shard_map/ppermute | solution.py:531
  281.0 6.6 %collective-permute-start.23 = (f32[256,128]{1,0:T(8,128)}, f32[256,128]{1,0:T(8,128)S(1)}, u32[]{:S(2)}, u32[]{:S(2)}) collective-permute-start(f32[256,128]{1,0:T(8,128)} %get-tuple-element.158), channel_id=1, source_target_pairs={{0,1},{1,2},{2,3},{3,4},{4,5},{5,6},{6,7},{7,8},{8,9},{9,10},{10,1... | collective-permute-start | bytes 393224 | tf_op jit(solution)/shard_map/ppermute | solution.py:530
  283.2 6.6 %collective-permute-start.24 = (f32[256,128]{1,0:T(8,128)}, f32[256,128]{1,0:T(8,128)S(1)}, u32[]{:S(2)}, u32[]{:S(2)}) collective-permute-start(f32[256,128]{1,0:T(8,128)} %get-tuple-element.159), channel_id=1, source_target_pairs={{1,0},{2,1},{3,2},{4,3},{5,4},{6,5},{7,6},{8,7},{9,8},{10,9},{11,1... | collective-permute-start | bytes 393224 | tf_op jit(solution)/shard_map/ppermute | solution.py:531
  287.6 2.3 copy-start.20
  287.6 2.2 copy-start.21
  287.6 2.2 copy-start.22
  289.8 0.7 copy-start.24
  289.8 0.7 copy-start.15

commit v3 on v2

--- a/solution.py
+++ b/solution.py
@@ -17,11 +17,13 @@
 SL = R // NY
 NCG = 1024
 VMEM_BYTES = 60 * 1024 * 1024
+SOME_BYTES = 16 * 1024 * 1024
 PAD = 32
 LONG = SL * 128 + 128
 WIN = 32
 
 ANY = pl.BlockSpec(memory_space=pl.ANY)
+VMEM = pl.BlockSpec(memory_space=pltpu.VMEM)
 SMEM = pl.BlockSpec(memory_space=pltpu.SMEM)
 
 
@@ -78,11 +80,21 @@
         return ref.at[rows] if self.array.ndim == 2 else ref.at[:, rows]
 
 
-def call(kernel, args, outs, scratch=(), smem=0, flops=0):
+class Near(NamedTuple):
+    array: jax.Array
+
+
+class Small(NamedTuple):
+    shape: tuple
+    dtype: jnp.dtype
+
+
+def call(kernel, args, outs, scratch=(), smem=0, flops=0, limit=VMEM_BYTES):
     inputs = args[smem:]
     count = len(inputs)
     parts = [a if isinstance(a, Part) else None for a in inputs]
-    args = [a.array if isinstance(a, Part) else a for a in args]
+    near = [isinstance(a, Near) for a in inputs] + [isinstance(t, Small) for t in outs]
+    args = [a.array if isinstance(a, (Part, Near)) else a for a in args]
     size = sum(a.size * a.dtype.itemsize for a in args)
     shapes = [
         a.shape if part is None else part.shape() for a, part in zip(args[smem:], parts)
@@ -96,26 +108,36 @@
         sources = [
             ref if part is None else part.of(ref) for ref, part in zip(outside, parts)
         ]
-        taken = [Taken(sources[i], buffers[i], semaphores.at[i]) for i in range(count)]
-        given = [Given(outside[i], buffers[i], semaphores.at[i]) for i in range(count, whole)]
-        kernel(*scalars, *taken, *given, *rest)
-        for value in given:
-            value.send()
-        for value in taken:
-            value.wait()
-        for value in given:
-            value.copy.wait()
+        moving = [i for i in range(whole) if not near[i]]
+        values = list(outside)
+        for i in moving:
+            if i < count:
+                values[i] = Taken(sources[i], buffers[i], semaphores.at[i])
+            else:
+                values[i] = Given(outside[i], buffers[i], semaphores.at[i])
+        kernel(*scalars, *values, *rest)
+        for i in moving:
+            if i >= count:
+                values[i].send()
+        for i in moving:
+            if i < count:
+                values[i].wait()
+            else:
+                values[i].copy.wait()
 
     return pl.pallas_call(
         moved,
-        out_shape=tuple(jax.ShapeDtypeStruct(s, d) for s, d in outs),
-        in_specs=[SMEM] * smem + [ANY] * count,
-        out_specs=tuple(ANY for _ in outs),
-        scratch_shapes=[pltpu.VMEM(t, a.dtype) for t, a in zip(shapes, args[smem:])]
-        + [pltpu.VMEM(s, d) for s, d in outs]
+        out_shape=tuple(jax.ShapeDtypeStruct(*t) for t in outs),
+        in_specs=[SMEM] * smem + [VMEM if n else ANY for n in near[:count]],
+        out_specs=tuple(VMEM if n else ANY for n in near[count:]),
+        scratch_shapes=[
+            pltpu.VMEM((8, 128) if n else t, a.dtype)
+            for n, t, a in zip(near, shapes, args[smem:])
+        ]
+        + [pltpu.VMEM((8, 128) if n else t[0], t[1]) for n, t in zip(near[count:], outs)]
         + [pltpu.SemaphoreType.DMA((whole,))]
         + list(scratch),
-        compiler_params=pltpu.CompilerParams(vmem_limit_bytes=VMEM_BYTES),
+        compiler_params=pltpu.CompilerParams(vmem_limit_bytes=limit),
         cost_estimate=pl.CostEstimate(flops=flops, bytes_accessed=size, transcendentals=0),
     )(*args)
 
@@ -150,9 +172,19 @@
             out[row : row + 2, column : column + width] = piece[slot : slot + 2]
 
 
+def shared(ax, ay):
+    return ax[0] > 0, ax[0] < NX - 1, ay[0] > 0, ay[0] < NY - 1
+
+
 def weights(ax, ay):
-    shared = (ax[0] > 0, ax[0] < NX - 1, ay[0] > 0, ay[0] < NY - 1)
-    return [jnp.where(face, 0.5, 1.0).astype(F32) for face in shared]
+    return [jnp.where(face, 0.5, 1.0).astype(F32) for face in shared(ax, ay)]
+
+
+def facing(ax, ay, faces):
+    return [
+        jnp.where(there, face[0:FACE].astype(F32), 0.0)
+        for there, face in zip(shared(ax, ay), faces)
+    ]
 
 
 def thirds(value):
@@ -190,18 +222,13 @@
         face[FACE + 8 : FACE + 16] = basis[:, FACE * i + 128 : FACE * (i + 1)].astype(F32)
 
 
-def faces_kernel(s, f0, f1, f2, f3):
-    for i, face in enumerate((f0, f1, f2, f3)):
-        face[...] = s[rows(i)]
-        face.send()
-
-
-def window_kernel(basis, f0, f1, f2, f3, b_out, bt_out, table):
+def window_kernel(ax, ay, basis, f0, f1, f2, f3, b_out, bt_out, table):
     table[...] = jnp.zeros((2 * WIN, NI), F32)
     place(table, 0, 0, basis[...].astype(F32), 1, 1)
+    there = shared(ax, ay)
     for i, (face, dx0, dy0) in enumerate(((f0, 0, 1), (f1, 2, 1), (f2, 1, 0), (f3, 1, 2))):
         for h in range(2):
-            piece = face[FACE + 8 * h : FACE + 8 * h + 8]
+            piece = jnp.where(there[i], face[FACE + 8 * h : FACE + 8 * h + 8], 0.0)
             place(table, WIN, FACE * i + 128 * h, piece, dx0, dy0)
     b_out[...] = table[...].astype(BF16)
     bt_out[...] = jnp.transpose(table[...]).astype(BF16)
@@ -210,8 +237,8 @@
 def local_kernel(ax, ay, s, f0, f1, f2, f3, inverse, q_out, l_out, g0, g1, g2, g3):
     wt = weights(ax, ay)
     parts = []
-    for i, face in enumerate((f0, f1, f2, f3)):
-        q = s[rows(i)].astype(F32) + face[...].astype(F32)
+    for i, face in enumerate(facing(ax, ay, (f0, f1, f2, f3))):
+        q = s[rows(i)].astype(F32) + face
         q_out[rows(i)] = q
         parts.append((wt[i] * q).astype(BF16))
     q_out.send()
@@ -227,11 +254,11 @@
     return jnp.transpose(m[...].reshape(R, 128))
 
 
-def blended(wt, i, window_t, y, mine, facing):
+def blended(wt, i, window_t, y, mine, other):
     y = y[0:WIN].astype(BF16)
     mine = mine + wt[i] * dot(window_t[rows(i), 0:WIN], y)
-    facing = facing + wt[i] * dot(window_t[rows(i), WIN:], y)
-    return mine.astype(BF16).astype(F32) + facing.astype(BF16).astype(F32)
+    other = other + wt[i] * dot(window_t[rows(i), WIN:], y)
+    return mine.astype(BF16).astype(F32) + other.astype(BF16).astype(F32)
 
 
 def split(value):
@@ -275,8 +302,8 @@
 ):
     wt = weights(ax, ay)
     y = arrived(m)
-    for i, face in enumerate((f0, f1, f2, f3)):
-        z = blended(wt, i, window_t, y, l0[rows(i)], face[0:FACE])
+    for i, face in enumerate(facing(ax, ay, (f0, f1, f2, f3))):
+        z = blended(wt, i, window_t, y, l0[rows(i)], face)
         z_out[rows(i)] = z
         zb[rows(i)] = z.astype(BF16)
     z_out.send()
@@ -303,10 +330,11 @@
     got = arrived(m)
     got_out[...] = got[WIN : WIN + 8]
     alpha = got[WIN : WIN + 1]
-    for i, (before, face) in enumerate(((e0, f0), (e1, f1), (e2, f2), (e3, f3))):
+    before = facing(ax, ay, (e0, e1, e2, e3))
+    first = facing(ax, ay, (f0, f1, f2, f3))
+    for i in range(4):
         mine = l0[rows(i)] - alpha * l1[rows(i)]
-        facing = before[0:FACE] - alpha * face[...]
-        z = blended(wt, i, window_t, got, mine, facing)
+        z = blended(wt, i, window_t, got, mine, before[i] - alpha * first[i])
         z_out[rows(i)] = z
         zb[rows(i)] = split(z)
     z_out.send()
@@ -326,7 +354,7 @@
 def third_kernel(
     ax, ay, m, got0, window_t, l0, d0, d1, d2, d3, l1, e0, e1, e2, e3, l2, f0, f1, f2, f3,
     schur, q0, q1, s0, s1, load,
-    z_out, s_out, msg_out, got_out, zb,
+    z_out, s_out, g0, g1, g2, g3, msg_out, got_out, zb,
 ):
     wt = weights(ax, ay)
     got = arrived(m)
@@ -335,15 +363,17 @@
     alpha = got[WIN : WIN + 1]
     beta = got[WIN + 1 : WIN + 2]
     scale = alpha0 + alpha * beta
-    faces = ((d0, e0, f0), (d1, e1, f1), (d2, e2, f2), (d3, e3, f3))
-    for i, (before, first, second) in enumerate(faces):
+    before = facing(ax, ay, (d0, d1, d2, d3))
+    first = facing(ax, ay, (e0, e1, e2, e3))
+    second = facing(ax, ay, (f0, f1, f2, f3))
+    for i in range(4):
         mine = l0[rows(i)] - scale * l1[rows(i)] - alpha * l2[rows(i)]
-        facing = before[0:FACE] - scale * first[...] - alpha * second[...]
-        z = blended(wt, i, window_t, got, mine, facing)
+        other = before[i] - scale * first[i] - alpha * second[i]
+        z = blended(wt, i, window_t, got, mine, other)
         z_out[rows(i)] = z
         zb[rows(i)] = split(z)
     z_out.send()
-    apply_schur(schur, zb, s_out, ())
+    apply_schur(schur, zb, s_out, (g0, g1, g2, g3))
     rz = jnp.zeros((1, R), F32)
     zz = jnp.zeros((1, R), F32)
     zq = jnp.zeros((1, R), F32)
@@ -354,8 +384,8 @@
         rz += total(wt[i] * r * z)
         zz += total(z * s_out[rows(i)])
         zq += total(z * s)
-    inner = jnp.concatenate([rz, zz, zq, jnp.zeros((5, R), F32)], axis=0)
-    msg_out[...] = jnp.broadcast_to(inner[None], (NY, 8, R))
+    inner = jnp.concatenate([rz, zz, zq, jnp.zeros((PAD - 3, R), F32)], axis=0)
+    msg_out[...] = jnp.broadcast_to(inner[None], (NY, PAD, R))
 
 
 def update_kernel(got0, got1, z0, z1, q0, q1, load, x_out, p_out, q_out, r_out):
@@ -371,7 +401,7 @@
         r_out[rows(i)] = load[rows(i)].astype(F32) - alpha0 * q0[rows(i)] - alpha * q
 
 
-def last_kernel(m, got, s, f0, f1, f2, f3, z, p, q, x, r, x_out, r_out):
+def last_kernel(ax, ay, m, got, s, f0, f1, f2, f3, z, p, q, x, r, x_out, r_out):
     inner = jnp.sum(m[...], axis=0)
     rz1 = got[2:3]
     pq1 = got[3:4]
@@ -379,8 +409,8 @@
     beta = rz / rz1
     pq = inner[1:2] + 2.0 * beta * inner[2:3] + beta * beta * pq1
     alpha = rz / pq
-    for i, face in enumerate((f0, f1, f2, f3)):
-        product = s[rows(i)] + face[...] + beta * q[rows(i)]
+    for i, face in enumerate(facing(ax, ay, (f0, f1, f2, f3))):
+        product = s[rows(i)] + face + beta * q[rows(i)]
         direction = z[rows(i)] + beta * p[rows(i)]
         x_out[rows(i)] = (x[rows(i)] + alpha * direction).astype(BF16)
         r_out[rows(i)] = (r[rows(i)] - alpha * product).astype(BF16)
@@ -521,23 +551,24 @@
     out[...] = jnp.broadcast_to(jnp.sum(m[...], axis=0)[None], (NX, 8, R))
 
 
-def across(faces):
-    low_x, high_x, low_y, high_y = faces
-    result = []
-    for axis, size, low, high in (("gx", NX, low_x, high_x), ("gy", NY, low_y, high_y)):
-        up = [(i, i + 1) for i in range(size - 1)]
-        down = [(j, i) for i, j in up]
-        result.append(lax.ppermute(high, axis, up))
-        result.append(lax.ppermute(low, axis, down))
-    return result
+def across(axis, low, high):
+    size = {"gx": NX, "gy": NY}[axis]
+    up = [(i, (i + 1) % size) for i in range(size)]
+    down = [(j, i) for i, j in up]
+    return lax.ppermute(high, axis, up), lax.ppermute(low, axis, down)
+
+
+def all_across(low_x, high_x, low_y, high_y):
+    y = across("gy", low_y, high_y)
+    return *across("gx", low_x, high_x), *y
+
+
+def together(*values):
+    return lax.optimization_barrier(values)
 
 
 def swap(value, axis):
     return lax.all_to_all(value, axis, 0, 0, tiled=True)
-
-
-def after(value, *others):
-    return lax.optimization_barrier((value, *others))[0]
 
 
 def body(load_cases, schur_blocks, local_inverse, coarse_basis, corner_ids, coarse_inverse):
@@ -550,6 +581,7 @@
 
     tall = (NI, R)
     msg = ((NY, SL, 128), F32)
+    padded = ((NY, PAD, 128), F32)
     wide = ((NX, 1, LONG), F32)
     columns = pltpu.VMEM((NX, SL, 128), F32)
     block = 2 * NI * NI * R
@@ -571,20 +603,21 @@
         [((FACE + 16, R), F32)] * 4,
         flops=block,
     )
-    faces0 = across((f0, f1, f2, f3))
-    mine, *faces0 = lax.optimization_barrier((swap(m, "gy"), *faces0))
+    faces0 = all_across(f0, f1, f2, f3)
+    mine, *faces0 = together(swap(m, "gy"), *faces0)
     other = lax.ppermute(mine, "gx", [(i, i ^ 1) for i in range(NX)])
-    (m,) = call(first_column_kernel, (Part(mine, FACE, 32),), [wide])
+    (m,) = call(first_column_kernel, (Part(mine, FACE, 32),), [wide], limit=SOME_BYTES)
     m = swap(m, "gx")
     window, window_t = call(
         window_kernel,
-        (basis, *faces0),
+        (*here, basis, *faces0),
         [((2 * WIN, NI), BF16), ((NI, 2 * WIN), BF16)],
         [pltpu.VMEM((2 * WIN, NI), F32)],
+        smem=2,
     )
     sums0, picked, m = call(
         first_solve_kernel,
-        (here[0], after(m, window), Part(mine, 0, FACE), Part(other, 0, FACE)),
+        (here[0], together(m, window)[0], Part(mine, 0, FACE), Part(other, 0, FACE)),
         [((SL, NCG), F32), ((NCG, 128), BF16), msg],
         [columns, pltpu.VMEM((NCG, 128), BF16), pltpu.VMEM((NCG, NCG), BF16)],
         smem=1,
@@ -594,15 +627,15 @@
     z0, s0, g0, g1, g2, g3, m = call(
         first_kernel,
         (*here, m, window_t, l0, *faces0, schur, window, load),
-        [(tall, F32), (tall, BF16)] + [((FACE, R), BF16)] * 4 + [((NY, PAD, 128), F32)],
+        [(tall, F32), (tall, BF16)] + [((FACE, R), BF16)] * 4 + [padded],
         [table, pltpu.VMEM(tall, BF16)],
         smem=2,
         flops=block,
     )
 
     def stage(s, faces, m):
-        m, *faces = lax.optimization_barrier((swap(m, "gy"), *across(faces)))
-        (m,) = call(column_kernel, (Part(m, 0, SL),), [wide])
+        m, *faces = together(swap(m, "gy"), *all_across(*faces))
+        (m,) = call(column_kernel, (Part(m, 0, SL),), [wide], limit=SOME_BYTES)
         q, l, *faces = call(
             local_kernel,
             (*here, s, *faces, inverse),
@@ -610,21 +643,22 @@
             smem=2,
             flops=block,
         )
-        m, *faces = lax.optimization_barrier((swap(m, "gx"), *across(faces)))
+        m, *faces = together(swap(m, "gx"), *all_across(*faces))
         return m, q, l, faces
 
     m, q0, l1, faces1 = stage(s0, (g0, g1, g2, g3), m)
     change0, sums1, kept, m = call(
         second_solve_kernel,
-        (m, sums0, picked),
+        (Near(m), sums0, picked),
         [((SL, NCG), F32), ((SL, NCG), F32), ((SL, 128), F32), msg],
         [columns],
+        limit=SOME_BYTES,
     )
     m = swap(m, "gy")
     z1, s1, g0, g1, g2, g3, m, got0 = call(
         second_kernel,
         (*here, m, window_t, l0, *faces0, l1, *faces1, schur, window, q0, s0, load),
-        [(tall, F32), (tall, F32)] + [face] * 4 + [((NY, PAD, 128), F32), ((8, R), F32)],
+        [(tall, F32), (tall, F32)] + [face] * 4 + [padded, ((8, R), F32)],
         [table, zb],
         smem=2,
         flops=block,
@@ -633,37 +667,39 @@
     m, q1, l2, faces2 = stage(s1, (g0, g1, g2, g3), m)
     (m,) = call(
         third_solve_kernel,
-        (m, sums1, picked, change0, kept),
+        (Near(m), sums1, picked, change0, kept),
         [msg],
         [columns, pltpu.VMEM((SL, NCG), F32)],
+        limit=SOME_BYTES,
     )
     m = swap(m, "gy")
-    z2, s2, m, got1 = call(
+    z2, s2, g0, g1, g2, g3, m, got1 = call(
         third_kernel,
         (
             *here, m, got0, window_t, l0, *faces0, l1, *faces1, l2, *faces2,
             schur, q0, q1, s0, s1, load,
         ),
-        [(tall, F32), (tall, F32), ((NY, 8, R), F32), ((8, R), F32)],
+        [(tall, F32), (tall, F32)] + [face] * 4 + [padded, ((8, R), F32)],
         [zb],
         smem=2,
         flops=block,
     )
 
-    m = swap(m, "gy")
-    (sums,) = call(last_column_kernel, (m,), [((NX, 8, R), F32)])
-    faces = across(call(faces_kernel, (after(s2, m),), [face] * 4, flops=block))
+    m, *faces, g2, g3, z0 = together(swap(m, "gy"), *across("gx", g0, g1), g2, g3, z0)
+    (sums,) = call(last_column_kernel, (Part(m, 0, SL),), [((NX, 8, R), F32)], limit=SOME_BYTES)
+    faces += across("gy", g2, g3)
     x2, p1, q1, r2 = call(
         update_kernel,
-        (got0, got1, after(z0, m), z1, q0, q1, load),
+        (got0, got1, z0, z1, q0, q1, load),
         [(tall, F32)] * 4,
         flops=block,
     )
     m = swap(sums, "gx")
     x, r = call(
         last_kernel,
-        (m, got1, s2, *faces, z2, p1, q1, x2, r2),
+        (*here, m, got1, s2, *faces, z2, p1, q1, x2, r2),
         [(tall, BF16), (tall, BF16)],
+        smem=2,
     )
     return x[None, None], r[None, None]
 

time: 298 us -> 272 us (0.913)
  blocking collectives: 56.4 us -> 37 us
  starting transfers between devices: 136 us -> 148 us
  Pallas kernels: 52.8 us -> 44.6 us
  waiting for transfers between devices: 41.8 us -> 37.3 us
    all_to_all x4 -> x3, blocking collectives: 56.4 us -> 37 us  [swap(): return lax.all_to_all(value, axis, 0, 0, tiled=True)]
    ppermute x24, waiting for transfers between devices: 27.4 us -> 18.5 us  [across(): return (lax.ppermute(high, axis, up), lax.ppermute(low, axis, down))]
    pallas_call x18 -> x17, Pallas kernels: 52.8 us -> 44.6 us  [call(): pl.pallas_call(moved, out_shape=tuple((jax.ShapeDtypeStruct(*t) for t in...]
    ppermute x24, starting transfers between devices: 64 us -> 70.7 us  [across(): return (lax.ppermute(high, axis, up), lax.ppermute(low, axis, down))]
    all_to_all x7 -> x8, waiting for transfers between devices: 14.4 us -> 18.7 us  [swap(): return lax.all_to_all(value, axis, 0, 0, tiled=True)]
    ppermute x1, starting transfers between devices: 3.27 us -> 6.32 us  [body(): other = lax.ppermute(mine, 'gx', [(i, i ^ 1) for i in range(NX)])]
    all_to_all x7 -> x8, starting transfers between devices: 68.7 us -> 70.6 us  [swap(): return lax.all_to_all(value, axis, 0, 0, tiled=True)]
  transfers between devices with their start and end apart: 32 -> 33, of which waited for: 16 -> 13; matrix products, arithmetic and copies ran while one was open for 0% -> 0% of each run, Pallas kernels for 6% -> 6%
where the time goes in v3:
time: 272 us; the launch traced here: 270 us
  starting transfers between devices  148 us (54%)
  Pallas kernels  44.6 us (16%)
  waiting for transfers between devices  37.3 us (14%)
  blocking collectives  37 us (14%)
    ppermute x24, starting transfers between devices, across(): return (lax.ppermute(high, axis, up), lax.ppermute(low, axis, down))  70.7 us
    all_to_all x8, starting transfers between devices, swap(): return lax.all_to_all(value, axis, 0, 0, tiled=True)  70.6 us
    pallas_call x17, Pallas kernels, call(): pl.pallas_call(moved, out_shape=tuple((jax.ShapeDtypeStruct(*t) for t in...  44.6 us
    all_to_all x3, blocking collectives, swap(): return lax.all_to_all(value, axis, 0, 0, tiled=True)  37 us
    all_to_all x8, waiting for transfers between devices, swap(): return lax.all_to_all(value, axis, 0, 0, tiled=True)  18.7 us
    ppermute x24, waiting for transfers between devices, across(): return (lax.ppermute(high, axis, up), lax.ppermute(low, axis, down))  18.5 us
    ppermute x1, starting transfers between devices, body(): other = lax.ppermute(mine, 'gx', [(i, i ^ 1) for i in range(NX)])  6.32 us
  transfers between devices with their start and end apart: 33, of which 13 were waited for; matrix products, arithmetic and copies ran while one was open for 0% of the time, Pallas kernels for 6%

profile of v3, /device:TPU:1, one launch (start us, length us, event | category | flops | bytes accessed | tf_op | source)
XLA Modules:
  0.0 270.4 jit_solution(16593193410440449355)
XLA Ops:
  0.6 4.3 %shard_map.77 = (f32[1024,128]{1,0:T(8,128)}, bf16[16,288,128]{2,1,0:T(8,128)(2,1)}) custom-call(s32[1]{0:T(128)} %bitcast.refs_0_, s32[1]{0:T(128)} %bitcast.1.refs_1_, s32[8]{0:T(128)} %bitcast.23, bf16[1024,128]{1,0:T(8,128)(2,1)} %bitcast.15, bf16[8,1024]{1,0:T(8,128)(2,1)} %bitcast.20, bf16[1024,1024]{1,0:T(8,128)(2,1)} %bitcast.12, ...), custom_call_target="tpu_custom_call" | custom-call | flops 268435456 | bytes 2506792 | tf_op jit(solution)/shard_map/pallas_call | solution.py:128
  4.9 7.6 %all-to-all-start = ((bf16[16,288,128]{2,1,0:T(8,128)(2,1)}), bf16[16,288,128]{2,1,0:T(8,128)(2,1)S(1)}, u32[]{:S(2)}, u32[]{:S(2)}) async-start(bf16[16,288,128]{2,1,0:T(8,128)(2,1)} %get-tuple-element.90), calls=%async_computation | async-start | bytes 2359296 | tf_op jit(solution)/shard_map/all_to_all | solution.py:571
  12.5 1.9 shard_map.78
  14.4 2.5 collective-permute-start
  16.9 0.5 collective-permute-start.1
  17.5 3.4 %collective-permute-start.2 = (f32[272,128]{1,0:T(8,128)}, f32[272,128]{1,0:T(8,128)S(1)}, u32[]{:S(2)}, u32[]{:S(2)}) collective-permute-start(f32[272,128]{1,0:T(8,128)} %get-tuple-element.94), channel_id=1, source_target_pairs={{0,1},{1,2},{2,3},{3,4},{4,5},{5,6},{6,7},{7,8},{8,9},{9,10},{10,1... | collective-permute-start | bytes 417800 | tf_op jit(solution)/shard_map/ppermute | solution.py:558
  20.9 5.3 %collective-permute-start.3 = (f32[272,128]{1,0:T(8,128)}, f32[272,128]{1,0:T(8,128)S(1)}, u32[]{:S(2)}, u32[]{:S(2)}) collective-permute-start(f32[272,128]{1,0:T(8,128)} %get-tuple-element.95), channel_id=1, source_target_pairs={{1,0},{2,1},{3,2},{4,3},{5,4},{6,5},{7,6},{8,7},{9,8},{10,9},{11,1... | collective-permute-start | bytes 417800 | tf_op jit(solution)/shard_map/ppermute | solution.py:558
  26.3 5.4 %collective-permute-done.2.refs_5_.refs_7_.refs_8_ = f32[272,128]{1,0:T(8,128)S(1)} collective-permute-done((f32[272,128]{1,0:T(8,128)}, f32[272,128]{1,0:T(8,128)S(1)}, u32[]{:S(2)}, u32[]{:S(2)}) %collective-permute-start.2) | collective-permute-done | bytes 139296 | tf_op jit(solution)/shard_map/ppermute | solution.py:558
  31.7 6.3 %collective-permute-start.4 = (bf16[16,288,128]{2,1,0:T(8,128)(2,1)S(1)}, bf16[16,288,128]{2,1,0:T(8,128)(2,1)S(1)}, u32[]{:S(2)}, u32[]{:S(2)}) collective-permute-start(bf16[16,288,128]{2,1,0:T(8,128)(2,1)S(1)} %all-to-all-done.refs_0_.refs_2_), channel_id=1, source_target_pairs={{0,16},{16,0},{32,48},{48,32},{64,80},{80,64},{96,112},{112,96},{1... | collective-permute-start | bytes 3538952 | tf_op jit(solution)/shard_map/ppermute | solution.py:608
  38.1 0.9 shard_map.79
  38.9 14.1 %all-to-all-start.1 = ((f32[32,1,1152]{2,1,0:T(1,128)}), f32[32,1,1152]{2,1,0:T(1,128)S(1)}, u32[]{:S(2)}, u32[]{:S(2)}) async-start(f32[32,1,1152]{2,1,0:T(1,128)} %shard_map.79), calls=%async_computation.1 | async-start | bytes 294912 | tf_op jit(solution)/shard_map/all_to_all | solution.py:571
  53.1 2.0 shard_map.80
  55.1 14.4 %all-to-all-done.1.refs_1_ = f32[32,1,1152]{2,1,0:T(1,128)S(1)} async-done(((f32[32,1,1152]{2,1,0:T(1,128)}), f32[32,1,1152]{2,1,0:T(1,128)S(1)}, u32[]{:S(2)}, u32[]{:S(2)}) %all-to-all-start.1) | async-done | bytes 147488 | tf_op jit(solution)/shard_map/all_to_all | solution.py:571
  69.5 0.6 copy-done.8
  70.2 1.0 copy-done.7
  71.2 4.6 %shard_map.81 = (f32[8,1024]{1,0:T(8,128)}, bf16[1024,128]{1,0:T(8,128)(2,1)}, f32[16,8,128]{2,1,0:T(8,128)}) custom-call(s32[1]{0:T(128)} %bitcast.refs_0_, f32[32,1,1152]{2,1,0:T(1,128)} %copy-done.8, bf16[16,288,128]{2,1,0:T(8,128)(2,1)} %copy-done, bf16[16,288,128]{2,1,0:T(8,128)(2,1)} %copy-done.7), custom_call_target="tpu_custom_call" | custom-call | flops 536870912 | bytes 2506756 | tf_op jit(solution)/shard_map/pallas_call | solution.py:128
  75.8 10.6 %all_to_all.55.refs_2_ = f32[16,8,128]{2,1,0:T(8,128)} all-to-all(f32[16,8,128]{2,1,0:T(8,128)} %get-tuple-element.103), channel_id=1, replica_groups=mesh['gx'=32,'gy'=16] {'gy'}, dimensions={0} | all-to-all | bytes 131072 | tf_op jit(solution)/shard_map/all_to_all | solution.py:571
  86.4 4.2 %shard_map.82 = (f32[1024,128]{1,0:T(8,128)}, bf16[1024,128]{1,0:T(8,128)(2,1)}, bf16[256,128]{1,0:T(8,128)(2,1)}, bf16[256,128]{1,0:T(8,128)(2,1)}, bf16[256,12...) custom-call(s32[1]{0:T(128)} %bitcast.refs_0_, s32[1]{0:T(128)} %bitcast.1.refs_1_, ...), custom_call_target="tpu_custom_call" | custom-call | flops 268435456 | bytes 3768328 | tf_op jit(solution)/shard_map/pallas_call | solution.py:128
  90.6 3.5 %all-to-all-start.3 = ((f32[16,32,128]{2,1,0:T(8,128)}), f32[16,32,128]{2,1,0:T(8,128)S(1)}, u32[]{:S(2)}, u32[]{:S(2)}) async-start(f32[16,32,128]{2,1,0:T(8,128)} %get-tuple-element.105), calls=%async_computation.3 | async-start | bytes 524288 | tf_op jit(solution)/shard_map/all_to_all | solution.py:571
  94.1 2.7 %collective-permute-start.5 = (bf16[256,128]{1,0:T(8,128)(2,1)}, bf16[256,128]{1,0:T(8,128)(2,1)S(1)}, u32[]{:S(2)}, u32[]{:S(2)}) collective-permute-start(bf16[256,128]{1,0:T(8,128)(2,1)} %get-tuple-element.106), channel_id=1, source_target_pairs={{0,16},{16,32},{32,48},{48,64},{64,80},{80,96},{96,112},{112,128},... | collective-permute-start | bytes 196616 | tf_op jit(solution)/shard_map/ppermute | solution.py:558
  97.0 3.4 %collective-permute-start.7 = (bf16[256,128]{1,0:T(8,128)(2,1)}, bf16[256,128]{1,0:T(8,128)(2,1)S(1)}, u32[]{:S(2)}, u32[]{:S(2)}) collective-permute-start(bf16[256,128]{1,0:T(8,128)(2,1)} %get-tuple-element.108), channel_id=1, source_target_pairs={{0,1},{1,2},{2,3},{3,4},{4,5},{5,6},{6,7},{7,8},{8,9},{9,10},{10,1... | collective-permute-start | bytes 196616 | tf_op jit(solution)/shard_map/ppermute | solution.py:558
  100.4 5.3 %collective-permute-start.8 = (bf16[256,128]{1,0:T(8,128)(2,1)}, bf16[256,128]{1,0:T(8,128)(2,1)S(1)}, u32[]{:S(2)}, u32[]{:S(2)}) collective-permute-start(bf16[256,128]{1,0:T(8,128)(2,1)} %get-tuple-element.109), channel_id=1, source_target_pairs={{1,0},{2,1},{3,2},{4,3},{5,4},{6,5},{7,6},{8,7},{9,8},{10,9},{11,1... | collective-permute-start | bytes 196616 | tf_op jit(solution)/shard_map/ppermute | solution.py:558
  105.8 1.6 collective-permute-done.8.refs_6_
  107.4 0.8 shard_map.83
  108.2 7.4 %all-to-all-start.4 = ((f32[32,1,1152]{2,1,0:T(1,128)}), f32[32,1,1152]{2,1,0:T(1,128)S(1)}, u32[]{:S(2)}, u32[]{:S(2)}) async-start(f32[32,1,1152]{2,1,0:T(1,128)} %shard_map.83), calls=%async_computation.4 | async-start | bytes 294912 | tf_op jit(solution)/shard_map/all_to_all | solution.py:571
  115.7 3.5 %shard_map.84 = (f32[1024,128]{1,0:T(8,128)}, f32[1024,128]{1,0:T(8,128)}, f32[256,128]{1,0:T(8,128)}, f32[256,128]{1,0:T(8,128)}, f32[256,128]{1,0:T(8,128)}, /*index=5*/f32[256,128]{1,0:T(8,128)}) custom-call(s32[1]{0:T(128)} %bitcast.refs_0_, s32[1]{0:T(128)} %bitcast.1.refs_1_, bf16[1024,128]{1,0:T(8,128)(2,1)} %get-tuple-element.111.refs_2_.refs_17_.refs_23_, ...), custom_call_target="tpu_custom_call" | custom-call | flops 268435456 | bytes 2621448 | tf_op jit(solution)/shard_map/pallas_call | solution.py:128
  119.3 1.7 collective-permute-start.9
  120.9 1.9 collective-permute-start.11
  122.8 7.2 %collective-permute-start.12 = (f32[256,128]{1,0:T(8,128)}, f32[256,128]{1,0:T(8,128)S(1)}, u32[]{:S(2)}, u32[]{:S(2)}) collective-permute-start(f32[256,128]{1,0:T(8,128)} %get-tuple-element.119), channel_id=1, source_target_pairs={{1,0},{2,1},{3,2},{4,3},{5,4},{6,5},{7,6},{8,7},{9,8},{10,9},{11,1... | collective-permute-start | bytes 393224 | tf_op jit(solution)/shard_map/ppermute | solution.py:558
  130.1 0.6 collective-permute-done.11.refs_12_.refs_13_
  130.7 1.6 collective-permute-done.12.refs_13_.refs_14_
  132.3 0.3 all-to-all-done.4.refs_0_
  132.6 0.8 shard_map.85
  133.4 13.2 %all_to_all.56.refs_2_ = f32[16,8,128]{2,1,0:T(8,128)} all-to-all(f32[16,8,128]{2,1,0:T(8,128)S(1)} %get-tuple-element.123), channel_id=1, replica_groups=mesh['gx'=32,'gy'=16] {'gy'}, dimensions={0} | all-to-all | bytes 131072 | tf_op jit(solution)/shard_map/all_to_all | solution.py:571
  146.6 4.7 %shard_map.86 = (f32[1024,128]{1,0:T(8,128)}, f32[1024,128]{1,0:T(8,128)}, f32[256,128]{1,0:T(8,128)}, f32[256,128]{1,0:T(8,128)}, f32[256,128]{1,0:T(8,128)}, /...) custom-call(s32[1]{0:T(128)} %bitcast.refs_0_, s32[1]{0:T(128)} %bitcast.1.refs_1_, ...), custom_call_target="tpu_custom_call" | custom-call | flops 268435456 | bytes 5603336 | tf_op jit(solution)/shard_map/pallas_call | solution.py:128
  151.3 3.5 %all-to-all-start.6 = ((f32[16,32,128]{2,1,0:T(8,128)}), f32[16,32,128]{2,1,0:T(8,128)S(1)}, u32[]{:S(2)}, u32[]{:S(2)}) async-start(f32[16,32,128]{2,1,0:T(8,128)} %get-tuple-element.130), calls=%async_computation.6 | async-start | bytes 524288 | tf_op jit(solution)/shard_map/all_to_all | solution.py:571
  154.9 4.0 %collective-permute-start.13 = (f32[256,128]{1,0:T(8,128)}, f32[256,128]{1,0:T(8,128)S(1)}, u32[]{:S(2)}, u32[]{:S(2)}) collective-permute-start(f32[256,128]{1,0:T(8,128)} %get-tuple-element.131), channel_id=1, source_target_pairs={{0,16},{16,32},{32,48},{48,64},{64,80},{80,96},{96,112},{112,128},... | collective-permute-start | bytes 393224 | tf_op jit(solution)/shard_map/ppermute | solution.py:558
  158.9 3.4 %collective-permute-start.15 = (f32[256,128]{1,0:T(8,128)}, f32[256,128]{1,0:T(8,128)S(1)}, u32[]{:S(2)}, u32[]{:S(2)}) collective-permute-start(f32[256,128]{1,0:T(8,128)} %get-tuple-element.133), channel_id=1, source_target_pairs={{0,1},{1,2},{2,3},{3,4},{4,5},{5,6},{6,7},{7,8},{8,9},{9,10},{10,1... | collective-permute-start | bytes 393224 | tf_op jit(solution)/shard_map/ppermute | solution.py:558
  162.3 5.3 %collective-permute-start.16 = (f32[256,128]{1,0:T(8,128)}, f32[256,128]{1,0:T(8,128)S(1)}, u32[]{:S(2)}, u32[]{:S(2)}) collective-permute-start(f32[256,128]{1,0:T(8,128)} %get-tuple-element.134), channel_id=1, source_target_pairs={{1,0},{2,1},{3,2},{4,3},{5,4},{6,5},{7,6},{8,7},{9,8},{10,9},{11,1... | collective-permute-start | bytes 393224 | tf_op jit(solution)/shard_map/ppermute | solution.py:558
  167.7 0.6 collective-permute-done.15.refs_5_
  168.3 1.6 collective-permute-done.16.refs_6_
  169.9 0.9 shard_map.87
  170.8 15.5 %all-to-all-start.7 = ((f32[32,1,1152]{2,1,0:T(1,128)}), f32[32,1,1152]{2,1,0:T(1,128)S(1)}, u32[]{:S(2)}, u32[]{:S(2)}) async-start(f32[32,1,1152]{2,1,0:T(1,128)} %shard_map.87), calls=%async_computation.7 | async-start | bytes 294912 | tf_op jit(solution)/shard_map/all_to_all | solution.py:571
  186.3 3.6 %shard_map.88 = (f32[1024,128]{1,0:T(8,128)}, f32[1024,128]{1,0:T(8,128)}, f32[256,128]{1,0:T(8,128)}, f32[256,128]{1,0:T(8,128)}, f32[256,128]{1,0:T(8,128)}, /*index=5*/f32[256,128]{1,0:T(8,128)}) custom-call(s32[1]{0:T(128)} %bitcast.refs_0_, s32[1]{0:T(128)} %bitcast.1.refs_1_, f32[1024,128]{1,0:T(8,128)} %get-tuple-element.136.refs_2_.refs_24_, ...), custom_call_target="tpu_custom_call" | custom-call | flops 268435456 | bytes 3145736 | tf_op jit(solution)/shard_map/pallas_call | solution.py:128
  189.9 1.6 collective-permute-start.17
  191.6 1.9 collective-permute-start.19
  193.5 7.3 %collective-permute-start.20 = (f32[256,128]{1,0:T(8,128)}, f32[256,128]{1,0:T(8,128)S(1)}, u32[]{:S(2)}, u32[]{:S(2)}) collective-permute-start(f32[256,128]{1,0:T(8,128)} %get-tuple-element.144), channel_id=1, source_target_pairs={{1,0},{2,1},{3,2},{4,3},{5,4},{6,5},{7,6},{8,7},{9,8},{10,9},{11,1... | collective-permute-start | bytes 393224 | tf_op jit(solution)/shard_map/ppermute | solution.py:558
  200.8 0.9 collective-permute-done.19.refs_18_
  201.7 1.3 collective-permute-done.20.refs_19_
  203.0 0.9 shard_map.89
  203.9 13.2 %all_to_all.57.refs_2_ = f32[16,8,128]{2,1,0:T(8,128)} all-to-all(f32[16,8,128]{2,1,0:T(8,128)S(1)} %shard_map.89), channel_id=1, replica_groups=mesh['gx'=32,'gy'=16] {'gy'}, dimensions={0} | all-to-all | bytes 131072 | tf_op jit(solution)/shard_map/all_to_all | solution.py:571
  217.1 4.7 %shard_map.90 = (f32[1024,128]{1,0:T(8,128)}, f32[1024,128]{1,0:T(8,128)}, f32[256,128]{1,0:T(8,128)}, f32[256,128]{1,0:T(8,128)}, f32[256,128]{1,0:T(8,128)}, /...) custom-call(s32[1]{0:T(128)} %bitcast.refs_0_, s32[1]{0:T(128)} %bitcast.1.refs_1_, ...), custom_call_target="tpu_custom_call" | custom-call | flops 268435456 | bytes 7573512 | tf_op jit(solution)/shard_map/pallas_call | solution.py:128
  221.9 3.7 %all-to-all-start.9 = ((f32[16,32,128]{2,1,0:T(8,128)}), f32[16,32,128]{2,1,0:T(8,128)S(1)}, u32[]{:S(2)}, u32[]{:S(2)}) async-start(f32[16,32,128]{2,1,0:T(8,128)} %get-tuple-element.156), calls=%async_computation.9 | async-start | bytes 524288 | tf_op jit(solution)/shard_map/all_to_all | solution.py:571
  225.6 4.3 %collective-permute-start.21 = (f32[256,128]{1,0:T(8,128)}, f32[256,128]{1,0:T(8,128)S(1)}, u32[]{:S(2)}, u32[]{:S(2)}) collective-permute-start(f32[256,128]{1,0:T(8,128)} %get-tuple-element.157), channel_id=1, source_target_pairs={{0,16},{16,32},{32,48},{48,64},{64,80},{80,96},{96,112},{112,128},... | collective-permute-start | bytes 393224 | tf_op jit(solution)/shard_map/ppermute | solution.py:558
  229.9 2.3 collective-permute-done.21.refs_5_
  232.2 2.6 collective-permute-done.22.refs_6_
  234.8 0.7 shard_map.91
  235.5 15.2 %all-to-all-start.10 = ((f32[32,8,128]{2,1,0:T(8,128)}), f32[32,8,128]{2,1,0:T(8,128)S(1)}, u32[]{:S(2)}, u32[]{:S(2)}) async-start(f32[32,8,128]{2,1,0:T(8,128)} %shard_map.91), calls=%async_computation.10 | async-start | bytes 262144 | tf_op jit(solution)/shard_map/all_to_all | solution.py:571
  250.7 2.2 collective-permute-start.23
  253.0 6.4 %collective-permute-start.24 = (f32[256,128]{1,0:T(8,128)S(1)}, f32[256,128]{1,0:T(8,128)S(1)}, u32[]{:S(2)}, u32[]{:S(2)}) collective-permute-start(f32[256,128]{1,0:T(8,128)S(1)} %copy-done.30), channel_id=1, source_target_pairs={{1,0},{2,1},{3,2},{4,3},{5,4},{6,5},{7,6},{8,7},{9,8},{10,9},{11,1... | collective-permute-start | bytes 393224 | tf_op jit(solution)/shard_map/ppermute | solution.py:558
  259.4 3.1 %shard_map.92 = (f32[1024,128]{1,0:T(8,128)}, f32[1024,128]{1,0:T(8,128)}, f32[1024,128]{1,0:T(8,128)}, f32[1024,128]{1,0:T(8,128)}) custom-call(f32[8,128]{1,0:T(8,128)} %get-tuple-element.149.refs_3_.refs_0_, f32[8,128]{1,0:T(8,128)} %get-tuple-element.163.refs_1_.refs_3_, f32[1024,128]{1,0:T(8,128)} %get-tuple-element.170.refs_2_, ...), custom_call_target="tpu_custom_call" | custom-call | flops 268435456 | bytes 2367488 | tf_op jit(solution)/shard_map/pallas_call | solution.py:128
  262.6 4.0 %all-to-all-done.10.refs_2_ = f32[32,8,128]{2,1,0:T(8,128)S(1)} async-done(((f32[32,8,128]{2,1,0:T(8,128)}), f32[32,8,128]{2,1,0:T(8,128)S(1)}, u32[]{:S(2)}, u32[]{:S(2)}) %all-to-all-start.10) | async-done | bytes 131104 | tf_op jit(solution)/shard_map/all_to_all | solution.py:571
  266.6 0.6 copy-done.13
  267.2 3.0 %shard_map.93 = (bf16[1024,128]{1,0:T(8,128)(2,1)}, bf16[1024,128]{1,0:T(8,128)(2,1)}) custom-call(s32[1]{0:T(128)} %bitcast.refs_0_, s32[1]{0:T(128)} %bitcast.1.refs_1_, f32[32,8,128]{2,1,0:T(8,128)} %copy-done.13, f32[8,128]{1,0:T(8,128)} %get-tuple-element.163.refs_1_.refs_3_, f32[1024,128]{1,0:T(8,128)} %get-tuple-element.164.refs_4_, ...), custom_call_target="tpu_custom_call" | custom-call | bytes 3805192 | tf_op jit(solution)/shard_map/pallas_call | solution.py:128
  (86 shorter events, 0.3 us)
Async XLA Ops:
  4.9 26.8 %all-to-all-start = ((bf16[16,288,128]{2,1,0:T(8,128)(2,1)}), bf16[16,288,128]{2,1,0:T(8,128)(2,1)S(1)}, u32[]{:S(2)}, u32[]{:S(2)}) async-start(bf16[16,288,128]{2,1,0:T(8,128)(2,1)} %get-tuple-element.90), calls=%async_computation | async-start | bytes 2359296 | tf_op jit(solution)/shard_map/all_to_all | solution.py:571
  14.4 11.8 %collective-permute-start = (f32[272,128]{1,0:T(8,128)}, f32[272,128]{1,0:T(8,128)S(1)}, u32[]{:S(2)}, u32[]{:S(2)}) collective-permute-start(f32[272,128]{1,0:T(8,128)} %get-tuple-element.92), channel_id=1, source_target_pairs={{0,16},{16,32},{32,48},{48,64},{64,80},{80,96},{96,112},{112,128},... | collective-permute-start | bytes 417800 | tf_op jit(solution)/shard_map/ppermute | solution.py:558
  16.9 9.3 %collective-permute-start.1 = (f32[272,128]{1,0:T(8,128)}, f32[272,128]{1,0:T(8,128)S(1)}, u32[]{:S(2)}, u32[]{:S(2)}) collective-permute-start(f32[272,128]{1,0:T(8,128)} %get-tuple-element.93), channel_id=1, source_target_pairs={{16,0},{32,16},{48,32},{64,48},{80,64},{96,80},{112,96},{128,112},... | collective-permute-start | bytes 417800 | tf_op jit(solution)/shard_map/ppermute | solution.py:558
  17.5 14.2 %collective-permute-start.2 = (f32[272,128]{1,0:T(8,128)}, f32[272,128]{1,0:T(8,128)S(1)}, u32[]{:S(2)}, u32[]{:S(2)}) collective-permute-start(f32[272,128]{1,0:T(8,128)} %get-tuple-element.94), channel_id=1, source_target_pairs={{0,1},{1,2},{2,3},{3,4},{4,5},{5,6},{6,7},{7,8},{8,9},{9,10},{10,1... | collective-permute-start | bytes 417800 | tf_op jit(solution)/shard_map/ppermute | solution.py:558
  20.9 10.8 %collective-permute-start.3 = (f32[272,128]{1,0:T(8,128)}, f32[272,128]{1,0:T(8,128)S(1)}, u32[]{:S(2)}, u32[]{:S(2)}) collective-permute-start(f32[272,128]{1,0:T(8,128)} %get-tuple-element.95), channel_id=1, source_target_pairs={{1,0},{2,1},{3,2},{4,3},{5,4},{6,5},{7,6},{8,7},{9,8},{10,9},{11,1... | collective-permute-start | bytes 417800 | tf_op jit(solution)/shard_map/ppermute | solution.py:558
  26.3 26.8 %copy-start.3 = (f32[272,128]{1,0:T(8,128)}, f32[272,128]{1,0:T(8,128)S(1)}, u32[]{:S(2)}) copy-start(f32[272,128]{1,0:T(8,128)S(1)} %collective-permute-done.refs_3_.refs_5_.refs_6_) | copy-start | bytes 417796
  26.3 26.8 %copy-start.4 = (f32[272,128]{1,0:T(8,128)}, f32[272,128]{1,0:T(8,128)S(1)}, u32[]{:S(2)}) copy-start(f32[272,128]{1,0:T(8,128)S(1)} %collective-permute-done.1.refs_4_.refs_6_.refs_7_) | copy-start | bytes 417796
  31.7 21.3 %copy-start.5 = (f32[272,128]{1,0:T(8,128)}, f32[272,128]{1,0:T(8,128)S(1)}, u32[]{:S(2)}) copy-start(f32[272,128]{1,0:T(8,128)S(1)} %collective-permute-done.2.refs_5_.refs_7_.refs_8_) | copy-start | bytes 417796
  31.7 21.3 %copy-start.6 = (f32[272,128]{1,0:T(8,128)}, f32[272,128]{1,0:T(8,128)S(1)}, u32[]{:S(2)}) copy-start(f32[272,128]{1,0:T(8,128)S(1)} %collective-permute-done.3.refs_6_.refs_8_.refs_9_) | copy-start | bytes 417796
  31.7 37.8 %copy-start = (bf16[16,288,128]{2,1,0:T(8,128)(2,1)}, bf16[16,288,128]{2,1,0:T(8,128)(2,1)S(1)}, u32[]{:S(2)}) copy-start(bf16[16,288,128]{2,1,0:T(8,128)(2,1)S(1)} %all-to-all-done.refs_0_.refs_2_) | copy-start | bytes 3538948
  31.7 37.8 %collective-permute-start.4 = (bf16[16,288,128]{2,1,0:T(8,128)(2,1)S(1)}, bf16[16,288,128]{2,1,0:T(8,128)(2,1)S(1)}, u32[]{:S(2)}, u32[]{:S(2)}) collective-permute-start(bf16[16,288,128]{2,1,0:T(8,128)(2,1)S(1)} %all-to-all-done.refs_0_.refs_2_), channel_id=1, source_target_pairs={{0,16},{16,0},{32,48},{48,32},{64,80},{80,64},{96,112},{112,96},{1... | collective-permute-start | bytes 3538952 | tf_op jit(solution)/shard_map/ppermute | solution.py:608
  38.9 30.6 %all-to-all-start.1 = ((f32[32,1,1152]{2,1,0:T(1,128)}), f32[32,1,1152]{2,1,0:T(1,128)S(1)}, u32[]{:S(2)}, u32[]{:S(2)}) async-start(f32[32,1,1152]{2,1,0:T(1,128)} %shard_map.79), calls=%async_computation.1 | async-start | bytes 294912 | tf_op jit(solution)/shard_map/all_to_all | solution.py:571
  70.2 1.0 copy-start.7
  90.6 16.8 %all-to-all-start.3 = ((f32[16,32,128]{2,1,0:T(8,128)}), f32[16,32,128]{2,1,0:T(8,128)S(1)}, u32[]{:S(2)}, u32[]{:S(2)}) async-start(f32[16,32,128]{2,1,0:T(8,128)} %get-tuple-element.105), calls=%async_computation.3 | async-start | bytes 524288 | tf_op jit(solution)/shard_map/all_to_all | solution.py:571
  94.1 11.6 %collective-permute-start.5 = (bf16[256,128]{1,0:T(8,128)(2,1)}, bf16[256,128]{1,0:T(8,128)(2,1)S(1)}, u32[]{:S(2)}, u32[]{:S(2)}) collective-permute-start(bf16[256,128]{1,0:T(8,128)(2,1)} %get-tuple-element.106), channel_id=1, source_target_pairs={{0,16},{16,32},{32,48},{48,64},{64,80},{80,96},{96,112},{112,128},... | collective-permute-start | bytes 196616 | tf_op jit(solution)/shard_map/ppermute | solution.py:558
  96.9 8.9 %collective-permute-start.6 = (bf16[256,128]{1,0:T(8,128)(2,1)}, bf16[256,128]{1,0:T(8,128)(2,1)S(1)}, u32[]{:S(2)}, u32[]{:S(2)}) collective-permute-start(bf16[256,128]{1,0:T(8,128)(2,1)} %get-tuple-element.107), channel_id=1, source_target_pairs={{16,0},{32,16},{48,32},{64,48},{80,64},{96,80},{112,96},{128,112},... | collective-permute-start | bytes 196616 | tf_op jit(solution)/shard_map/ppermute | solution.py:558
  97.0 8.8 %collective-permute-start.7 = (bf16[256,128]{1,0:T(8,128)(2,1)}, bf16[256,128]{1,0:T(8,128)(2,1)S(1)}, u32[]{:S(2)}, u32[]{:S(2)}) collective-permute-start(bf16[256,128]{1,0:T(8,128)(2,1)} %get-tuple-element.108), channel_id=1, source_target_pairs={{0,1},{1,2},{2,3},{3,4},{4,5},{5,6},{6,7},{7,8},{8,9},{9,10},{10,1... | collective-permute-start | bytes 196616 | tf_op jit(solution)/shard_map/ppermute | solution.py:558
  100.4 7.0 %collective-permute-start.8 = (bf16[256,128]{1,0:T(8,128)(2,1)}, bf16[256,128]{1,0:T(8,128)(2,1)S(1)}, u32[]{:S(2)}, u32[]{:S(2)}) collective-permute-start(bf16[256,128]{1,0:T(8,128)(2,1)} %get-tuple-element.109), channel_id=1, source_target_pairs={{1,0},{2,1},{3,2},{4,3},{5,4},{6,5},{7,6},{8,7},{9,8},{10,9},{11,1... | collective-permute-start | bytes 196616 | tf_op jit(solution)/shard_map/ppermute | solution.py:558
  105.8 9.9 %copy-start.26 = (bf16[256,128]{1,0:T(8,128)(2,1)}, bf16[256,128]{1,0:T(8,128)(2,1)S(1)}, u32[]{:S(2)}) copy-start(bf16[256,128]{1,0:T(8,128)(2,1)S(1)} %collective-permute-done.5.refs_3_) | copy-start | bytes 196612
  105.8 9.9 %copy-start.27 = (bf16[256,128]{1,0:T(8,128)(2,1)}, bf16[256,128]{1,0:T(8,128)(2,1)S(1)}, u32[]{:S(2)}) copy-start(bf16[256,128]{1,0:T(8,128)(2,1)S(1)} %collective-permute-done.6.refs_4_) | copy-start | bytes 196612
  105.8 9.9 %copy-start.28 = (bf16[256,128]{1,0:T(8,128)(2,1)}, bf16[256,128]{1,0:T(8,128)(2,1)S(1)}, u32[]{:S(2)}) copy-start(bf16[256,128]{1,0:T(8,128)(2,1)S(1)} %collective-permute-done.7.refs_5_) | copy-start | bytes 196612
  107.4 8.3 %copy-start.29 = (bf16[256,128]{1,0:T(8,128)(2,1)}, bf16[256,128]{1,0:T(8,128)(2,1)S(1)}, u32[]{:S(2)}) copy-start(bf16[256,128]{1,0:T(8,128)(2,1)S(1)} %collective-permute-done.8.refs_6_) | copy-start | bytes 196612
  108.2 24.4 %all-to-all-start.4 = ((f32[32,1,1152]{2,1,0:T(1,128)}), f32[32,1,1152]{2,1,0:T(1,128)S(1)}, u32[]{:S(2)}, u32[]{:S(2)}) async-start(f32[32,1,1152]{2,1,0:T(1,128)} %shard_map.83), calls=%async_computation.4 | async-start | bytes 294912 | tf_op jit(solution)/shard_map/all_to_all | solution.py:571
  115.7 16.9 %copy-start.1 = (bf16[1024,128]{1,0:T(8,128)(2,1)S(1)}, bf16[1024,128]{1,0:T(8,128)(2,1)}, u32[]{:S(2)}) copy-start(bf16[1024,128]{1,0:T(8,128)(2,1)} %get-tuple-element.122.refs_2_) | copy-start | bytes 786436
  115.7 16.9 %copy-start.2 = (f32[8,1024]{1,0:T(8,128)S(1)}, f32[8,1024]{1,0:T(8,128)}, u32[]{:S(2)}) copy-start(f32[8,1024]{1,0:T(8,128)} %get-tuple-element.121.refs_1_) | copy-start | bytes 98308
  119.3 10.8 %collective-permute-start.9 = (f32[256,128]{1,0:T(8,128)}, f32[256,128]{1,0:T(8,128)S(1)}, u32[]{:S(2)}, u32[]{:S(2)}) collective-permute-start(f32[256,128]{1,0:T(8,128)} %get-tuple-element.116), channel_id=1, source_target_pairs={{0,16},{16,32},{32,48},{48,64},{64,80},{80,96},{96,112},{112,128},... | collective-permute-start | bytes 393224 | tf_op jit(solution)/shard_map/ppermute | solution.py:558
  120.9 9.2 %collective-permute-start.10 = (f32[256,128]{1,0:T(8,128)}, f32[256,128]{1,0:T(8,128)S(1)}, u32[]{:S(2)}, u32[]{:S(2)}) collective-permute-start(f32[256,128]{1,0:T(8,128)} %get-tuple-element.117), channel_id=1, source_target_pairs={{16,0},{32,16},{48,32},{64,48},{80,64},{96,80},{112,96},{128,112},... | collective-permute-start | bytes 393224 | tf_op jit(solution)/shard_map/ppermute | solution.py:558
  120.9 9.7 %collective-permute-start.11 = (f32[256,128]{1,0:T(8,128)}, f32[256,128]{1,0:T(8,128)S(1)}, u32[]{:S(2)}, u32[]{:S(2)}) collective-permute-start(f32[256,128]{1,0:T(8,128)} %get-tuple-element.118), channel_id=1, source_target_pairs={{0,1},{1,2},{2,3},{3,4},{4,5},{5,6},{6,7},{7,8},{8,9},{9,10},{10,1... | collective-permute-start | bytes 393224 | tf_op jit(solution)/shard_map/ppermute | solution.py:558
  122.8 9.4 %collective-permute-start.12 = (f32[256,128]{1,0:T(8,128)}, f32[256,128]{1,0:T(8,128)S(1)}, u32[]{:S(2)}, u32[]{:S(2)}) collective-permute-start(f32[256,128]{1,0:T(8,128)} %get-tuple-element.119), channel_id=1, source_target_pairs={{1,0},{2,1},{3,2},{4,3},{5,4},{6,5},{7,6},{8,7},{9,8},{10,9},{11,1... | collective-permute-start | bytes 393224 | tf_op jit(solution)/shard_map/ppermute | solution.py:558
  130.1 16.5 %copy-start.9 = (f32[256,128]{1,0:T(8,128)}, f32[256,128]{1,0:T(8,128)S(1)}, u32[]{:S(2)}) copy-start(f32[256,128]{1,0:T(8,128)S(1)} %collective-permute-done.9.refs_10_.refs_11_) | copy-start | bytes 393220
  130.1 16.5 %copy-start.10 = (f32[256,128]{1,0:T(8,128)}, f32[256,128]{1,0:T(8,128)S(1)}, u32[]{:S(2)}) copy-start(f32[256,128]{1,0:T(8,128)S(1)} %collective-permute-done.10.refs_11_.refs_12_) | copy-start | bytes 393220
  130.7 15.9 %copy-start.11 = (f32[256,128]{1,0:T(8,128)}, f32[256,128]{1,0:T(8,128)S(1)}, u32[]{:S(2)}) copy-start(f32[256,128]{1,0:T(8,128)S(1)} %collective-permute-done.11.refs_12_.refs_13_) | copy-start | bytes 393220
  132.3 14.3 %copy-start.12 = (f32[256,128]{1,0:T(8,128)}, f32[256,128]{1,0:T(8,128)S(1)}, u32[]{:S(2)}) copy-start(f32[256,128]{1,0:T(8,128)S(1)} %collective-permute-done.12.refs_13_.refs_14_) | copy-start | bytes 393220
  151.3 18.6 %all-to-all-start.6 = ((f32[16,32,128]{2,1,0:T(8,128)}), f32[16,32,128]{2,1,0:T(8,128)S(1)}, u32[]{:S(2)}, u32[]{:S(2)}) async-start(f32[16,32,128]{2,1,0:T(8,128)} %get-tuple-element.130), calls=%async_computation.6 | async-start | bytes 524288 | tf_op jit(solution)/shard_map/all_to_all | solution.py:571
  154.9 12.8 %collective-permute-start.13 = (f32[256,128]{1,0:T(8,128)}, f32[256,128]{1,0:T(8,128)S(1)}, u32[]{:S(2)}, u32[]{:S(2)}) collective-permute-start(f32[256,128]{1,0:T(8,128)} %get-tuple-element.131), channel_id=1, source_target_pairs={{0,16},{16,32},{32,48},{48,64},{64,80},{80,96},{96,112},{112,128},... | collective-permute-start | bytes 393224 | tf_op jit(solution)/shard_map/ppermute | solution.py:558
  158.9 8.8 %collective-permute-start.14 = (f32[256,128]{1,0:T(8,128)}, f32[256,128]{1,0:T(8,128)S(1)}, u32[]{:S(2)}, u32[]{:S(2)}) collective-permute-start(f32[256,128]{1,0:T(8,128)} %get-tuple-element.132), channel_id=1, source_target_pairs={{16,0},{32,16},{48,32},{64,48},{80,64},{96,80},{112,96},{128,112},... | collective-permute-start | bytes 393224 | tf_op jit(solution)/shard_map/ppermute | solution.py:558
  158.9 9.4 %collective-permute-start.15 = (f32[256,128]{1,0:T(8,128)}, f32[256,128]{1,0:T(8,128)S(1)}, u32[]{:S(2)}, u32[]{:S(2)}) collective-permute-start(f32[256,128]{1,0:T(8,128)} %get-tuple-element.133), channel_id=1, source_target_pairs={{0,1},{1,2},{2,3},{3,4},{4,5},{5,6},{6,7},{7,8},{8,9},{9,10},{10,1... | collective-permute-start | bytes 393224 | tf_op jit(solution)/shard_map/ppermute | solution.py:558
  162.3 7.6 %collective-permute-start.16 = (f32[256,128]{1,0:T(8,128)}, f32[256,128]{1,0:T(8,128)S(1)}, u32[]{:S(2)}, u32[]{:S(2)}) collective-permute-start(f32[256,128]{1,0:T(8,128)} %get-tuple-element.134), channel_id=1, source_target_pairs={{1,0},{2,1},{3,2},{4,3},{5,4},{6,5},{7,6},{8,7},{9,8},{10,9},{11,1... | collective-permute-start | bytes 393224 | tf_op jit(solution)/shard_map/ppermute | solution.py:558
  167.7 18.6 %copy-start.20 = (f32[256,128]{1,0:T(8,128)}, f32[256,128]{1,0:T(8,128)S(1)}, u32[]{:S(2)}) copy-start(f32[256,128]{1,0:T(8,128)S(1)} %collective-permute-done.13.refs_3_) | copy-start | bytes 393220
  167.7 18.6 %copy-start.21 = (f32[256,128]{1,0:T(8,128)}, f32[256,128]{1,0:T(8,128)S(1)}, u32[]{:S(2)}) copy-start(f32[256,128]{1,0:T(8,128)S(1)} %collective-permute-done.14.refs_4_) | copy-start | bytes 393220
  168.3 18.0 %copy-start.22 = (f32[256,128]{1,0:T(8,128)}, f32[256,128]{1,0:T(8,128)S(1)}, u32[]{:S(2)}) copy-start(f32[256,128]{1,0:T(8,128)S(1)} %collective-permute-done.15.refs_5_) | copy-start | bytes 393220
  169.9 16.4 %copy-start.24 = (f32[256,128]{1,0:T(8,128)}, f32[256,128]{1,0:T(8,128)S(1)}, u32[]{:S(2)}) copy-start(f32[256,128]{1,0:T(8,128)S(1)} %collective-permute-done.16.refs_6_) | copy-start | bytes 393220
  170.8 32.3 %all-to-all-start.7 = ((f32[32,1,1152]{2,1,0:T(1,128)}), f32[32,1,1152]{2,1,0:T(1,128)S(1)}, u32[]{:S(2)}, u32[]{:S(2)}) async-start(f32[32,1,1152]{2,1,0:T(1,128)} %shard_map.87), calls=%async_computation.7 | async-start | bytes 294912 | tf_op jit(solution)/shard_map/all_to_all | solution.py:571
  189.9 10.9 %collective-permute-start.17 = (f32[256,128]{1,0:T(8,128)}, f32[256,128]{1,0:T(8,128)S(1)}, u32[]{:S(2)}, u32[]{:S(2)}) collective-permute-start(f32[256,128]{1,0:T(8,128)} %get-tuple-element.141), channel_id=1, source_target_pairs={{0,16},{16,32},{32,48},{48,64},{64,80},{80,96},{96,112},{112,128},... | collective-permute-start | bytes 393224 | tf_op jit(solution)/shard_map/ppermute | solution.py:558
  191.6 9.2 %collective-permute-start.18 = (f32[256,128]{1,0:T(8,128)}, f32[256,128]{1,0:T(8,128)S(1)}, u32[]{:S(2)}, u32[]{:S(2)}) collective-permute-start(f32[256,128]{1,0:T(8,128)} %get-tuple-element.142), channel_id=1, source_target_pairs={{16,0},{32,16},{48,32},{64,48},{80,64},{96,80},{112,96},{128,112},... | collective-permute-start | bytes 393224 | tf_op jit(solution)/shard_map/ppermute | solution.py:558
  191.6 10.1 %collective-permute-start.19 = (f32[256,128]{1,0:T(8,128)}, f32[256,128]{1,0:T(8,128)S(1)}, u32[]{:S(2)}, u32[]{:S(2)}) collective-permute-start(f32[256,128]{1,0:T(8,128)} %get-tuple-element.143), channel_id=1, source_target_pairs={{0,1},{1,2},{2,3},{3,4},{4,5},{5,6},{6,7},{7,8},{8,9},{9,10},{10,1... | collective-permute-start | bytes 393224 | tf_op jit(solution)/shard_map/ppermute | solution.py:558
  193.5 9.5 %collective-permute-start.20 = (f32[256,128]{1,0:T(8,128)}, f32[256,128]{1,0:T(8,128)S(1)}, u32[]{:S(2)}, u32[]{:S(2)}) collective-permute-start(f32[256,128]{1,0:T(8,128)} %get-tuple-element.144), channel_id=1, source_target_pairs={{1,0},{2,1},{3,2},{4,3},{5,4},{6,5},{7,6},{8,7},{9,8},{10,9},{11,1... | collective-permute-start | bytes 393224 | tf_op jit(solution)/shard_map/ppermute | solution.py:558
  200.8 16.3 %copy-start.14 = (f32[256,128]{1,0:T(8,128)}, f32[256,128]{1,0:T(8,128)S(1)}, u32[]{:S(2)}) copy-start(f32[256,128]{1,0:T(8,128)S(1)} %collective-permute-done.17.refs_16_) | copy-start | bytes 393220
  200.8 16.3 %copy-start.15 = (f32[256,128]{1,0:T(8,128)}, f32[256,128]{1,0:T(8,128)S(1)}, u32[]{:S(2)}) copy-start(f32[256,128]{1,0:T(8,128)S(1)} %collective-permute-done.18.refs_17_) | copy-start | bytes 393220
  201.7 15.4 %copy-start.16 = (f32[256,128]{1,0:T(8,128)}, f32[256,128]{1,0:T(8,128)S(1)}, u32[]{:S(2)}) copy-start(f32[256,128]{1,0:T(8,128)S(1)} %collective-permute-done.19.refs_18_) | copy-start | bytes 393220
  203.0 14.1 %copy-start.17 = (f32[256,128]{1,0:T(8,128)}, f32[256,128]{1,0:T(8,128)S(1)}, u32[]{:S(2)}) copy-start(f32[256,128]{1,0:T(8,128)S(1)} %collective-permute-done.20.refs_19_) | copy-start | bytes 393220
  221.9 28.9 %copy-start.31 = (f32[256,128]{1,0:T(8,128)S(1)}, f32[256,128]{1,0:T(8,128)}, u32[]{:S(2)}) copy-start(f32[256,128]{1,0:T(8,128)} %get-tuple-element.167) | copy-start | bytes 393220
  221.9 31.1 %copy-start.30 = (f32[256,128]{1,0:T(8,128)S(1)}, f32[256,128]{1,0:T(8,128)}, u32[]{:S(2)}) copy-start(f32[256,128]{1,0:T(8,128)} %get-tuple-element.168) | copy-start | bytes 393220
  221.9 12.9 %all-to-all-start.9 = ((f32[16,32,128]{2,1,0:T(8,128)}), f32[16,32,128]{2,1,0:T(8,128)S(1)}, u32[]{:S(2)}, u32[]{:S(2)}) async-start(f32[16,32,128]{2,1,0:T(8,128)} %get-tuple-element.156), calls=%async_computation.9 | async-start | bytes 524288 | tf_op jit(solution)/shard_map/all_to_all | solution.py:571
  225.6 6.6 %collective-permute-start.21 = (f32[256,128]{1,0:T(8,128)}, f32[256,128]{1,0:T(8,128)S(1)}, u32[]{:S(2)}, u32[]{:S(2)}) collective-permute-start(f32[256,128]{1,0:T(8,128)} %get-tuple-element.157), channel_id=1, source_target_pairs={{0,16},{16,32},{32,48},{48,64},{64,80},{80,96},{96,112},{112,128},... | collective-permute-start | bytes 393224 | tf_op jit(solution)/shard_map/ppermute | solution.py:558
  229.9 4.9 %collective-permute-start.22 = (f32[256,128]{1,0:T(8,128)}, f32[256,128]{1,0:T(8,128)S(1)}, u32[]{:S(2)}, u32[]{:S(2)}) collective-permute-start(f32[256,128]{1,0:T(8,128)} %get-tuple-element.158), channel_id=1, source_target_pairs={{16,0},{32,16},{48,32},{64,48},{80,64},{96,80},{112,96},{128,112},... | collective-permute-start | bytes 393224 | tf_op jit(solution)/shard_map/ppermute | solution.py:558
  232.1 30.3 %copy-start.18 = (f32[256,128]{1,0:T(8,128)}, f32[256,128]{1,0:T(8,128)S(1)}, u32[]{:S(2)}) copy-start(f32[256,128]{1,0:T(8,128)S(1)} %collective-permute-done.21.refs_5_) | copy-start | bytes 393220
  234.8 27.7 %copy-start.19 = (f32[256,128]{1,0:T(8,128)}, f32[256,128]{1,0:T(8,128)S(1)}, u32[]{:S(2)}) copy-start(f32[256,128]{1,0:T(8,128)S(1)} %collective-permute-done.22.refs_6_) | copy-start | bytes 393220
  235.5 31.1 %all-to-all-start.10 = ((f32[32,8,128]{2,1,0:T(8,128)}), f32[32,8,128]{2,1,0:T(8,128)S(1)}, u32[]{:S(2)}, u32[]{:S(2)}) async-start(f32[32,8,128]{2,1,0:T(8,128)} %shard_map.91), calls=%async_computation.10 | async-start | bytes 262144 | tf_op jit(solution)/shard_map/all_to_all | solution.py:571
  250.7 11.8 %collective-permute-start.23 = (f32[256,128]{1,0:T(8,128)S(1)}, f32[256,128]{1,0:T(8,128)S(1)}, u32[]{:S(2)}, u32[]{:S(2)}) collective-permute-start(f32[256,128]{1,0:T(8,128)S(1)} %copy-done.31), channel_id=1, source_target_pairs={{0,1},{1,2},{2,3},{3,4},{4,5},{5,6},{6,7},{7,8},{8,9},{9,10},{10,1... | collective-permute-start | bytes 393224 | tf_op jit(solution)/shard_map/ppermute | solution.py:558
  253.0 9.6 %collective-permute-start.24 = (f32[256,128]{1,0:T(8,128)S(1)}, f32[256,128]{1,0:T(8,128)S(1)}, u32[]{:S(2)}, u32[]{:S(2)}) collective-permute-start(f32[256,128]{1,0:T(8,128)S(1)} %copy-done.30), channel_id=1, source_target_pairs={{1,0},{2,1},{3,2},{4,3},{5,4},{6,5},{7,6},{8,7},{9,8},{10,9},{11,1... | collective-permute-start | bytes 393224 | tf_op jit(solution)/shard_map/ppermute | solution.py:558
  262.5 4.1 %copy-start.23 = (f32[256,128]{1,0:T(8,128)}, f32[256,128]{1,0:T(8,128)S(1)}, u32[]{:S(2)}) copy-start(f32[256,128]{1,0:T(8,128)S(1)} %collective-permute-done.23.refs_7_) | copy-start | bytes 393220
  262.5 4.0 %copy-start.25 = (f32[256,128]{1,0:T(8,128)}, f32[256,128]{1,0:T(8,128)S(1)}, u32[]{:S(2)}) copy-start(f32[256,128]{1,0:T(8,128)S(1)} %collective-permute-done.24.refs_8_) | copy-start | bytes 393220
  266.6 0.6 copy-start.13
  (1 other events, 0.6 us)

commit v4 on v3

--- a/solution.py
+++ b/solution.py
@@ -193,7 +193,9 @@
     return high, middle, value - high - middle
 
 
-def start_kernel(ax, ay, ids, load, basis, inverse, coarse, l_out, msg_out, table, own):
+def start_kernel(
+    ax, ay, ids, load, basis, inverse, coarse, l_out, f0, f1, f2, f3, msg_out, table, own
+):
     wt = weights(ax, ay)
     piece = coarse.rows(32 * (ax[0] % 2), 32)
     for k in range(8):
@@ -211,15 +213,13 @@
     terms = jnp.concatenate([*terms, jnp.zeros((NY, SL, 128), F32)], axis=1)
     msg_out[:, FACE : FACE + 32] = terms.astype(BF16)
     msg_out.send()
-    for i in range(4):
-        l_out[rows(i)] = wt[i] * dot(inverse[rows(i)], scaled)
-
-
-def first_faces_kernel(l, basis, f0, f1, f2, f3):
     for i, face in enumerate((f0, f1, f2, f3)):
-        face[0:FACE] = l[rows(i)]
+        local = wt[i] * dot(inverse[rows(i)], scaled)
+        l_out[rows(i)] = local
+        face[0:FACE] = local
         face[FACE : FACE + 8] = basis[:, FACE * i : FACE * i + 128].astype(F32)
         face[FACE + 8 : FACE + 16] = basis[:, FACE * i + 128 : FACE * (i + 1)].astype(F32)
+        face.send()
 
 
 def window_kernel(ax, ay, basis, f0, f1, f2, f3, b_out, bt_out, table):
@@ -589,22 +589,18 @@
     zb = pltpu.VMEM((NI, 2 * R), BF16)
     face = ((FACE, R), F32)
 
-    l0, m = call(
+    l0, f0, f1, f2, f3, m = call(
         start_kernel,
         (*here, ids, load, basis, inverse, coarse_inverse),
-        [(tall, F32), ((NY, FACE + 32, 128), BF16)],
+        [(tall, F32)] + [((FACE + 16, R), F32)] * 4 + [((NY, FACE + 32, 128), BF16)],
         [table, pltpu.VMEM((WIN, NI), F32)],
         smem=3,
         flops=block,
     )
-    f0, f1, f2, f3 = call(
-        first_faces_kernel,
-        (l0, basis),
-        [((FACE + 16, R), F32)] * 4,
-        flops=block,
-    )
     faces0 = all_across(f0, f1, f2, f3)
-    mine, *faces0 = together(swap(m, "gy"), *faces0)
+    fx0, fx1, fy0, fy1 = faces0
+    fy0, fy1, fx0, fx1, mine = together(fy0, fy1, fx0, fx1, swap(m, "gy"))
+    faces0 = (fx0, fx1, fy0, fy1)
     other = lax.ppermute(mine, "gx", [(i, i ^ 1) for i in range(NX)])
     (m,) = call(first_column_kernel, (Part(mine, FACE, 32),), [wide], limit=SOME_BYTES)
     m = swap(m, "gx")
@@ -617,11 +613,12 @@
     )
     sums0, picked, m = call(
         first_solve_kernel,
-        (here[0], together(m, window)[0], Part(mine, 0, FACE), Part(other, 0, FACE)),
+        (here[0], Near(together(m, window)[0]), Near(mine), Near(other)),
         [((SL, NCG), F32), ((NCG, 128), BF16), msg],
         [columns, pltpu.VMEM((NCG, 128), BF16), pltpu.VMEM((NCG, NCG), BF16)],
         smem=1,
         flops=2 * block,
+        limit=SOME_BYTES,
     )
     m = swap(m, "gy")
     z0, s0, g0, g1, g2, g3, m = call(
@@ -634,7 +631,9 @@
     )
 
     def stage(s, faces, m):
-        m, *faces = together(swap(m, "gy"), *all_across(*faces))
+        fx0, fx1, fy0, fy1 = all_across(*faces)
+        fy0, fy1, fx0, fx1, m = together(fy0, fy1, fx0, fx1, swap(m, "gy"))
+        faces = (fx0, fx1, fy0, fy1)
         (m,) = call(column_kernel, (Part(m, 0, SL),), [wide], limit=SOME_BYTES)
         q, l, *faces = call(
             local_kernel,
@@ -643,7 +642,9 @@
             smem=2,
             flops=block,
         )
-        m, *faces = together(swap(m, "gx"), *all_across(*faces))
+        fx0, fx1, fy0, fy1 = all_across(*faces)
+        fy0, fy1, fx0, fx1, m = together(fy0, fy1, fx0, fx1, swap(m, "gx"))
+        faces = (fx0, fx1, fy0, fy1)
         return m, q, l, faces
 
     m, q0, l1, faces1 = stage(s0, (g0, g1, g2, g3), m)

time: 272 us -> 263 us (0.967)
  waiting for transfers between devices: 37.3 us -> 48.8 us
  blocking collectives: 37 us -> 29.5 us
  starting transfers between devices: 148 us -> 141 us
  Pallas kernels: 44.6 us -> 40.6 us
    ppermute x24, waiting for transfers between devices: 18.5 us -> 30.3 us  [across(): return (lax.ppermute(high, axis, up), lax.ppermute(low, axis, down))]
    all_to_all x3, blocking collectives: 37 us -> 29.5 us  [swap(): return lax.all_to_all(value, axis, 0, 0, tiled=True)]
    all_to_all x8, starting transfers between devices: 70.6 us -> 65.8 us  [swap(): return lax.all_to_all(value, axis, 0, 0, tiled=True)]
    pallas_call x17 -> x16, Pallas kernels: 44.6 us -> 40.6 us  [call(): pl.pallas_call(moved, out_shape=tuple((jax.ShapeDtypeStruct(*t) for t in...]
  transfers between devices with their start and end apart: 33 -> 33, of which waited for: 13 -> 15; matrix products, arithmetic and copies ran while one was open for 0% -> 0% of each run, Pallas kernels for 6% -> 5%
where the time goes in v4:
time: 263 us; the launch traced here: 262 us
  starting transfers between devices  141 us (54%)
  waiting for transfers between devices  48.8 us (19%)
  Pallas kernels  40.6 us (15%)
  blocking collectives  29.5 us (11%)
    ppermute x24, starting transfers between devices, across(): return (lax.ppermute(high, axis, up), lax.ppermute(low, axis, down))  70.7 us
    all_to_all x8, starting transfers between devices, swap(): return lax.all_to_all(value, axis, 0, 0, tiled=True)  65.8 us
    pallas_call x16, Pallas kernels, call(): pl.pallas_call(moved, out_shape=tuple((jax.ShapeDtypeStruct(*t) for t in...  40.6 us
    ppermute x24, waiting for transfers between devices, across(): return (lax.ppermute(high, axis, up), lax.ppermute(low, axis, down))  30.3 us
    all_to_all x3, blocking collectives, swap(): return lax.all_to_all(value, axis, 0, 0, tiled=True)  29.5 us
    all_to_all x8, waiting for transfers between devices, swap(): return lax.all_to_all(value, axis, 0, 0, tiled=True)  18.5 us
  transfers between devices with their start and end apart: 33, of which 15 were waited for; matrix products, arithmetic and copies ran while one was open for 0% of the time, Pallas kernels for 5%

profile of v4, /device:TPU:1, one launch (start us, length us, event | category | flops | bytes accessed | tf_op | source)
XLA Modules:
  0.0 261.8 jit_solution(17468168301324844005)
XLA Ops:
  0.6 4.4 %shard_map.77 = (f32[1024,128]{1,0:T(8,128)}, f32[272,128]{1,0:T(8,128)}, f32[272,128]{1,0:T(8,128)}, f32[272,128]{1,0:T(8,128)}, f32[272,128]{1,0:T(8,128)}, /*index=5*/bf16[16,288,128]{2,1,0:T(8,128)(2,1)}) custom-call(s32[1]{0:T(128)} %bitcast.refs_0_, s32[1]{0:T(128)} %bitcast.1.refs_1_, s32[8]{0:T(128)} %bitcast.22, bf16[1024,128]{1,0:T(8,128)(2,1)} %bitcast.15, ...), custom_call_target="tpu_custom_call" | custom-call | flops 268435456 | bytes 2506792 | tf_op jit(solution)/shard_map/pallas_call | solution.py:128
  5.1 7.7 %all-to-all-start = ((bf16[16,288,128]{2,1,0:T(8,128)(2,1)}), bf16[16,288,128]{2,1,0:T(8,128)(2,1)S(1)}, u32[]{:S(2)}, u32[]{:S(2)}) async-start(bf16[16,288,128]{2,1,0:T(8,128)(2,1)} %get-tuple-element.94), calls=%async_computation | async-start | bytes 2359296 | tf_op jit(solution)/shard_map/all_to_all | solution.py:571
  12.9 3.3 %collective-permute-start = (f32[272,128]{1,0:T(8,128)S(1)}, f32[272,128]{1,0:T(8,128)S(1)}, u32[]{:S(2)}, u32[]{:S(2)}) collective-permute-start(f32[272,128]{1,0:T(8,128)S(1)} %copy-done.28), channel_id=1, source_target_pairs={{0,1},{1,2},{2,3},{3,4},{4,5},{5,6},{6,7},{7,8},{8,9},{9,10},{10,1... | collective-permute-start | bytes 417800 | tf_op jit(solution)/shard_map/ppermute | solution.py:558
  16.2 5.3 %collective-permute-start.1 = (f32[272,128]{1,0:T(8,128)S(1)}, f32[272,128]{1,0:T(8,128)S(1)}, u32[]{:S(2)}, u32[]{:S(2)}) collective-permute-start(f32[272,128]{1,0:T(8,128)S(1)} %copy-done.27), channel_id=1, source_target_pairs={{1,0},{2,1},{3,2},{4,3},{5,4},{6,5},{7,6},{8,7},{9,8},{10,9},{11,1... | collective-permute-start | bytes 417800 | tf_op jit(solution)/shard_map/ppermute | solution.py:558
  21.5 3.0 %collective-permute-start.2 = (f32[272,128]{1,0:T(8,128)S(1)}, f32[272,128]{1,0:T(8,128)S(1)}, u32[]{:S(2)}, u32[]{:S(2)}) collective-permute-start(f32[272,128]{1,0:T(8,128)S(1)} %copy-done.26), channel_id=1, source_target_pairs={{0,16},{16,32},{32,48},{48,64},{64,80},{80,96},{96,112},{112,128},... | collective-permute-start | bytes 417800 | tf_op jit(solution)/shard_map/ppermute | solution.py:558
  24.6 0.6 collective-permute-start.3
  25.1 7.6 %collective-permute-done.refs_5_.refs_7_.refs_8_ = f32[272,128]{1,0:T(8,128)S(1)} collective-permute-done((f32[272,128]{1,0:T(8,128)S(1)}, f32[272,128]{1,0:T(8,128)S(1)}, u32[]{:S(2)}, u32[]{:S(2)}) %collective-permute-start) | collective-permute-done | bytes 139296 | tf_op jit(solution)/shard_map/ppermute | solution.py:558
  32.8 4.2 %collective-permute-start.4 = (bf16[16,288,128]{2,1,0:T(8,128)(2,1)S(1)}, bf16[16,288,128]{2,1,0:T(8,128)(2,1)S(1)}, u32[]{:S(2)}, u32[]{:S(2)}) collective-permute-start(bf16[16,288,128]{2,1,0:T(8,128)(2,1)S(1)} %all-to-all-done.refs_0_.refs_2_), channel_id=1, source_target_pairs={{0,16},{16,0},{32,48},{48,32},{64,80},{80,64},{96,112},{112,96},{1... | collective-permute-start | bytes 3538952 | tf_op jit(solution)/shard_map/ppermute | solution.py:604
  37.0 0.9 shard_map.78
  37.9 15.5 %all-to-all-start.1 = ((f32[32,1,1152]{2,1,0:T(1,128)}), f32[32,1,1152]{2,1,0:T(1,128)S(1)}, u32[]{:S(2)}, u32[]{:S(2)}) async-start(f32[32,1,1152]{2,1,0:T(1,128)} %shard_map.78), calls=%async_computation.1 | async-start | bytes 294912 | tf_op jit(solution)/shard_map/all_to_all | solution.py:571
  53.4 2.0 shard_map.79
  55.5 14.4 %all-to-all-done.1.refs_1_ = f32[32,1,1152]{2,1,0:T(1,128)S(1)} async-done(((f32[32,1,1152]{2,1,0:T(1,128)}), f32[32,1,1152]{2,1,0:T(1,128)S(1)}, u32[]{:S(2)}, u32[]{:S(2)}) %all-to-all-start.1) | async-done | bytes 147488 | tf_op jit(solution)/shard_map/all_to_all | solution.py:571
  69.9 2.5 shard_map.80
  72.3 10.0 %all_to_all.55.refs_2_ = f32[16,8,128]{2,1,0:T(8,128)} all-to-all(f32[16,8,128]{2,1,0:T(8,128)S(1)} %get-tuple-element.102), channel_id=1, replica_groups=mesh['gx'=32,'gy'=16] {'gy'}, dimensions={0} | all-to-all | bytes 131072 | tf_op jit(solution)/shard_map/all_to_all | solution.py:571
  82.3 4.2 %shard_map.81 = (f32[1024,128]{1,0:T(8,128)}, bf16[1024,128]{1,0:T(8,128)(2,1)}, bf16[256,128]{1,0:T(8,128)(2,1)}, bf16[256,128]{1,0:T(8,128)(2,1)}, bf16[256,12...) custom-call(s32[1]{0:T(128)} %bitcast.refs_0_, s32[1]{0:T(128)} %bitcast.1.refs_1_, ...), custom_call_target="tpu_custom_call" | custom-call | flops 268435456 | bytes 3768328 | tf_op jit(solution)/shard_map/pallas_call | solution.py:128
  86.5 3.5 %all-to-all-start.3 = ((f32[16,32,128]{2,1,0:T(8,128)}), f32[16,32,128]{2,1,0:T(8,128)S(1)}, u32[]{:S(2)}, u32[]{:S(2)}) async-start(f32[16,32,128]{2,1,0:T(8,128)} %get-tuple-element.110), calls=%async_computation.3 | async-start | bytes 524288 | tf_op jit(solution)/shard_map/all_to_all | solution.py:571
  90.1 3.1 %collective-permute-start.5 = (bf16[256,128]{1,0:T(8,128)(2,1)}, bf16[256,128]{1,0:T(8,128)(2,1)S(1)}, u32[]{:S(2)}, u32[]{:S(2)}) collective-permute-start(bf16[256,128]{1,0:T(8,128)(2,1)} %get-tuple-element.106), channel_id=1, source_target_pairs={{0,1},{1,2},{2,3},{3,4},{4,5},{5,6},{6,7},{7,8},{8,9},{9,10},{10,1... | collective-permute-start | bytes 196616 | tf_op jit(solution)/shard_map/ppermute | solution.py:558
  93.2 5.5 %collective-permute-start.6 = (bf16[256,128]{1,0:T(8,128)(2,1)}, bf16[256,128]{1,0:T(8,128)(2,1)S(1)}, u32[]{:S(2)}, u32[]{:S(2)}) collective-permute-start(bf16[256,128]{1,0:T(8,128)(2,1)} %get-tuple-element.107), channel_id=1, source_target_pairs={{1,0},{2,1},{3,2},{4,3},{5,4},{6,5},{7,6},{8,7},{9,8},{10,9},{11,1... | collective-permute-start | bytes 196616 | tf_op jit(solution)/shard_map/ppermute | solution.py:558
  98.7 3.6 %collective-permute-start.7 = (bf16[256,128]{1,0:T(8,128)(2,1)}, bf16[256,128]{1,0:T(8,128)(2,1)S(1)}, u32[]{:S(2)}, u32[]{:S(2)}) collective-permute-start(bf16[256,128]{1,0:T(8,128)(2,1)} %get-tuple-element.108), channel_id=1, source_target_pairs={{0,16},{16,32},{32,48},{48,64},{64,80},{80,96},{96,112},{112,128},... | collective-permute-start | bytes 196616 | tf_op jit(solution)/shard_map/ppermute | solution.py:558
  102.2 0.1 collective-permute-start.8
  102.4 1.5 collective-permute-done.7.refs_3_
  103.9 2.5 collective-permute-done.8.refs_4_
  106.4 0.9 shard_map.83
  107.3 5.4 %all-to-all-start.4 = ((f32[32,1,1152]{2,1,0:T(1,128)}), f32[32,1,1152]{2,1,0:T(1,128)S(1)}, u32[]{:S(2)}, u32[]{:S(2)}) async-start(f32[32,1,1152]{2,1,0:T(1,128)} %shard_map.83), calls=%async_computation.4 | async-start | bytes 294912 | tf_op jit(solution)/shard_map/all_to_all | solution.py:571
  112.8 3.5 %shard_map.82 = (f32[1024,128]{1,0:T(8,128)}, f32[1024,128]{1,0:T(8,128)}, f32[256,128]{1,0:T(8,128)}, f32[256,128]{1,0:T(8,128)}, f32[256,128]{1,0:T(8,128)}, /*index=5*/f32[256,128]{1,0:T(8,128)}) custom-call(s32[1]{0:T(128)} %bitcast.refs_0_, s32[1]{0:T(128)} %bitcast.1.refs_1_, bf16[1024,128]{1,0:T(8,128)(2,1)} %get-tuple-element.105.refs_2_.refs_17_.refs_23_, ...), custom_call_target="tpu_custom_call" | custom-call | flops 268435456 | bytes 2621448 | tf_op jit(solution)/shard_map/pallas_call | solution.py:128
  116.3 1.9 collective-permute-start.9
  118.2 6.7 %collective-permute-start.10 = (f32[256,128]{1,0:T(8,128)}, f32[256,128]{1,0:T(8,128)S(1)}, u32[]{:S(2)}, u32[]{:S(2)}) collective-permute-start(f32[256,128]{1,0:T(8,128)} %get-tuple-element.116), channel_id=1, source_target_pairs={{1,0},{2,1},{3,2},{4,3},{5,4},{6,5},{7,6},{8,7},{9,8},{10,9},{11,1... | collective-permute-start | bytes 393224 | tf_op jit(solution)/shard_map/ppermute | solution.py:558
  124.9 2.2 collective-permute-start.11
  127.1 0.4 collective-permute-done.10.refs_13_.refs_14_
  127.5 1.8 collective-permute-done.11.refs_10_.refs_11_
  129.4 2.3 collective-permute-done.12.refs_11_.refs_12_
  131.7 0.8 shard_map.84
  132.5 9.8 %all_to_all.56.refs_2_ = f32[16,8,128]{2,1,0:T(8,128)} all-to-all(f32[16,8,128]{2,1,0:T(8,128)S(1)} %get-tuple-element.123), channel_id=1, replica_groups=mesh['gx'=32,'gy'=16] {'gy'}, dimensions={0} | all-to-all | bytes 131072 | tf_op jit(solution)/shard_map/all_to_all | solution.py:571
  142.3 4.7 %shard_map.85 = (f32[1024,128]{1,0:T(8,128)}, f32[1024,128]{1,0:T(8,128)}, f32[256,128]{1,0:T(8,128)}, f32[256,128]{1,0:T(8,128)}, f32[256,128]{1,0:T(8,128)}, /...) custom-call(s32[1]{0:T(128)} %bitcast.refs_0_, s32[1]{0:T(128)} %bitcast.1.refs_1_, ...), custom_call_target="tpu_custom_call" | custom-call | flops 268435456 | bytes 5603336 | tf_op jit(solution)/shard_map/pallas_call | solution.py:128
  147.0 3.5 %all-to-all-start.6 = ((f32[16,32,128]{2,1,0:T(8,128)}), f32[16,32,128]{2,1,0:T(8,128)S(1)}, u32[]{:S(2)}, u32[]{:S(2)}) async-start(f32[16,32,128]{2,1,0:T(8,128)} %get-tuple-element.135), calls=%async_computation.6 | async-start | bytes 524288 | tf_op jit(solution)/shard_map/all_to_all | solution.py:571
  150.5 3.1 %collective-permute-start.13 = (f32[256,128]{1,0:T(8,128)}, f32[256,128]{1,0:T(8,128)S(1)}, u32[]{:S(2)}, u32[]{:S(2)}) collective-permute-start(f32[256,128]{1,0:T(8,128)} %get-tuple-element.131), channel_id=1, source_target_pairs={{0,1},{1,2},{2,3},{3,4},{4,5},{5,6},{6,7},{7,8},{8,9},{9,10},{10,1... | collective-permute-start | bytes 393224 | tf_op jit(solution)/shard_map/ppermute | solution.py:558
  153.7 5.5 %collective-permute-start.14 = (f32[256,128]{1,0:T(8,128)}, f32[256,128]{1,0:T(8,128)S(1)}, u32[]{:S(2)}, u32[]{:S(2)}) collective-permute-start(f32[256,128]{1,0:T(8,128)} %get-tuple-element.132), channel_id=1, source_target_pairs={{1,0},{2,1},{3,2},{4,3},{5,4},{6,5},{7,6},{8,7},{9,8},{10,9},{11,1... | collective-permute-start | bytes 393224 | tf_op jit(solution)/shard_map/ppermute | solution.py:558
  159.1 4.0 %collective-permute-start.15 = (f32[256,128]{1,0:T(8,128)}, f32[256,128]{1,0:T(8,128)S(1)}, u32[]{:S(2)}, u32[]{:S(2)}) collective-permute-start(f32[256,128]{1,0:T(8,128)} %get-tuple-element.133), channel_id=1, source_target_pairs={{0,16},{16,32},{32,48},{48,64},{64,80},{80,96},{96,112},{112,128},... | collective-permute-start | bytes 393224 | tf_op jit(solution)/shard_map/ppermute | solution.py:558
  163.1 2.2 collective-permute-done.15.refs_3_
  165.4 2.3 collective-permute-done.16.refs_4_
  167.7 0.9 shard_map.87
  168.6 12.0 %all-to-all-start.7 = ((f32[32,1,1152]{2,1,0:T(1,128)}), f32[32,1,1152]{2,1,0:T(1,128)S(1)}, u32[]{:S(2)}, u32[]{:S(2)}) async-start(f32[32,1,1152]{2,1,0:T(1,128)} %shard_map.87), calls=%async_computation.7 | async-start | bytes 294912 | tf_op jit(solution)/shard_map/all_to_all | solution.py:571
  180.7 3.6 %shard_map.86 = (f32[1024,128]{1,0:T(8,128)}, f32[1024,128]{1,0:T(8,128)}, f32[256,128]{1,0:T(8,128)}, f32[256,128]{1,0:T(8,128)}, f32[256,128]{1,0:T(8,128)}, /*index=5*/f32[256,128]{1,0:T(8,128)}) custom-call(s32[1]{0:T(128)} %bitcast.refs_0_, s32[1]{0:T(128)} %bitcast.1.refs_1_, f32[1024,128]{1,0:T(8,128)} %get-tuple-element.130.refs_2_.refs_24_, ...), custom_call_target="tpu_custom_call" | custom-call | flops 268435456 | bytes 3145736 | tf_op jit(solution)/shard_map/pallas_call | solution.py:128
  184.3 1.9 collective-permute-start.17
  186.2 6.9 %collective-permute-start.18 = (f32[256,128]{1,0:T(8,128)}, f32[256,128]{1,0:T(8,128)S(1)}, u32[]{:S(2)}, u32[]{:S(2)}) collective-permute-start(f32[256,128]{1,0:T(8,128)} %get-tuple-element.141), channel_id=1, source_target_pairs={{1,0},{2,1},{3,2},{4,3},{5,4},{6,5},{7,6},{8,7},{9,8},{10,9},{11,1... | collective-permute-start | bytes 393224 | tf_op jit(solution)/shard_map/ppermute | solution.py:558
  193.1 2.2 collective-permute-start.19
  195.3 0.2 collective-permute-done.18.refs_19_
  195.5 2.0 collective-permute-done.19.refs_16_
  197.5 2.3 collective-permute-done.20.refs_17_
  199.9 0.9 shard_map.88
  200.7 9.8 %all_to_all.57.refs_2_ = f32[16,8,128]{2,1,0:T(8,128)} all-to-all(f32[16,8,128]{2,1,0:T(8,128)S(1)} %shard_map.88), channel_id=1, replica_groups=mesh['gx'=32,'gy'=16] {'gy'}, dimensions={0} | all-to-all | bytes 131072 | tf_op jit(solution)/shard_map/all_to_all | solution.py:571
  210.5 4.7 %shard_map.89 = (f32[1024,128]{1,0:T(8,128)}, f32[1024,128]{1,0:T(8,128)}, f32[256,128]{1,0:T(8,128)}, f32[256,128]{1,0:T(8,128)}, f32[256,128]{1,0:T(8,128)}, /...) custom-call(s32[1]{0:T(128)} %bitcast.refs_0_, s32[1]{0:T(128)} %bitcast.1.refs_1_, ...), custom_call_target="tpu_custom_call" | custom-call | flops 268435456 | bytes 7573512 | tf_op jit(solution)/shard_map/pallas_call | solution.py:128
  215.3 3.7 %all-to-all-start.9 = ((f32[16,32,128]{2,1,0:T(8,128)}), f32[16,32,128]{2,1,0:T(8,128)S(1)}, u32[]{:S(2)}, u32[]{:S(2)}) async-start(f32[16,32,128]{2,1,0:T(8,128)} %get-tuple-element.156), calls=%async_computation.9 | async-start | bytes 524288 | tf_op jit(solution)/shard_map/all_to_all | solution.py:571
  219.0 3.2 %collective-permute-start.21 = (f32[256,128]{1,0:T(8,128)}, f32[256,128]{1,0:T(8,128)S(1)}, u32[]{:S(2)}, u32[]{:S(2)}) collective-permute-start(f32[256,128]{1,0:T(8,128)} %get-tuple-element.157), channel_id=1, source_target_pairs={{0,16},{16,32},{32,48},{48,64},{64,80},{80,96},{96,112},{112,128},... | collective-permute-start | bytes 393224 | tf_op jit(solution)/shard_map/ppermute | solution.py:558
  222.2 2.3 collective-permute-done.21.refs_5_
  224.5 2.6 %collective-permute-done.22.refs_6_ = f32[256,128]{1,0:T(8,128)S(1)} collective-permute-done((f32[256,128]{1,0:T(8,128)}, f32[256,128]{1,0:T(8,128)S(1)}, u32[]{:S(2)}, u32[]{:S(2)}) %collective-permute-start.22) | collective-permute-done | bytes 131104 | tf_op jit(solution)/shard_map/ppermute | solution.py:558
  227.1 0.7 shard_map.90
  227.8 14.3 %all-to-all-start.10 = ((f32[32,8,128]{2,1,0:T(8,128)}), f32[32,8,128]{2,1,0:T(8,128)S(1)}, u32[]{:S(2)}, u32[]{:S(2)}) async-start(f32[32,8,128]{2,1,0:T(8,128)} %shard_map.90), calls=%async_computation.10 | async-start | bytes 262144 | tf_op jit(solution)/shard_map/all_to_all | solution.py:571
  242.1 2.2 collective-permute-start.23
  244.3 6.4 %collective-permute-start.24 = (f32[256,128]{1,0:T(8,128)S(1)}, f32[256,128]{1,0:T(8,128)S(1)}, u32[]{:S(2)}, u32[]{:S(2)}) collective-permute-start(f32[256,128]{1,0:T(8,128)S(1)} %copy-done.29), channel_id=1, source_target_pairs={{1,0},{2,1},{3,2},{4,3},{5,4},{6,5},{7,6},{8,7},{9,8},{10,9},{11,1... | collective-permute-start | bytes 393224 | tf_op jit(solution)/shard_map/ppermute | solution.py:558
  250.8 3.1 %shard_map.91 = (f32[1024,128]{1,0:T(8,128)}, f32[1024,128]{1,0:T(8,128)}, f32[1024,128]{1,0:T(8,128)}, f32[1024,128]{1,0:T(8,128)}) custom-call(f32[8,128]{1,0:T(8,128)} %get-tuple-element.149.refs_3_.refs_0_, f32[8,128]{1,0:T(8,128)} %get-tuple-element.163.refs_1_.refs_3_, f32[1024,128]{1,0:T(8,128)} %get-tuple-element.170.refs_2_, ...), custom_call_target="tpu_custom_call" | custom-call | flops 268435456 | bytes 2367488 | tf_op jit(solution)/shard_map/pallas_call | solution.py:128
  253.9 4.1 %all-to-all-done.10.refs_2_ = f32[32,8,128]{2,1,0:T(8,128)S(1)} async-done(((f32[32,8,128]{2,1,0:T(8,128)}), f32[32,8,128]{2,1,0:T(8,128)S(1)}, u32[]{:S(2)}, u32[]{:S(2)}) %all-to-all-start.10) | async-done | bytes 131104 | tf_op jit(solution)/shard_map/all_to_all | solution.py:571
  258.0 0.7 copy-done.8
  258.6 3.0 %shard_map.92 = (bf16[1024,128]{1,0:T(8,128)(2,1)}, bf16[1024,128]{1,0:T(8,128)(2,1)}) custom-call(s32[1]{0:T(128)} %bitcast.refs_0_, s32[1]{0:T(128)} %bitcast.1.refs_1_, f32[32,8,128]{2,1,0:T(8,128)} %copy-done.8, f32[8,128]{1,0:T(8,128)} %get-tuple-element.163.refs_1_.refs_3_, f32[1024,128]{1,0:T(8,128)} %get-tuple-element.164.refs_4_, ...), custom_call_target="tpu_custom_call" | custom-call | bytes 3805192 | tf_op jit(solution)/shard_map/pallas_call | solution.py:128
  (83 shorter events, 0.2 us)
Async XLA Ops:
  5.1 7.8 %copy-start.28 = (f32[272,128]{1,0:T(8,128)S(1)}, f32[272,128]{1,0:T(8,128)}, u32[]{:S(2)}) copy-start(f32[272,128]{1,0:T(8,128)} %get-tuple-element.90) | copy-start | bytes 417796
  5.1 11.1 %copy-start.27 = (f32[272,128]{1,0:T(8,128)S(1)}, f32[272,128]{1,0:T(8,128)}, u32[]{:S(2)}) copy-start(f32[272,128]{1,0:T(8,128)} %get-tuple-element.91) | copy-start | bytes 417796
  5.1 16.4 %copy-start.26 = (f32[272,128]{1,0:T(8,128)S(1)}, f32[272,128]{1,0:T(8,128)}, u32[]{:S(2)}) copy-start(f32[272,128]{1,0:T(8,128)} %get-tuple-element.92) | copy-start | bytes 417796
  5.1 19.4 %copy-start.25 = (f32[272,128]{1,0:T(8,128)S(1)}, f32[272,128]{1,0:T(8,128)}, u32[]{:S(2)}) copy-start(f32[272,128]{1,0:T(8,128)} %get-tuple-element.93) | copy-start | bytes 417796
  5.1 27.6 %all-to-all-start = ((bf16[16,288,128]{2,1,0:T(8,128)(2,1)}), bf16[16,288,128]{2,1,0:T(8,128)(2,1)S(1)}, u32[]{:S(2)}, u32[]{:S(2)}) async-start(bf16[16,288,128]{2,1,0:T(8,128)(2,1)} %get-tuple-element.94), calls=%async_computation | async-start | bytes 2359296 | tf_op jit(solution)/shard_map/all_to_all | solution.py:571
  12.9 19.8 %collective-permute-start = (f32[272,128]{1,0:T(8,128)S(1)}, f32[272,128]{1,0:T(8,128)S(1)}, u32[]{:S(2)}, u32[]{:S(2)}) collective-permute-start(f32[272,128]{1,0:T(8,128)S(1)} %copy-done.28), channel_id=1, source_target_pairs={{0,1},{1,2},{2,3},{3,4},{4,5},{5,6},{6,7},{7,8},{8,9},{9,10},{10,1... | collective-permute-start | bytes 417800 | tf_op jit(solution)/shard_map/ppermute | solution.py:558
  16.2 16.6 %collective-permute-start.1 = (f32[272,128]{1,0:T(8,128)S(1)}, f32[272,128]{1,0:T(8,128)S(1)}, u32[]{:S(2)}, u32[]{:S(2)}) collective-permute-start(f32[272,128]{1,0:T(8,128)S(1)} %copy-done.27), channel_id=1, source_target_pairs={{1,0},{2,1},{3,2},{4,3},{5,4},{6,5},{7,6},{8,7},{9,8},{10,9},{11,1... | collective-permute-start | bytes 417800 | tf_op jit(solution)/shard_map/ppermute | solution.py:558
  21.5 11.2 %collective-permute-start.2 = (f32[272,128]{1,0:T(8,128)S(1)}, f32[272,128]{1,0:T(8,128)S(1)}, u32[]{:S(2)}, u32[]{:S(2)}) collective-permute-start(f32[272,128]{1,0:T(8,128)S(1)} %copy-done.26), channel_id=1, source_target_pairs={{0,16},{16,32},{32,48},{48,64},{64,80},{80,96},{96,112},{112,128},... | collective-permute-start | bytes 417800 | tf_op jit(solution)/shard_map/ppermute | solution.py:558
  24.6 8.2 %collective-permute-start.3 = (f32[272,128]{1,0:T(8,128)S(1)}, f32[272,128]{1,0:T(8,128)S(1)}, u32[]{:S(2)}, u32[]{:S(2)}) collective-permute-start(f32[272,128]{1,0:T(8,128)S(1)} %copy-done.25), channel_id=1, source_target_pairs={{16,0},{32,16},{48,32},{64,48},{80,64},{96,80},{112,96},{128,112},... | collective-permute-start | bytes 417800 | tf_op jit(solution)/shard_map/ppermute | solution.py:558
  32.7 20.7 %copy-start = (f32[272,128]{1,0:T(8,128)}, f32[272,128]{1,0:T(8,128)S(1)}, u32[]{:S(2)}) copy-start(f32[272,128]{1,0:T(8,128)S(1)} %collective-permute-done.refs_5_.refs_7_.refs_8_) | copy-start | bytes 417796
  32.7 20.7 %copy-start.1 = (f32[272,128]{1,0:T(8,128)}, f32[272,128]{1,0:T(8,128)S(1)}, u32[]{:S(2)}) copy-start(f32[272,128]{1,0:T(8,128)S(1)} %collective-permute-done.1.refs_6_.refs_8_.refs_9_) | copy-start | bytes 417796
  32.7 20.7 %copy-start.2 = (f32[272,128]{1,0:T(8,128)}, f32[272,128]{1,0:T(8,128)S(1)}, u32[]{:S(2)}) copy-start(f32[272,128]{1,0:T(8,128)S(1)} %collective-permute-done.2.refs_3_.refs_5_.refs_6_) | copy-start | bytes 417796
  32.8 20.7 %copy-start.3 = (f32[272,128]{1,0:T(8,128)}, f32[272,128]{1,0:T(8,128)S(1)}, u32[]{:S(2)}) copy-start(f32[272,128]{1,0:T(8,128)S(1)} %collective-permute-done.3.refs_4_.refs_6_.refs_7_) | copy-start | bytes 417796
  32.8 37.1 %collective-permute-start.4 = (bf16[16,288,128]{2,1,0:T(8,128)(2,1)S(1)}, bf16[16,288,128]{2,1,0:T(8,128)(2,1)S(1)}, u32[]{:S(2)}, u32[]{:S(2)}) collective-permute-start(bf16[16,288,128]{2,1,0:T(8,128)(2,1)S(1)} %all-to-all-done.refs_0_.refs_2_), channel_id=1, source_target_pairs={{0,16},{16,0},{32,48},{48,32},{64,80},{80,64},{96,112},{112,96},{1... | collective-permute-start | bytes 3538952 | tf_op jit(solution)/shard_map/ppermute | solution.py:604
  37.9 32.0 %all-to-all-start.1 = ((f32[32,1,1152]{2,1,0:T(1,128)}), f32[32,1,1152]{2,1,0:T(1,128)S(1)}, u32[]{:S(2)}, u32[]{:S(2)}) async-start(f32[32,1,1152]{2,1,0:T(1,128)} %shard_map.78), calls=%async_computation.1 | async-start | bytes 294912 | tf_op jit(solution)/shard_map/all_to_all | solution.py:571
  86.5 19.9 %all-to-all-start.3 = ((f32[16,32,128]{2,1,0:T(8,128)}), f32[16,32,128]{2,1,0:T(8,128)S(1)}, u32[]{:S(2)}, u32[]{:S(2)}) async-start(f32[16,32,128]{2,1,0:T(8,128)} %get-tuple-element.110), calls=%async_computation.3 | async-start | bytes 524288 | tf_op jit(solution)/shard_map/all_to_all | solution.py:571
  90.1 12.3 %collective-permute-start.5 = (bf16[256,128]{1,0:T(8,128)(2,1)}, bf16[256,128]{1,0:T(8,128)(2,1)S(1)}, u32[]{:S(2)}, u32[]{:S(2)}) collective-permute-start(bf16[256,128]{1,0:T(8,128)(2,1)} %get-tuple-element.106), channel_id=1, source_target_pairs={{0,1},{1,2},{2,3},{3,4},{4,5},{5,6},{6,7},{7,8},{8,9},{9,10},{10,1... | collective-permute-start | bytes 196616 | tf_op jit(solution)/shard_map/ppermute | solution.py:558
  93.2 9.2 %collective-permute-start.6 = (bf16[256,128]{1,0:T(8,128)(2,1)}, bf16[256,128]{1,0:T(8,128)(2,1)S(1)}, u32[]{:S(2)}, u32[]{:S(2)}) collective-permute-start(bf16[256,128]{1,0:T(8,128)(2,1)} %get-tuple-element.107), channel_id=1, source_target_pairs={{1,0},{2,1},{3,2},{4,3},{5,4},{6,5},{7,6},{8,7},{9,8},{10,9},{11,1... | collective-permute-start | bytes 196616 | tf_op jit(solution)/shard_map/ppermute | solution.py:558
  98.7 5.2 %collective-permute-start.7 = (bf16[256,128]{1,0:T(8,128)(2,1)}, bf16[256,128]{1,0:T(8,128)(2,1)S(1)}, u32[]{:S(2)}, u32[]{:S(2)}) collective-permute-start(bf16[256,128]{1,0:T(8,128)(2,1)} %get-tuple-element.108), channel_id=1, source_target_pairs={{0,16},{16,32},{32,48},{48,64},{64,80},{80,96},{96,112},{112,128},... | collective-permute-start | bytes 196616 | tf_op jit(solution)/shard_map/ppermute | solution.py:558
  102.2 4.2 %collective-permute-start.8 = (bf16[256,128]{1,0:T(8,128)(2,1)}, bf16[256,128]{1,0:T(8,128)(2,1)S(1)}, u32[]{:S(2)}, u32[]{:S(2)}) collective-permute-start(bf16[256,128]{1,0:T(8,128)(2,1)} %get-tuple-element.109), channel_id=1, source_target_pairs={{16,0},{32,16},{48,32},{64,48},{80,64},{96,80},{112,96},{128,112},... | collective-permute-start | bytes 196616 | tf_op jit(solution)/shard_map/ppermute | solution.py:558
  102.4 10.4 %copy-start.21 = (bf16[256,128]{1,0:T(8,128)(2,1)}, bf16[256,128]{1,0:T(8,128)(2,1)S(1)}, u32[]{:S(2)}) copy-start(bf16[256,128]{1,0:T(8,128)(2,1)S(1)} %collective-permute-done.5.refs_5_) | copy-start | bytes 196612
  102.4 10.4 %copy-start.22 = (bf16[256,128]{1,0:T(8,128)(2,1)}, bf16[256,128]{1,0:T(8,128)(2,1)S(1)}, u32[]{:S(2)}) copy-start(bf16[256,128]{1,0:T(8,128)(2,1)S(1)} %collective-permute-done.6.refs_6_) | copy-start | bytes 196612
  103.9 8.9 %copy-start.23 = (bf16[256,128]{1,0:T(8,128)(2,1)}, bf16[256,128]{1,0:T(8,128)(2,1)S(1)}, u32[]{:S(2)}) copy-start(bf16[256,128]{1,0:T(8,128)(2,1)S(1)} %collective-permute-done.7.refs_3_) | copy-start | bytes 196612
  106.4 6.3 %copy-start.24 = (bf16[256,128]{1,0:T(8,128)(2,1)}, bf16[256,128]{1,0:T(8,128)(2,1)S(1)}, u32[]{:S(2)}) copy-start(bf16[256,128]{1,0:T(8,128)(2,1)S(1)} %collective-permute-done.8.refs_4_) | copy-start | bytes 196612
  107.3 24.4 %all-to-all-start.4 = ((f32[32,1,1152]{2,1,0:T(1,128)}), f32[32,1,1152]{2,1,0:T(1,128)S(1)}, u32[]{:S(2)}, u32[]{:S(2)}) async-start(f32[32,1,1152]{2,1,0:T(1,128)} %shard_map.83), calls=%async_computation.4 | async-start | bytes 294912 | tf_op jit(solution)/shard_map/all_to_all | solution.py:571
  116.3 10.8 %collective-permute-start.9 = (f32[256,128]{1,0:T(8,128)}, f32[256,128]{1,0:T(8,128)S(1)}, u32[]{:S(2)}, u32[]{:S(2)}) collective-permute-start(f32[256,128]{1,0:T(8,128)} %get-tuple-element.115), channel_id=1, source_target_pairs={{0,1},{1,2},{2,3},{3,4},{4,5},{5,6},{6,7},{7,8},{8,9},{9,10},{10,1... | collective-permute-start | bytes 393224 | tf_op jit(solution)/shard_map/ppermute | solution.py:558
  118.2 9.3 %collective-permute-start.10 = (f32[256,128]{1,0:T(8,128)}, f32[256,128]{1,0:T(8,128)S(1)}, u32[]{:S(2)}, u32[]{:S(2)}) collective-permute-start(f32[256,128]{1,0:T(8,128)} %get-tuple-element.116), channel_id=1, source_target_pairs={{1,0},{2,1},{3,2},{4,3},{5,4},{6,5},{7,6},{8,7},{9,8},{10,9},{11,1... | collective-permute-start | bytes 393224 | tf_op jit(solution)/shard_map/ppermute | solution.py:558
  124.9 4.5 %collective-permute-start.11 = (f32[256,128]{1,0:T(8,128)}, f32[256,128]{1,0:T(8,128)S(1)}, u32[]{:S(2)}, u32[]{:S(2)}) collective-permute-start(f32[256,128]{1,0:T(8,128)} %get-tuple-element.117), channel_id=1, source_target_pairs={{0,16},{16,32},{32,48},{48,64},{64,80},{80,96},{96,112},{112,128},... | collective-permute-start | bytes 393224 | tf_op jit(solution)/shard_map/ppermute | solution.py:558
  127.1 4.6 %collective-permute-start.12 = (f32[256,128]{1,0:T(8,128)}, f32[256,128]{1,0:T(8,128)S(1)}, u32[]{:S(2)}, u32[]{:S(2)}) collective-permute-start(f32[256,128]{1,0:T(8,128)} %get-tuple-element.118), channel_id=1, source_target_pairs={{16,0},{32,16},{48,32},{64,48},{80,64},{96,80},{112,96},{128,112},... | collective-permute-start | bytes 393224 | tf_op jit(solution)/shard_map/ppermute | solution.py:558
  127.1 15.1 %copy-start.4 = (f32[256,128]{1,0:T(8,128)}, f32[256,128]{1,0:T(8,128)S(1)}, u32[]{:S(2)}) copy-start(f32[256,128]{1,0:T(8,128)S(1)} %collective-permute-done.9.refs_12_.refs_13_) | copy-start | bytes 393220
  127.5 14.7 %copy-start.5 = (f32[256,128]{1,0:T(8,128)}, f32[256,128]{1,0:T(8,128)S(1)}, u32[]{:S(2)}) copy-start(f32[256,128]{1,0:T(8,128)S(1)} %collective-permute-done.10.refs_13_.refs_14_) | copy-start | bytes 393220
  129.4 12.9 %copy-start.6 = (f32[256,128]{1,0:T(8,128)}, f32[256,128]{1,0:T(8,128)S(1)}, u32[]{:S(2)}) copy-start(f32[256,128]{1,0:T(8,128)S(1)} %collective-permute-done.11.refs_10_.refs_11_) | copy-start | bytes 393220
  131.7 10.5 %copy-start.7 = (f32[256,128]{1,0:T(8,128)}, f32[256,128]{1,0:T(8,128)S(1)}, u32[]{:S(2)}) copy-start(f32[256,128]{1,0:T(8,128)S(1)} %collective-permute-done.12.refs_11_.refs_12_) | copy-start | bytes 393220
  147.0 20.8 %all-to-all-start.6 = ((f32[16,32,128]{2,1,0:T(8,128)}), f32[16,32,128]{2,1,0:T(8,128)S(1)}, u32[]{:S(2)}, u32[]{:S(2)}) async-start(f32[16,32,128]{2,1,0:T(8,128)} %get-tuple-element.135), calls=%async_computation.6 | async-start | bytes 524288 | tf_op jit(solution)/shard_map/all_to_all | solution.py:571
  150.5 12.6 %collective-permute-start.13 = (f32[256,128]{1,0:T(8,128)}, f32[256,128]{1,0:T(8,128)S(1)}, u32[]{:S(2)}, u32[]{:S(2)}) collective-permute-start(f32[256,128]{1,0:T(8,128)} %get-tuple-element.131), channel_id=1, source_target_pairs={{0,1},{1,2},{2,3},{3,4},{4,5},{5,6},{6,7},{7,8},{8,9},{9,10},{10,1... | collective-permute-start | bytes 393224 | tf_op jit(solution)/shard_map/ppermute | solution.py:558
  153.7 9.5 %collective-permute-start.14 = (f32[256,128]{1,0:T(8,128)}, f32[256,128]{1,0:T(8,128)S(1)}, u32[]{:S(2)}, u32[]{:S(2)}) collective-permute-start(f32[256,128]{1,0:T(8,128)} %get-tuple-element.132), channel_id=1, source_target_pairs={{1,0},{2,1},{3,2},{4,3},{5,4},{6,5},{7,6},{8,7},{9,8},{10,9},{11,1... | collective-permute-start | bytes 393224 | tf_op jit(solution)/shard_map/ppermute | solution.py:558
  159.1 6.2 %collective-permute-start.15 = (f32[256,128]{1,0:T(8,128)}, f32[256,128]{1,0:T(8,128)S(1)}, u32[]{:S(2)}, u32[]{:S(2)}) collective-permute-start(f32[256,128]{1,0:T(8,128)} %get-tuple-element.133), channel_id=1, source_target_pairs={{0,16},{16,32},{32,48},{48,64},{64,80},{80,96},{96,112},{112,128},... | collective-permute-start | bytes 393224 | tf_op jit(solution)/shard_map/ppermute | solution.py:558
  163.1 4.6 %collective-permute-start.16 = (f32[256,128]{1,0:T(8,128)}, f32[256,128]{1,0:T(8,128)S(1)}, u32[]{:S(2)}, u32[]{:S(2)}) collective-permute-start(f32[256,128]{1,0:T(8,128)} %get-tuple-element.134), channel_id=1, source_target_pairs={{16,0},{32,16},{48,32},{64,48},{80,64},{96,80},{112,96},{128,112},... | collective-permute-start | bytes 393224 | tf_op jit(solution)/shard_map/ppermute | solution.py:558
  163.1 17.5 %copy-start.15 = (f32[256,128]{1,0:T(8,128)}, f32[256,128]{1,0:T(8,128)S(1)}, u32[]{:S(2)}) copy-start(f32[256,128]{1,0:T(8,128)S(1)} %collective-permute-done.13.refs_5_) | copy-start | bytes 393220
  163.1 17.5 %copy-start.16 = (f32[256,128]{1,0:T(8,128)}, f32[256,128]{1,0:T(8,128)S(1)}, u32[]{:S(2)}) copy-start(f32[256,128]{1,0:T(8,128)S(1)} %collective-permute-done.14.refs_6_) | copy-start | bytes 393220
  165.4 15.3 %copy-start.17 = (f32[256,128]{1,0:T(8,128)}, f32[256,128]{1,0:T(8,128)S(1)}, u32[]{:S(2)}) copy-start(f32[256,128]{1,0:T(8,128)S(1)} %collective-permute-done.15.refs_3_) | copy-start | bytes 393220
  167.7 13.0 %copy-start.19 = (f32[256,128]{1,0:T(8,128)}, f32[256,128]{1,0:T(8,128)S(1)}, u32[]{:S(2)}) copy-start(f32[256,128]{1,0:T(8,128)S(1)} %collective-permute-done.16.refs_4_) | copy-start | bytes 393220
  168.6 31.3 %all-to-all-start.7 = ((f32[32,1,1152]{2,1,0:T(1,128)}), f32[32,1,1152]{2,1,0:T(1,128)S(1)}, u32[]{:S(2)}, u32[]{:S(2)}) async-start(f32[32,1,1152]{2,1,0:T(1,128)} %shard_map.87), calls=%async_computation.7 | async-start | bytes 294912 | tf_op jit(solution)/shard_map/all_to_all | solution.py:571
  184.3 11.0 %collective-permute-start.17 = (f32[256,128]{1,0:T(8,128)}, f32[256,128]{1,0:T(8,128)S(1)}, u32[]{:S(2)}, u32[]{:S(2)}) collective-permute-start(f32[256,128]{1,0:T(8,128)} %get-tuple-element.140), channel_id=1, source_target_pairs={{0,1},{1,2},{2,3},{3,4},{4,5},{5,6},{6,7},{7,8},{8,9},{9,10},{10,1... | collective-permute-start | bytes 393224 | tf_op jit(solution)/shard_map/ppermute | solution.py:558
  186.2 9.3 %collective-permute-start.18 = (f32[256,128]{1,0:T(8,128)}, f32[256,128]{1,0:T(8,128)S(1)}, u32[]{:S(2)}, u32[]{:S(2)}) collective-permute-start(f32[256,128]{1,0:T(8,128)} %get-tuple-element.141), channel_id=1, source_target_pairs={{1,0},{2,1},{3,2},{4,3},{5,4},{6,5},{7,6},{8,7},{9,8},{10,9},{11,1... | collective-permute-start | bytes 393224 | tf_op jit(solution)/shard_map/ppermute | solution.py:558
  193.1 4.5 %collective-permute-start.19 = (f32[256,128]{1,0:T(8,128)}, f32[256,128]{1,0:T(8,128)S(1)}, u32[]{:S(2)}, u32[]{:S(2)}) collective-permute-start(f32[256,128]{1,0:T(8,128)} %get-tuple-element.142), channel_id=1, source_target_pairs={{0,16},{16,32},{32,48},{48,64},{64,80},{80,96},{96,112},{112,128},... | collective-permute-start | bytes 393224 | tf_op jit(solution)/shard_map/ppermute | solution.py:558
  195.3 4.6 %collective-permute-start.20 = (f32[256,128]{1,0:T(8,128)}, f32[256,128]{1,0:T(8,128)S(1)}, u32[]{:S(2)}, u32[]{:S(2)}) collective-permute-start(f32[256,128]{1,0:T(8,128)} %get-tuple-element.143), channel_id=1, source_target_pairs={{16,0},{32,16},{48,32},{64,48},{80,64},{96,80},{112,96},{128,112},... | collective-permute-start | bytes 393224 | tf_op jit(solution)/shard_map/ppermute | solution.py:558
  195.3 15.2 %copy-start.9 = (f32[256,128]{1,0:T(8,128)}, f32[256,128]{1,0:T(8,128)S(1)}, u32[]{:S(2)}) copy-start(f32[256,128]{1,0:T(8,128)S(1)} %collective-permute-done.17.refs_18_) | copy-start | bytes 393220
  195.5 15.0 %copy-start.10 = (f32[256,128]{1,0:T(8,128)}, f32[256,128]{1,0:T(8,128)S(1)}, u32[]{:S(2)}) copy-start(f32[256,128]{1,0:T(8,128)S(1)} %collective-permute-done.18.refs_19_) | copy-start | bytes 393220
  197.5 13.0 %copy-start.11 = (f32[256,128]{1,0:T(8,128)}, f32[256,128]{1,0:T(8,128)S(1)}, u32[]{:S(2)}) copy-start(f32[256,128]{1,0:T(8,128)S(1)} %collective-permute-done.19.refs_16_) | copy-start | bytes 393220
  199.9 10.6 %copy-start.12 = (f32[256,128]{1,0:T(8,128)}, f32[256,128]{1,0:T(8,128)S(1)}, u32[]{:S(2)}) copy-start(f32[256,128]{1,0:T(8,128)S(1)} %collective-permute-done.20.refs_17_) | copy-start | bytes 393220
  215.3 26.9 %copy-start.30 = (f32[256,128]{1,0:T(8,128)S(1)}, f32[256,128]{1,0:T(8,128)}, u32[]{:S(2)}) copy-start(f32[256,128]{1,0:T(8,128)} %get-tuple-element.167) | copy-start | bytes 393220
  215.3 29.1 %copy-start.29 = (f32[256,128]{1,0:T(8,128)S(1)}, f32[256,128]{1,0:T(8,128)}, u32[]{:S(2)}) copy-start(f32[256,128]{1,0:T(8,128)} %get-tuple-element.168) | copy-start | bytes 393220
  215.3 11.8 %all-to-all-start.9 = ((f32[16,32,128]{2,1,0:T(8,128)}), f32[16,32,128]{2,1,0:T(8,128)S(1)}, u32[]{:S(2)}, u32[]{:S(2)}) async-start(f32[16,32,128]{2,1,0:T(8,128)} %get-tuple-element.156), calls=%async_computation.9 | async-start | bytes 524288 | tf_op jit(solution)/shard_map/all_to_all | solution.py:571
  219.0 5.5 %collective-permute-start.21 = (f32[256,128]{1,0:T(8,128)}, f32[256,128]{1,0:T(8,128)S(1)}, u32[]{:S(2)}, u32[]{:S(2)}) collective-permute-start(f32[256,128]{1,0:T(8,128)} %get-tuple-element.157), channel_id=1, source_target_pairs={{0,16},{16,32},{32,48},{48,64},{64,80},{80,96},{96,112},{112,128},... | collective-permute-start | bytes 393224 | tf_op jit(solution)/shard_map/ppermute | solution.py:558
  222.2 4.9 %collective-permute-start.22 = (f32[256,128]{1,0:T(8,128)}, f32[256,128]{1,0:T(8,128)S(1)}, u32[]{:S(2)}, u32[]{:S(2)}) collective-permute-start(f32[256,128]{1,0:T(8,128)} %get-tuple-element.158), channel_id=1, source_target_pairs={{16,0},{32,16},{48,32},{64,48},{80,64},{96,80},{112,96},{128,112},... | collective-permute-start | bytes 393224 | tf_op jit(solution)/shard_map/ppermute | solution.py:558
  224.5 29.4 %copy-start.13 = (f32[256,128]{1,0:T(8,128)}, f32[256,128]{1,0:T(8,128)S(1)}, u32[]{:S(2)}) copy-start(f32[256,128]{1,0:T(8,128)S(1)} %collective-permute-done.21.refs_5_) | copy-start | bytes 393220
  227.1 26.7 %copy-start.14 = (f32[256,128]{1,0:T(8,128)}, f32[256,128]{1,0:T(8,128)S(1)}, u32[]{:S(2)}) copy-start(f32[256,128]{1,0:T(8,128)S(1)} %collective-permute-done.22.refs_6_) | copy-start | bytes 393220
  227.8 30.1 %all-to-all-start.10 = ((f32[32,8,128]{2,1,0:T(8,128)}), f32[32,8,128]{2,1,0:T(8,128)S(1)}, u32[]{:S(2)}, u32[]{:S(2)}) async-start(f32[32,8,128]{2,1,0:T(8,128)} %shard_map.90), calls=%async_computation.10 | async-start | bytes 262144 | tf_op jit(solution)/shard_map/all_to_all | solution.py:571
  242.1 11.7 %collective-permute-start.23 = (f32[256,128]{1,0:T(8,128)S(1)}, f32[256,128]{1,0:T(8,128)S(1)}, u32[]{:S(2)}, u32[]{:S(2)}) collective-permute-start(f32[256,128]{1,0:T(8,128)S(1)} %copy-done.30), channel_id=1, source_target_pairs={{0,1},{1,2},{2,3},{3,4},{4,5},{5,6},{6,7},{7,8},{8,9},{9,10},{10,1... | collective-permute-start | bytes 393224 | tf_op jit(solution)/shard_map/ppermute | solution.py:558
  244.3 9.5 %collective-permute-start.24 = (f32[256,128]{1,0:T(8,128)S(1)}, f32[256,128]{1,0:T(8,128)S(1)}, u32[]{:S(2)}, u32[]{:S(2)}) collective-permute-start(f32[256,128]{1,0:T(8,128)S(1)} %copy-done.29), channel_id=1, source_target_pairs={{1,0},{2,1},{3,2},{4,3},{5,4},{6,5},{7,6},{8,7},{9,8},{10,9},{11,1... | collective-permute-start | bytes 393224 | tf_op jit(solution)/shard_map/ppermute | solution.py:558
  253.9 4.1 %copy-start.18 = (f32[256,128]{1,0:T(8,128)}, f32[256,128]{1,0:T(8,128)S(1)}, u32[]{:S(2)}) copy-start(f32[256,128]{1,0:T(8,128)S(1)} %collective-permute-done.23.refs_7_) | copy-start | bytes 393220
  253.9 4.1 %copy-start.20 = (f32[256,128]{1,0:T(8,128)}, f32[256,128]{1,0:T(8,128)S(1)}, u32[]{:S(2)}) copy-start(f32[256,128]{1,0:T(8,128)S(1)} %collective-permute-done.24.refs_8_) | copy-start | bytes 393220
  258.0 0.7 copy-start.8

commit v5 on v4

--- a/solution.py
+++ b/solution.py
@@ -18,7 +18,7 @@
 NCG = 1024
 VMEM_BYTES = 60 * 1024 * 1024
 SOME_BYTES = 16 * 1024 * 1024
-PAD = 32
+PAD = 16
 LONG = SL * 128 + 128
 WIN = 32
 
@@ -246,7 +246,7 @@
     for i, face in enumerate((g0, g1, g2, g3)):
         local = wt[i] * dot(inverse[rows(i)], scaled)
         l_out[rows(i)] = local
-        face[...] = local
+        face[...] = local.astype(BF16)
         face.send()
 
 
@@ -275,7 +275,7 @@
         s = joined(dot(schur[rows(i)], zb[...]))
         s_out[rows(i)] = s
         if faces:
-            faces[i][...] = s
+            faces[i][...] = s.astype(BF16)
             faces[i].send()
     s_out.send()
 
@@ -587,7 +587,7 @@
     block = 2 * NI * NI * R
     table = pltpu.VMEM((128, 128), F32)
     zb = pltpu.VMEM((NI, 2 * R), BF16)
-    face = ((FACE, R), F32)
+    face = ((FACE, R), BF16)
 
     l0, f0, f1, f2, f3, m = call(
         start_kernel,

time: 263 us -> 259 us (0.985)
  waiting for transfers between devices: 48.8 us -> 46 us
    ppermute x24, waiting for transfers between devices: 30.3 us -> 27.5 us  [across(): return (lax.ppermute(high, axis, up), lax.ppermute(low, axis, down))]
  transfers between devices with their start and end apart: 33 -> 33, of which waited for: 15 -> 13; matrix products, arithmetic and copies ran while one was open for 0% -> 0% of each run, Pallas kernels for 5% -> 5%
where the time goes in v5:
time: 259 us; the launch traced here: 258 us
  starting transfers between devices  140 us (54%)
  waiting for transfers between devices  46 us (18%)
  Pallas kernels  40 us (15%)
  blocking collectives  29.5 us (11%)
    ppermute x24, starting transfers between devices, across(): return (lax.ppermute(high, axis, up), lax.ppermute(low, axis, down))  70.1 us
    all_to_all x8, starting transfers between devices, swap(): return lax.all_to_all(value, axis, 0, 0, tiled=True)  65.6 us
    pallas_call x16, Pallas kernels, call(): pl.pallas_call(moved, out_shape=tuple((jax.ShapeDtypeStruct(*t) for t in...  40 us
    all_to_all x3, blocking collectives, swap(): return lax.all_to_all(value, axis, 0, 0, tiled=True)  29.5 us
    ppermute x24, waiting for transfers between devices, across(): return (lax.ppermute(high, axis, up), lax.ppermute(low, axis, down))  27.5 us
    all_to_all x8, waiting for transfers between devices, swap(): return lax.all_to_all(value, axis, 0, 0, tiled=True)  18.5 us
  transfers between devices with their start and end apart: 33, of which 13 were waited for; matrix products, arithmetic and copies ran while one was open for 0% of the time, Pallas kernels for 5%

profile of v5, /device:TPU:1, one launch (start us, length us, event | category | flops | bytes accessed | tf_op | source)
XLA Modules:
  0.0 257.6 jit_solution(16082493894640737477)
XLA Ops:
  0.6 4.4 %shard_map.77 = (f32[1024,128]{1,0:T(8,128)}, f32[272,128]{1,0:T(8,128)}, f32[272,128]{1,0:T(8,128)}, f32[272,128]{1,0:T(8,128)}, f32[272,128]{1,0:T(8,128)}, /*index=5*/bf16[16,288,128]{2,1,0:T(8,128)(2,1)}) custom-call(s32[1]{0:T(128)} %bitcast.refs_0_, s32[1]{0:T(128)} %bitcast.1.refs_1_, s32[8]{0:T(128)} %bitcast.22, bf16[1024,128]{1,0:T(8,128)(2,1)} %bitcast.15, ...), custom_call_target="tpu_custom_call" | custom-call | flops 268435456 | bytes 2506792 | tf_op jit(solution)/shard_map/pallas_call | solution.py:128
  5.1 0.0 copy-start.26
  5.1 0.0 copy-start.25
  5.1 7.7 %all-to-all-start = ((bf16[16,288,128]{2,1,0:T(8,128)(2,1)}), bf16[16,288,128]{2,1,0:T(8,128)(2,1)S(1)}, u32[]{:S(2)}, u32[]{:S(2)}) async-start(bf16[16,288,128]{2,1,0:T(8,128)(2,1)} %get-tuple-element.94), calls=%async_computation | async-start | bytes 2359296 | tf_op jit(solution)/shard_map/all_to_all | solution.py:571
  12.9 3.3 %collective-permute-start = (f32[272,128]{1,0:T(8,128)S(1)}, f32[272,128]{1,0:T(8,128)S(1)}, u32[]{:S(2)}, u32[]{:S(2)}) collective-permute-start(f32[272,128]{1,0:T(8,128)S(1)} %copy-done.28), channel_id=1, source_target_pairs={{0,1},{1,2},{2,3},{3,4},{4,5},{5,6},{6,7},{7,8},{8,9},{9,10},{10,1... | collective-permute-start | bytes 417800 | tf_op jit(solution)/shard_map/ppermute | solution.py:558
  16.2 5.3 %collective-permute-start.1 = (f32[272,128]{1,0:T(8,128)S(1)}, f32[272,128]{1,0:T(8,128)S(1)}, u32[]{:S(2)}, u32[]{:S(2)}) collective-permute-start(f32[272,128]{1,0:T(8,128)S(1)} %copy-done.27), channel_id=1, source_target_pairs={{1,0},{2,1},{3,2},{4,3},{5,4},{6,5},{7,6},{8,7},{9,8},{10,9},{11,1... | collective-permute-start | bytes 417800 | tf_op jit(solution)/shard_map/ppermute | solution.py:558
  21.5 3.0 %collective-permute-start.2 = (f32[272,128]{1,0:T(8,128)S(1)}, f32[272,128]{1,0:T(8,128)S(1)}, u32[]{:S(2)}, u32[]{:S(2)}) collective-permute-start(f32[272,128]{1,0:T(8,128)S(1)} %copy-done.26), channel_id=1, source_target_pairs={{0,16},{16,32},{32,48},{48,64},{64,80},{80,96},{96,112},{112,128},... | collective-permute-start | bytes 417800 | tf_op jit(solution)/shard_map/ppermute | solution.py:558
  24.6 0.6 collective-permute-start.3
  25.1 7.6 %collective-permute-done.refs_5_.refs_7_.refs_8_ = f32[272,128]{1,0:T(8,128)S(1)} collective-permute-done((f32[272,128]{1,0:T(8,128)S(1)}, f32[272,128]{1,0:T(8,128)S(1)}, u32[]{:S(2)}, u32[]{:S(2)}) %collective-permute-start) | collective-permute-done | bytes 139296 | tf_op jit(solution)/shard_map/ppermute | solution.py:558
  32.8 4.2 %collective-permute-start.4 = (bf16[16,288,128]{2,1,0:T(8,128)(2,1)S(1)}, bf16[16,288,128]{2,1,0:T(8,128)(2,1)S(1)}, u32[]{:S(2)}, u32[]{:S(2)}) collective-permute-start(bf16[16,288,128]{2,1,0:T(8,128)(2,1)S(1)} %all-to-all-done.refs_0_.refs_2_), channel_id=1, source_target_pairs={{0,16},{16,0},{32,48},{48,32},{64,80},{80,64},{96,112},{112,96},{1... | collective-permute-start | bytes 3538952 | tf_op jit(solution)/shard_map/ppermute | solution.py:604
  37.0 0.9 shard_map.78
  37.9 15.5 %all-to-all-start.1 = ((f32[32,1,1152]{2,1,0:T(1,128)}), f32[32,1,1152]{2,1,0:T(1,128)S(1)}, u32[]{:S(2)}, u32[]{:S(2)}) async-start(f32[32,1,1152]{2,1,0:T(1,128)} %shard_map.78), calls=%async_computation.1 | async-start | bytes 294912 | tf_op jit(solution)/shard_map/all_to_all | solution.py:571
  53.4 2.0 shard_map.79
  55.5 14.4 %all-to-all-done.1.refs_1_ = f32[32,1,1152]{2,1,0:T(1,128)S(1)} async-done(((f32[32,1,1152]{2,1,0:T(1,128)}), f32[32,1,1152]{2,1,0:T(1,128)S(1)}, u32[]{:S(2)}, u32[]{:S(2)}) %all-to-all-start.1) | async-done | bytes 147488 | tf_op jit(solution)/shard_map/all_to_all | solution.py:571
  69.9 2.4 shard_map.80
  72.3 10.0 %all_to_all.55.refs_2_ = f32[16,8,128]{2,1,0:T(8,128)} all-to-all(f32[16,8,128]{2,1,0:T(8,128)S(1)} %get-tuple-element.102), channel_id=1, replica_groups=mesh['gx'=32,'gy'=16] {'gy'}, dimensions={0} | all-to-all | bytes 131072 | tf_op jit(solution)/shard_map/all_to_all | solution.py:571
  82.3 4.1 %shard_map.81 = (f32[1024,128]{1,0:T(8,128)}, bf16[1024,128]{1,0:T(8,128)(2,1)}, bf16[256,128]{1,0:T(8,128)(2,1)}, bf16[256,128]{1,0:T(8,128)(2,1)}, bf16[256,12...) custom-call(s32[1]{0:T(128)} %bitcast.refs_0_, s32[1]{0:T(128)} %bitcast.1.refs_1_, ...), custom_call_target="tpu_custom_call" | custom-call | flops 268435456 | bytes 3768328 | tf_op jit(solution)/shard_map/pallas_call | solution.py:128
  86.4 3.5 %all-to-all-start.3 = ((f32[16,16,128]{2,1,0:T(8,128)}), f32[16,16,128]{2,1,0:T(8,128)S(1)}, u32[]{:S(2)}, u32[]{:S(2)}) async-start(f32[16,16,128]{2,1,0:T(8,128)} %get-tuple-element.110), calls=%async_computation.3 | async-start | bytes 262144 | tf_op jit(solution)/shard_map/all_to_all | solution.py:571
  90.0 3.1 %collective-permute-start.5 = (bf16[256,128]{1,0:T(8,128)(2,1)}, bf16[256,128]{1,0:T(8,128)(2,1)S(1)}, u32[]{:S(2)}, u32[]{:S(2)}) collective-permute-start(bf16[256,128]{1,0:T(8,128)(2,1)} %get-tuple-element.106), channel_id=1, source_target_pairs={{0,1},{1,2},{2,3},{3,4},{4,5},{5,6},{6,7},{7,8},{8,9},{9,10},{10,1... | collective-permute-start | bytes 196616 | tf_op jit(solution)/shard_map/ppermute | solution.py:558
  93.1 5.5 %collective-permute-start.6 = (bf16[256,128]{1,0:T(8,128)(2,1)}, bf16[256,128]{1,0:T(8,128)(2,1)S(1)}, u32[]{:S(2)}, u32[]{:S(2)}) collective-permute-start(bf16[256,128]{1,0:T(8,128)(2,1)} %get-tuple-element.107), channel_id=1, source_target_pairs={{1,0},{2,1},{3,2},{4,3},{5,4},{6,5},{7,6},{8,7},{9,8},{10,9},{11,1... | collective-permute-start | bytes 196616 | tf_op jit(solution)/shard_map/ppermute | solution.py:558
  98.6 3.6 %collective-permute-start.7 = (bf16[256,128]{1,0:T(8,128)(2,1)}, bf16[256,128]{1,0:T(8,128)(2,1)S(1)}, u32[]{:S(2)}, u32[]{:S(2)}) collective-permute-start(bf16[256,128]{1,0:T(8,128)(2,1)} %get-tuple-element.108), channel_id=1, source_target_pairs={{0,16},{16,32},{32,48},{48,64},{64,80},{80,96},{96,112},{112,128},... | collective-permute-start | bytes 196616 | tf_op jit(solution)/shard_map/ppermute | solution.py:558
  102.2 0.1 collective-permute-start.8
  102.3 1.5 collective-permute-done.7.refs_3_
  103.8 2.5 collective-permute-done.8.refs_4_
  106.4 0.9 shard_map.83
  107.2 5.4 %all-to-all-start.4 = ((f32[32,1,1152]{2,1,0:T(1,128)}), f32[32,1,1152]{2,1,0:T(1,128)S(1)}, u32[]{:S(2)}, u32[]{:S(2)}) async-start(f32[32,1,1152]{2,1,0:T(1,128)} %shard_map.83), calls=%async_computation.4 | async-start | bytes 294912 | tf_op jit(solution)/shard_map/all_to_all | solution.py:571
  112.7 3.5 %shard_map.82 = (f32[1024,128]{1,0:T(8,128)}, f32[1024,128]{1,0:T(8,128)}, bf16[256,128]{1,0:T(8,128)(2,1)}, bf16[256,128]{1,0:T(8,128)(2,1)}, bf16[256,128]{1,0:T(8,128)(2,1)}, /*index=5*/bf16[256,128]{1,0:T(8,128)(2,1)}) custom-call(s32[1]{0:T(128)} %bitcast.refs_0_, s32[1]{0:T(128)} %bitcast.1.refs_1_, ...), custom_call_target="tpu_custom_call" | custom-call | flops 268435456 | bytes 2621448 | tf_op jit(solution)/shard_map/pallas_call | solution.py:128
  116.2 1.9 collective-permute-start.9
  118.1 6.7 %collective-permute-start.10 = (bf16[256,128]{1,0:T(8,128)(2,1)}, bf16[256,128]{1,0:T(8,128)(2,1)S(1)}, u32[]{:S(2)}, u32[]{:S(2)}) collective-permute-start(bf16[256,128]{1,0:T(8,128)(2,1)} %get-tuple-element.116), channel_id=1, source_target_pairs={{1,0},{2,1},{3,2},{4,3},{5,4},{6,5},{7,6},{8,7},{9,8},{10,9},{11,1... | collective-permute-start | bytes 196616 | tf_op jit(solution)/shard_map/ppermute | solution.py:558
  124.8 2.2 collective-permute-start.11
  127.0 1.6 collective-permute-done.11.refs_10_.refs_11_
  128.7 2.3 collective-permute-done.12.refs_11_.refs_12_
  130.9 0.8 shard_map.84
  131.7 9.8 %all_to_all.56.refs_2_ = f32[16,8,128]{2,1,0:T(8,128)} all-to-all(f32[16,8,128]{2,1,0:T(8,128)S(1)} %get-tuple-element.123), channel_id=1, replica_groups=mesh['gx'=32,'gy'=16] {'gy'}, dimensions={0} | all-to-all | bytes 131072 | tf_op jit(solution)/shard_map/all_to_all | solution.py:571
  141.5 4.6 %shard_map.85 = (f32[1024,128]{1,0:T(8,128)}, f32[1024,128]{1,0:T(8,128)}, bf16[256,128]{1,0:T(8,128)(2,1)}, bf16[256,128]{1,0:T(8,128)(2,1)}, bf16[256,128]{1,0...) custom-call(s32[1]{0:T(128)} %bitcast.refs_0_, s32[1]{0:T(128)} %bitcast.1.refs_1_, ...), custom_call_target="tpu_custom_call" | custom-call | flops 268435456 | bytes 5341192 | tf_op jit(solution)/shard_map/pallas_call | solution.py:128
  146.0 3.5 %all-to-all-start.6 = ((f32[16,16,128]{2,1,0:T(8,128)}), f32[16,16,128]{2,1,0:T(8,128)S(1)}, u32[]{:S(2)}, u32[]{:S(2)}) async-start(f32[16,16,128]{2,1,0:T(8,128)} %get-tuple-element.135), calls=%async_computation.6 | async-start | bytes 262144 | tf_op jit(solution)/shard_map/all_to_all | solution.py:571
  149.6 3.1 %collective-permute-start.13 = (bf16[256,128]{1,0:T(8,128)(2,1)}, bf16[256,128]{1,0:T(8,128)(2,1)S(1)}, u32[]{:S(2)}, u32[]{:S(2)}) collective-permute-start(bf16[256,128]{1,0:T(8,128)(2,1)} %get-tuple-element.131), channel_id=1, source_target_pairs={{0,1},{1,2},{2,3},{3,4},{4,5},{5,6},{6,7},{7,8},{8,9},{9,10},{10,1... | collective-permute-start | bytes 196616 | tf_op jit(solution)/shard_map/ppermute | solution.py:558
  152.7 5.5 %collective-permute-start.14 = (bf16[256,128]{1,0:T(8,128)(2,1)}, bf16[256,128]{1,0:T(8,128)(2,1)S(1)}, u32[]{:S(2)}, u32[]{:S(2)}) collective-permute-start(bf16[256,128]{1,0:T(8,128)(2,1)} %get-tuple-element.132), channel_id=1, source_target_pairs={{1,0},{2,1},{3,2},{4,3},{5,4},{6,5},{7,6},{8,7},{9,8},{10,9},{11,1... | collective-permute-start | bytes 196616 | tf_op jit(solution)/shard_map/ppermute | solution.py:558
  158.2 3.7 %collective-permute-start.15 = (bf16[256,128]{1,0:T(8,128)(2,1)}, bf16[256,128]{1,0:T(8,128)(2,1)S(1)}, u32[]{:S(2)}, u32[]{:S(2)}) collective-permute-start(bf16[256,128]{1,0:T(8,128)(2,1)} %get-tuple-element.133), channel_id=1, source_target_pairs={{0,16},{16,32},{32,48},{48,64},{64,80},{80,96},{96,112},{112,128},... | collective-permute-start | bytes 196616 | tf_op jit(solution)/shard_map/ppermute | solution.py:558
  161.9 1.6 collective-permute-done.15.refs_3_
  163.5 2.3 collective-permute-done.16.refs_4_
  165.8 0.8 shard_map.87
  166.6 12.0 %all-to-all-start.7 = ((f32[32,1,1152]{2,1,0:T(1,128)}), f32[32,1,1152]{2,1,0:T(1,128)S(1)}, u32[]{:S(2)}, u32[]{:S(2)}) async-start(f32[32,1,1152]{2,1,0:T(1,128)} %shard_map.87), calls=%async_computation.7 | async-start | bytes 294912 | tf_op jit(solution)/shard_map/all_to_all | solution.py:571
  178.7 3.5 %shard_map.86 = (f32[1024,128]{1,0:T(8,128)}, f32[1024,128]{1,0:T(8,128)}, bf16[256,128]{1,0:T(8,128)(2,1)}, bf16[256,128]{1,0:T(8,128)(2,1)}, bf16[256,128]{1,0:T(8,128)(2,1)}, /*index=5*/bf16[256,128]{1,0:T(8,128)(2,1)}) custom-call(s32[1]{0:T(128)} %bitcast.refs_0_, s32[1]{0:T(128)} %bitcast.1.refs_1_, f32[1024,128]{1,0:T(8,128)} %get-tuple-element.130.refs_2_.refs_24_, ...), custom_call_target="tpu_custom_call" | custom-call | flops 268435456 | bytes 2883592 | tf_op jit(solution)/shard_map/pallas_call | solution.py:128
  182.2 1.9 collective-permute-start.17
  184.1 6.9 %collective-permute-start.18 = (bf16[256,128]{1,0:T(8,128)(2,1)}, bf16[256,128]{1,0:T(8,128)(2,1)S(1)}, u32[]{:S(2)}, u32[]{:S(2)}) collective-permute-start(bf16[256,128]{1,0:T(8,128)(2,1)} %get-tuple-element.141), channel_id=1, source_target_pairs={{1,0},{2,1},{3,2},{4,3},{5,4},{6,5},{7,6},{8,7},{9,8},{10,9},{11,1... | collective-permute-start | bytes 196616 | tf_op jit(solution)/shard_map/ppermute | solution.py:558
  191.0 2.2 collective-permute-start.19
  193.3 1.6 collective-permute-done.19.refs_16_
  194.9 2.3 collective-permute-done.20.refs_17_
  197.1 0.9 shard_map.88
  198.0 9.8 %all_to_all.57.refs_2_ = f32[16,8,128]{2,1,0:T(8,128)} all-to-all(f32[16,8,128]{2,1,0:T(8,128)S(1)} %shard_map.88), channel_id=1, replica_groups=mesh['gx'=32,'gy'=16] {'gy'}, dimensions={0} | all-to-all | bytes 131072 | tf_op jit(solution)/shard_map/all_to_all | solution.py:571
  207.8 4.5 %shard_map.89 = (f32[1024,128]{1,0:T(8,128)}, f32[1024,128]{1,0:T(8,128)}, bf16[256,128]{1,0:T(8,128)(2,1)}, bf16[256,128]{1,0:T(8,128)(2,1)}, bf16[256,128]{1,0...) custom-call(s32[1]{0:T(128)} %bitcast.refs_0_, s32[1]{0:T(128)} %bitcast.1.refs_1_, ...), custom_call_target="tpu_custom_call" | custom-call | flops 268435456 | bytes 7049224 | tf_op jit(solution)/shard_map/pallas_call | solution.py:128
  212.3 3.5 %all-to-all-start.9 = ((f32[16,16,128]{2,1,0:T(8,128)}), f32[16,16,128]{2,1,0:T(8,128)S(1)}, u32[]{:S(2)}, u32[]{:S(2)}) async-start(f32[16,16,128]{2,1,0:T(8,128)} %get-tuple-element.156), calls=%async_computation.9 | async-start | bytes 262144 | tf_op jit(solution)/shard_map/all_to_all | solution.py:571
  215.8 2.9 %collective-permute-start.21 = (bf16[256,128]{1,0:T(8,128)(2,1)}, bf16[256,128]{1,0:T(8,128)(2,1)S(1)}, u32[]{:S(2)}, u32[]{:S(2)}) collective-permute-start(bf16[256,128]{1,0:T(8,128)(2,1)} %get-tuple-element.157), channel_id=1, source_target_pairs={{0,16},{16,32},{32,48},{48,64},{64,80},{80,96},{96,112},{112,128},... | collective-permute-start | bytes 196616 | tf_op jit(solution)/shard_map/ppermute | solution.py:558
  218.8 1.6 collective-permute-done.21.refs_5_
  220.4 2.5 collective-permute-done.22.refs_6_
  223.0 0.7 shard_map.90
  223.7 14.3 %all-to-all-start.10 = ((f32[32,8,128]{2,1,0:T(8,128)}), f32[32,8,128]{2,1,0:T(8,128)S(1)}, u32[]{:S(2)}, u32[]{:S(2)}) async-start(f32[32,8,128]{2,1,0:T(8,128)} %shard_map.90), calls=%async_computation.10 | async-start | bytes 262144 | tf_op jit(solution)/shard_map/all_to_all | solution.py:571
  238.0 2.2 collective-permute-start.23
  240.2 6.4 %collective-permute-start.24 = (bf16[256,128]{1,0:T(8,128)(2,1)}, bf16[256,128]{1,0:T(8,128)(2,1)S(1)}, u32[]{:S(2)}, u32[]{:S(2)}) collective-permute-start(bf16[256,128]{1,0:T(8,128)(2,1)} %get-tuple-element.168), channel_id=1, source_target_pairs={{1,0},{2,1},{3,2},{4,3},{5,4},{6,5},{7,6},{8,7},{9,8},{10,9},{11,1... | collective-permute-start | bytes 196616 | tf_op jit(solution)/shard_map/ppermute | solution.py:558
  246.6 3.1 %shard_map.91 = (f32[1024,128]{1,0:T(8,128)}, f32[1024,128]{1,0:T(8,128)}, f32[1024,128]{1,0:T(8,128)}, f32[1024,128]{1,0:T(8,128)}) custom-call(f32[8,128]{1,0:T(8,128)} %get-tuple-element.149.refs_3_.refs_0_, f32[8,128]{1,0:T(8,128)} %get-tuple-element.163.refs_1_.refs_3_, f32[1024,128]{1,0:T(8,128)} %get-tuple-element.170.refs_2_, ...), custom_call_target="tpu_custom_call" | custom-call | flops 268435456 | bytes 2367488 | tf_op jit(solution)/shard_map/pallas_call | solution.py:128
  249.8 4.1 %all-to-all-done.10.refs_2_ = f32[32,8,128]{2,1,0:T(8,128)S(1)} async-done(((f32[32,8,128]{2,1,0:T(8,128)}), f32[32,8,128]{2,1,0:T(8,128)S(1)}, u32[]{:S(2)}, u32[]{:S(2)}) %all-to-all-start.10) | async-done | bytes 131104 | tf_op jit(solution)/shard_map/all_to_all | solution.py:571
  253.8 0.6 copy-done.4
  254.5 3.0 %shard_map.92 = (bf16[1024,128]{1,0:T(8,128)(2,1)}, bf16[1024,128]{1,0:T(8,128)(2,1)}) custom-call(s32[1]{0:T(128)} %bitcast.refs_0_, s32[1]{0:T(128)} %bitcast.1.refs_1_, f32[32,8,128]{2,1,0:T(8,128)} %copy-done.4, f32[8,128]{1,0:T(8,128)} %get-tuple-element.163.refs_1_.refs_3_, f32[1024,128]{1,0:T(8,128)} %get-tuple-element.164.refs_4_, ...), custom_call_target="tpu_custom_call" | custom-call | bytes 3543048 | tf_op jit(solution)/shard_map/pallas_call | solution.py:128
  (79 shorter events, 0.2 us)
Async XLA Ops:
  5.1 7.8 %copy-start.28 = (f32[272,128]{1,0:T(8,128)S(1)}, f32[272,128]{1,0:T(8,128)}, u32[]{:S(2)}) copy-start(f32[272,128]{1,0:T(8,128)} %get-tuple-element.90) | copy-start | bytes 417796
  5.1 11.1 %copy-start.27 = (f32[272,128]{1,0:T(8,128)S(1)}, f32[272,128]{1,0:T(8,128)}, u32[]{:S(2)}) copy-start(f32[272,128]{1,0:T(8,128)} %get-tuple-element.91) | copy-start | bytes 417796
  5.1 16.4 %copy-start.26 = (f32[272,128]{1,0:T(8,128)S(1)}, f32[272,128]{1,0:T(8,128)}, u32[]{:S(2)}) copy-start(f32[272,128]{1,0:T(8,128)} %get-tuple-element.92) | copy-start | bytes 417796
  5.1 19.4 %copy-start.25 = (f32[272,128]{1,0:T(8,128)S(1)}, f32[272,128]{1,0:T(8,128)}, u32[]{:S(2)}) copy-start(f32[272,128]{1,0:T(8,128)} %get-tuple-element.93) | copy-start | bytes 417796
  5.1 27.6 %all-to-all-start = ((bf16[16,288,128]{2,1,0:T(8,128)(2,1)}), bf16[16,288,128]{2,1,0:T(8,128)(2,1)S(1)}, u32[]{:S(2)}, u32[]{:S(2)}) async-start(bf16[16,288,128]{2,1,0:T(8,128)(2,1)} %get-tuple-element.94), calls=%async_computation | async-start | bytes 2359296 | tf_op jit(solution)/shard_map/all_to_all | solution.py:571
  12.9 19.8 %collective-permute-start = (f32[272,128]{1,0:T(8,128)S(1)}, f32[272,128]{1,0:T(8,128)S(1)}, u32[]{:S(2)}, u32[]{:S(2)}) collective-permute-start(f32[272,128]{1,0:T(8,128)S(1)} %copy-done.28), channel_id=1, source_target_pairs={{0,1},{1,2},{2,3},{3,4},{4,5},{5,6},{6,7},{7,8},{8,9},{9,10},{10,1... | collective-permute-start | bytes 417800 | tf_op jit(solution)/shard_map/ppermute | solution.py:558
  16.2 16.6 %collective-permute-start.1 = (f32[272,128]{1,0:T(8,128)S(1)}, f32[272,128]{1,0:T(8,128)S(1)}, u32[]{:S(2)}, u32[]{:S(2)}) collective-permute-start(f32[272,128]{1,0:T(8,128)S(1)} %copy-done.27), channel_id=1, source_target_pairs={{1,0},{2,1},{3,2},{4,3},{5,4},{6,5},{7,6},{8,7},{9,8},{10,9},{11,1... | collective-permute-start | bytes 417800 | tf_op jit(solution)/shard_map/ppermute | solution.py:558
  21.5 11.2 %collective-permute-start.2 = (f32[272,128]{1,0:T(8,128)S(1)}, f32[272,128]{1,0:T(8,128)S(1)}, u32[]{:S(2)}, u32[]{:S(2)}) collective-permute-start(f32[272,128]{1,0:T(8,128)S(1)} %copy-done.26), channel_id=1, source_target_pairs={{0,16},{16,32},{32,48},{48,64},{64,80},{80,96},{96,112},{112,128},... | collective-permute-start | bytes 417800 | tf_op jit(solution)/shard_map/ppermute | solution.py:558
  24.6 8.2 %collective-permute-start.3 = (f32[272,128]{1,0:T(8,128)S(1)}, f32[272,128]{1,0:T(8,128)S(1)}, u32[]{:S(2)}, u32[]{:S(2)}) collective-permute-start(f32[272,128]{1,0:T(8,128)S(1)} %copy-done.25), channel_id=1, source_target_pairs={{16,0},{32,16},{48,32},{64,48},{80,64},{96,80},{112,96},{128,112},... | collective-permute-start | bytes 417800 | tf_op jit(solution)/shard_map/ppermute | solution.py:558
  32.7 20.7 %copy-start = (f32[272,128]{1,0:T(8,128)}, f32[272,128]{1,0:T(8,128)S(1)}, u32[]{:S(2)}) copy-start(f32[272,128]{1,0:T(8,128)S(1)} %collective-permute-done.refs_5_.refs_7_.refs_8_) | copy-start | bytes 417796
  32.7 20.7 %copy-start.1 = (f32[272,128]{1,0:T(8,128)}, f32[272,128]{1,0:T(8,128)S(1)}, u32[]{:S(2)}) copy-start(f32[272,128]{1,0:T(8,128)S(1)} %collective-permute-done.1.refs_6_.refs_8_.refs_9_) | copy-start | bytes 417796
  32.7 20.7 %copy-start.2 = (f32[272,128]{1,0:T(8,128)}, f32[272,128]{1,0:T(8,128)S(1)}, u32[]{:S(2)}) copy-start(f32[272,128]{1,0:T(8,128)S(1)} %collective-permute-done.2.refs_3_.refs_5_.refs_6_) | copy-start | bytes 417796
  32.8 20.7 %copy-start.3 = (f32[272,128]{1,0:T(8,128)}, f32[272,128]{1,0:T(8,128)S(1)}, u32[]{:S(2)}) copy-start(f32[272,128]{1,0:T(8,128)S(1)} %collective-permute-done.3.refs_4_.refs_6_.refs_7_) | copy-start | bytes 417796
  32.8 37.1 %collective-permute-start.4 = (bf16[16,288,128]{2,1,0:T(8,128)(2,1)S(1)}, bf16[16,288,128]{2,1,0:T(8,128)(2,1)S(1)}, u32[]{:S(2)}, u32[]{:S(2)}) collective-permute-start(bf16[16,288,128]{2,1,0:T(8,128)(2,1)S(1)} %all-to-all-done.refs_0_.refs_2_), channel_id=1, source_target_pairs={{0,16},{16,0},{32,48},{48,32},{64,80},{80,64},{96,112},{112,96},{1... | collective-permute-start | bytes 3538952 | tf_op jit(solution)/shard_map/ppermute | solution.py:604
  37.9 32.0 %all-to-all-start.1 = ((f32[32,1,1152]{2,1,0:T(1,128)}), f32[32,1,1152]{2,1,0:T(1,128)S(1)}, u32[]{:S(2)}, u32[]{:S(2)}) async-start(f32[32,1,1152]{2,1,0:T(1,128)} %shard_map.78), calls=%async_computation.1 | async-start | bytes 294912 | tf_op jit(solution)/shard_map/all_to_all | solution.py:571
  86.4 19.9 %all-to-all-start.3 = ((f32[16,16,128]{2,1,0:T(8,128)}), f32[16,16,128]{2,1,0:T(8,128)S(1)}, u32[]{:S(2)}, u32[]{:S(2)}) async-start(f32[16,16,128]{2,1,0:T(8,128)} %get-tuple-element.110), calls=%async_computation.3 | async-start | bytes 262144 | tf_op jit(solution)/shard_map/all_to_all | solution.py:571
  90.0 12.3 %collective-permute-start.5 = (bf16[256,128]{1,0:T(8,128)(2,1)}, bf16[256,128]{1,0:T(8,128)(2,1)S(1)}, u32[]{:S(2)}, u32[]{:S(2)}) collective-permute-start(bf16[256,128]{1,0:T(8,128)(2,1)} %get-tuple-element.106), channel_id=1, source_target_pairs={{0,1},{1,2},{2,3},{3,4},{4,5},{5,6},{6,7},{7,8},{8,9},{9,10},{10,1... | collective-permute-start | bytes 196616 | tf_op jit(solution)/shard_map/ppermute | solution.py:558
  93.1 9.2 %collective-permute-start.6 = (bf16[256,128]{1,0:T(8,128)(2,1)}, bf16[256,128]{1,0:T(8,128)(2,1)S(1)}, u32[]{:S(2)}, u32[]{:S(2)}) collective-permute-start(bf16[256,128]{1,0:T(8,128)(2,1)} %get-tuple-element.107), channel_id=1, source_target_pairs={{1,0},{2,1},{3,2},{4,3},{5,4},{6,5},{7,6},{8,7},{9,8},{10,9},{11,1... | collective-permute-start | bytes 196616 | tf_op jit(solution)/shard_map/ppermute | solution.py:558
  98.6 5.2 %collective-permute-start.7 = (bf16[256,128]{1,0:T(8,128)(2,1)}, bf16[256,128]{1,0:T(8,128)(2,1)S(1)}, u32[]{:S(2)}, u32[]{:S(2)}) collective-permute-start(bf16[256,128]{1,0:T(8,128)(2,1)} %get-tuple-element.108), channel_id=1, source_target_pairs={{0,16},{16,32},{32,48},{48,64},{64,80},{80,96},{96,112},{112,128},... | collective-permute-start | bytes 196616 | tf_op jit(solution)/shard_map/ppermute | solution.py:558
  102.2 4.2 %collective-permute-start.8 = (bf16[256,128]{1,0:T(8,128)(2,1)}, bf16[256,128]{1,0:T(8,128)(2,1)S(1)}, u32[]{:S(2)}, u32[]{:S(2)}) collective-permute-start(bf16[256,128]{1,0:T(8,128)(2,1)} %get-tuple-element.109), channel_id=1, source_target_pairs={{16,0},{32,16},{48,32},{64,48},{80,64},{96,80},{112,96},{128,112},... | collective-permute-start | bytes 196616 | tf_op jit(solution)/shard_map/ppermute | solution.py:558
  102.3 10.4 %copy-start.15 = (bf16[256,128]{1,0:T(8,128)(2,1)}, bf16[256,128]{1,0:T(8,128)(2,1)S(1)}, u32[]{:S(2)}) copy-start(bf16[256,128]{1,0:T(8,128)(2,1)S(1)} %collective-permute-done.5.refs_5_) | copy-start | bytes 196612
  102.3 10.4 %copy-start.16 = (bf16[256,128]{1,0:T(8,128)(2,1)}, bf16[256,128]{1,0:T(8,128)(2,1)S(1)}, u32[]{:S(2)}) copy-start(bf16[256,128]{1,0:T(8,128)(2,1)S(1)} %collective-permute-done.6.refs_6_) | copy-start | bytes 196612
  103.8 8.9 %copy-start.17 = (bf16[256,128]{1,0:T(8,128)(2,1)}, bf16[256,128]{1,0:T(8,128)(2,1)S(1)}, u32[]{:S(2)}) copy-start(bf16[256,128]{1,0:T(8,128)(2,1)S(1)} %collective-permute-done.7.refs_3_) | copy-start | bytes 196612
  106.4 6.3 %copy-start.19 = (bf16[256,128]{1,0:T(8,128)(2,1)}, bf16[256,128]{1,0:T(8,128)(2,1)S(1)}, u32[]{:S(2)}) copy-start(bf16[256,128]{1,0:T(8,128)(2,1)S(1)} %collective-permute-done.8.refs_4_) | copy-start | bytes 196612
  107.2 23.7 %all-to-all-start.4 = ((f32[32,1,1152]{2,1,0:T(1,128)}), f32[32,1,1152]{2,1,0:T(1,128)S(1)}, u32[]{:S(2)}, u32[]{:S(2)}) async-start(f32[32,1,1152]{2,1,0:T(1,128)} %shard_map.83), calls=%async_computation.4 | async-start | bytes 294912 | tf_op jit(solution)/shard_map/all_to_all | solution.py:571
  116.2 10.8 %collective-permute-start.9 = (bf16[256,128]{1,0:T(8,128)(2,1)}, bf16[256,128]{1,0:T(8,128)(2,1)S(1)}, u32[]{:S(2)}, u32[]{:S(2)}) collective-permute-start(bf16[256,128]{1,0:T(8,128)(2,1)} %get-tuple-element.115), channel_id=1, source_target_pairs={{0,1},{1,2},{2,3},{3,4},{4,5},{5,6},{6,7},{7,8},{8,9},{9,10},{10,1... | collective-permute-start | bytes 196616 | tf_op jit(solution)/shard_map/ppermute | solution.py:558
  118.1 8.9 %collective-permute-start.10 = (bf16[256,128]{1,0:T(8,128)(2,1)}, bf16[256,128]{1,0:T(8,128)(2,1)S(1)}, u32[]{:S(2)}, u32[]{:S(2)}) collective-permute-start(bf16[256,128]{1,0:T(8,128)(2,1)} %get-tuple-element.116), channel_id=1, source_target_pairs={{1,0},{2,1},{3,2},{4,3},{5,4},{6,5},{7,6},{8,7},{9,8},{10,9},{11,1... | collective-permute-start | bytes 196616 | tf_op jit(solution)/shard_map/ppermute | solution.py:558
  124.8 3.9 %collective-permute-start.11 = (bf16[256,128]{1,0:T(8,128)(2,1)}, bf16[256,128]{1,0:T(8,128)(2,1)S(1)}, u32[]{:S(2)}, u32[]{:S(2)}) collective-permute-start(bf16[256,128]{1,0:T(8,128)(2,1)} %get-tuple-element.117), channel_id=1, source_target_pairs={{0,16},{16,32},{32,48},{48,64},{64,80},{80,96},{96,112},{112,128},... | collective-permute-start | bytes 196616 | tf_op jit(solution)/shard_map/ppermute | solution.py:558
  127.0 3.9 %collective-permute-start.12 = (bf16[256,128]{1,0:T(8,128)(2,1)}, bf16[256,128]{1,0:T(8,128)(2,1)S(1)}, u32[]{:S(2)}, u32[]{:S(2)}) collective-permute-start(bf16[256,128]{1,0:T(8,128)(2,1)} %get-tuple-element.118), channel_id=1, source_target_pairs={{16,0},{32,16},{48,32},{64,48},{80,64},{96,80},{112,96},{128,112},... | collective-permute-start | bytes 196616 | tf_op jit(solution)/shard_map/ppermute | solution.py:558
  127.0 14.4 %copy-start.5 = (bf16[256,128]{1,0:T(8,128)(2,1)}, bf16[256,128]{1,0:T(8,128)(2,1)S(1)}, u32[]{:S(2)}) copy-start(bf16[256,128]{1,0:T(8,128)(2,1)S(1)} %collective-permute-done.9.refs_12_.refs_13_) | copy-start | bytes 196612
  127.0 14.4 %copy-start.6 = (bf16[256,128]{1,0:T(8,128)(2,1)}, bf16[256,128]{1,0:T(8,128)(2,1)S(1)}, u32[]{:S(2)}) copy-start(bf16[256,128]{1,0:T(8,128)(2,1)S(1)} %collective-permute-done.10.refs_13_.refs_14_) | copy-start | bytes 196612
  128.7 12.8 %copy-start.7 = (bf16[256,128]{1,0:T(8,128)(2,1)}, bf16[256,128]{1,0:T(8,128)(2,1)S(1)}, u32[]{:S(2)}) copy-start(bf16[256,128]{1,0:T(8,128)(2,1)S(1)} %collective-permute-done.11.refs_10_.refs_11_) | copy-start | bytes 196612
  130.9 10.6 %copy-start.8 = (bf16[256,128]{1,0:T(8,128)(2,1)}, bf16[256,128]{1,0:T(8,128)(2,1)S(1)}, u32[]{:S(2)}) copy-start(bf16[256,128]{1,0:T(8,128)(2,1)S(1)} %collective-permute-done.12.refs_11_.refs_12_) | copy-start | bytes 196612
  146.0 19.7 %all-to-all-start.6 = ((f32[16,16,128]{2,1,0:T(8,128)}), f32[16,16,128]{2,1,0:T(8,128)S(1)}, u32[]{:S(2)}, u32[]{:S(2)}) async-start(f32[16,16,128]{2,1,0:T(8,128)} %get-tuple-element.135), calls=%async_computation.6 | async-start | bytes 262144 | tf_op jit(solution)/shard_map/all_to_all | solution.py:571
  149.6 12.3 %collective-permute-start.13 = (bf16[256,128]{1,0:T(8,128)(2,1)}, bf16[256,128]{1,0:T(8,128)(2,1)S(1)}, u32[]{:S(2)}, u32[]{:S(2)}) collective-permute-start(bf16[256,128]{1,0:T(8,128)(2,1)} %get-tuple-element.131), channel_id=1, source_target_pairs={{0,1},{1,2},{2,3},{3,4},{4,5},{5,6},{6,7},{7,8},{8,9},{9,10},{10,1... | collective-permute-start | bytes 196616 | tf_op jit(solution)/shard_map/ppermute | solution.py:558
  152.7 9.2 %collective-permute-start.14 = (bf16[256,128]{1,0:T(8,128)(2,1)}, bf16[256,128]{1,0:T(8,128)(2,1)S(1)}, u32[]{:S(2)}, u32[]{:S(2)}) collective-permute-start(bf16[256,128]{1,0:T(8,128)(2,1)} %get-tuple-element.132), channel_id=1, source_target_pairs={{1,0},{2,1},{3,2},{4,3},{5,4},{6,5},{7,6},{8,7},{9,8},{10,9},{11,1... | collective-permute-start | bytes 196616 | tf_op jit(solution)/shard_map/ppermute | solution.py:558
  158.2 5.3 %collective-permute-start.15 = (bf16[256,128]{1,0:T(8,128)(2,1)}, bf16[256,128]{1,0:T(8,128)(2,1)S(1)}, u32[]{:S(2)}, u32[]{:S(2)}) collective-permute-start(bf16[256,128]{1,0:T(8,128)(2,1)} %get-tuple-element.133), channel_id=1, source_target_pairs={{0,16},{16,32},{32,48},{48,64},{64,80},{80,96},{96,112},{112,128},... | collective-permute-start | bytes 196616 | tf_op jit(solution)/shard_map/ppermute | solution.py:558
  161.9 3.9 %collective-permute-start.16 = (bf16[256,128]{1,0:T(8,128)(2,1)}, bf16[256,128]{1,0:T(8,128)(2,1)S(1)}, u32[]{:S(2)}, u32[]{:S(2)}) collective-permute-start(bf16[256,128]{1,0:T(8,128)(2,1)} %get-tuple-element.134), channel_id=1, source_target_pairs={{16,0},{32,16},{48,32},{64,48},{80,64},{96,80},{112,96},{128,112},... | collective-permute-start | bytes 196616 | tf_op jit(solution)/shard_map/ppermute | solution.py:558
  161.9 16.8 %copy-start.21 = (bf16[256,128]{1,0:T(8,128)(2,1)}, bf16[256,128]{1,0:T(8,128)(2,1)S(1)}, u32[]{:S(2)}) copy-start(bf16[256,128]{1,0:T(8,128)(2,1)S(1)} %collective-permute-done.13.refs_5_) | copy-start | bytes 196612
  161.9 16.8 %copy-start.22 = (bf16[256,128]{1,0:T(8,128)(2,1)}, bf16[256,128]{1,0:T(8,128)(2,1)S(1)}, u32[]{:S(2)}) copy-start(bf16[256,128]{1,0:T(8,128)(2,1)S(1)} %collective-permute-done.14.refs_6_) | copy-start | bytes 196612
  163.5 15.2 %copy-start.23 = (bf16[256,128]{1,0:T(8,128)(2,1)}, bf16[256,128]{1,0:T(8,128)(2,1)S(1)}, u32[]{:S(2)}) copy-start(bf16[256,128]{1,0:T(8,128)(2,1)S(1)} %collective-permute-done.15.refs_3_) | copy-start | bytes 196612
  165.8 12.9 %copy-start.24 = (bf16[256,128]{1,0:T(8,128)(2,1)}, bf16[256,128]{1,0:T(8,128)(2,1)S(1)}, u32[]{:S(2)}) copy-start(bf16[256,128]{1,0:T(8,128)(2,1)S(1)} %collective-permute-done.16.refs_4_) | copy-start | bytes 196612
  166.6 30.5 %all-to-all-start.7 = ((f32[32,1,1152]{2,1,0:T(1,128)}), f32[32,1,1152]{2,1,0:T(1,128)S(1)}, u32[]{:S(2)}, u32[]{:S(2)}) async-start(f32[32,1,1152]{2,1,0:T(1,128)} %shard_map.87), calls=%async_computation.7 | async-start | bytes 294912 | tf_op jit(solution)/shard_map/all_to_all | solution.py:571
  182.2 11.0 %collective-permute-start.17 = (bf16[256,128]{1,0:T(8,128)(2,1)}, bf16[256,128]{1,0:T(8,128)(2,1)S(1)}, u32[]{:S(2)}, u32[]{:S(2)}) collective-permute-start(bf16[256,128]{1,0:T(8,128)(2,1)} %get-tuple-element.140), channel_id=1, source_target_pairs={{0,1},{1,2},{2,3},{3,4},{4,5},{5,6},{6,7},{7,8},{8,9},{9,10},{10,1... | collective-permute-start | bytes 196616 | tf_op jit(solution)/shard_map/ppermute | solution.py:558
  184.1 9.1 %collective-permute-start.18 = (bf16[256,128]{1,0:T(8,128)(2,1)}, bf16[256,128]{1,0:T(8,128)(2,1)S(1)}, u32[]{:S(2)}, u32[]{:S(2)}) collective-permute-start(bf16[256,128]{1,0:T(8,128)(2,1)} %get-tuple-element.141), channel_id=1, source_target_pairs={{1,0},{2,1},{3,2},{4,3},{5,4},{6,5},{7,6},{8,7},{9,8},{10,9},{11,1... | collective-permute-start | bytes 196616 | tf_op jit(solution)/shard_map/ppermute | solution.py:558
  191.0 3.9 %collective-permute-start.19 = (bf16[256,128]{1,0:T(8,128)(2,1)}, bf16[256,128]{1,0:T(8,128)(2,1)S(1)}, u32[]{:S(2)}, u32[]{:S(2)}) collective-permute-start(bf16[256,128]{1,0:T(8,128)(2,1)} %get-tuple-element.142), channel_id=1, source_target_pairs={{0,16},{16,32},{32,48},{48,64},{64,80},{80,96},{96,112},{112,128},... | collective-permute-start | bytes 196616 | tf_op jit(solution)/shard_map/ppermute | solution.py:558
  193.2 3.9 %collective-permute-start.20 = (bf16[256,128]{1,0:T(8,128)(2,1)}, bf16[256,128]{1,0:T(8,128)(2,1)S(1)}, u32[]{:S(2)}, u32[]{:S(2)}) collective-permute-start(bf16[256,128]{1,0:T(8,128)(2,1)} %get-tuple-element.143), channel_id=1, source_target_pairs={{16,0},{32,16},{48,32},{64,48},{80,64},{96,80},{112,96},{128,112},... | collective-permute-start | bytes 196616 | tf_op jit(solution)/shard_map/ppermute | solution.py:558
  193.2 14.5 %copy-start.9 = (bf16[256,128]{1,0:T(8,128)(2,1)}, bf16[256,128]{1,0:T(8,128)(2,1)S(1)}, u32[]{:S(2)}) copy-start(bf16[256,128]{1,0:T(8,128)(2,1)S(1)} %collective-permute-done.17.refs_18_) | copy-start | bytes 196612
  193.2 14.5 %copy-start.10 = (bf16[256,128]{1,0:T(8,128)(2,1)}, bf16[256,128]{1,0:T(8,128)(2,1)S(1)}, u32[]{:S(2)}) copy-start(bf16[256,128]{1,0:T(8,128)(2,1)S(1)} %collective-permute-done.18.refs_19_) | copy-start | bytes 196612
  194.9 12.9 %copy-start.11 = (bf16[256,128]{1,0:T(8,128)(2,1)}, bf16[256,128]{1,0:T(8,128)(2,1)S(1)}, u32[]{:S(2)}) copy-start(bf16[256,128]{1,0:T(8,128)(2,1)S(1)} %collective-permute-done.19.refs_16_) | copy-start | bytes 196612
  197.1 10.6 %copy-start.12 = (bf16[256,128]{1,0:T(8,128)(2,1)}, bf16[256,128]{1,0:T(8,128)(2,1)S(1)}, u32[]{:S(2)}) copy-start(bf16[256,128]{1,0:T(8,128)(2,1)S(1)} %collective-permute-done.20.refs_17_) | copy-start | bytes 196612
  212.3 10.7 %all-to-all-start.9 = ((f32[16,16,128]{2,1,0:T(8,128)}), f32[16,16,128]{2,1,0:T(8,128)S(1)}, u32[]{:S(2)}, u32[]{:S(2)}) async-start(f32[16,16,128]{2,1,0:T(8,128)} %get-tuple-element.156), calls=%async_computation.9 | async-start | bytes 262144 | tf_op jit(solution)/shard_map/all_to_all | solution.py:571
  215.8 4.6 %collective-permute-start.21 = (bf16[256,128]{1,0:T(8,128)(2,1)}, bf16[256,128]{1,0:T(8,128)(2,1)S(1)}, u32[]{:S(2)}, u32[]{:S(2)}) collective-permute-start(bf16[256,128]{1,0:T(8,128)(2,1)} %get-tuple-element.157), channel_id=1, source_target_pairs={{0,16},{16,32},{32,48},{48,64},{64,80},{80,96},{96,112},{112,128},... | collective-permute-start | bytes 196616 | tf_op jit(solution)/shard_map/ppermute | solution.py:558
  218.8 4.2 %collective-permute-start.22 = (bf16[256,128]{1,0:T(8,128)(2,1)}, bf16[256,128]{1,0:T(8,128)(2,1)S(1)}, u32[]{:S(2)}, u32[]{:S(2)}) collective-permute-start(bf16[256,128]{1,0:T(8,128)(2,1)} %get-tuple-element.158), channel_id=1, source_target_pairs={{16,0},{32,16},{48,32},{64,48},{80,64},{96,80},{112,96},{128,112},... | collective-permute-start | bytes 196616 | tf_op jit(solution)/shard_map/ppermute | solution.py:558
  220.4 29.3 %copy-start.13 = (bf16[256,128]{1,0:T(8,128)(2,1)}, bf16[256,128]{1,0:T(8,128)(2,1)S(1)}, u32[]{:S(2)}) copy-start(bf16[256,128]{1,0:T(8,128)(2,1)S(1)} %collective-permute-done.21.refs_5_) | copy-start | bytes 196612
  223.0 26.7 %copy-start.14 = (bf16[256,128]{1,0:T(8,128)(2,1)}, bf16[256,128]{1,0:T(8,128)(2,1)S(1)}, u32[]{:S(2)}) copy-start(bf16[256,128]{1,0:T(8,128)(2,1)S(1)} %collective-permute-done.22.refs_6_) | copy-start | bytes 196612
  223.7 30.1 %all-to-all-start.10 = ((f32[32,8,128]{2,1,0:T(8,128)}), f32[32,8,128]{2,1,0:T(8,128)S(1)}, u32[]{:S(2)}, u32[]{:S(2)}) async-start(f32[32,8,128]{2,1,0:T(8,128)} %shard_map.90), calls=%async_computation.10 | async-start | bytes 262144 | tf_op jit(solution)/shard_map/all_to_all | solution.py:571
  238.0 11.7 %collective-permute-start.23 = (bf16[256,128]{1,0:T(8,128)(2,1)}, bf16[256,128]{1,0:T(8,128)(2,1)S(1)}, u32[]{:S(2)}, u32[]{:S(2)}) collective-permute-start(bf16[256,128]{1,0:T(8,128)(2,1)} %get-tuple-element.167), channel_id=1, source_target_pairs={{0,1},{1,2},{2,3},{3,4},{4,5},{5,6},{6,7},{7,8},{8,9},{9,10},{10,1... | collective-permute-start | bytes 196616 | tf_op jit(solution)/shard_map/ppermute | solution.py:558
  240.2 9.6 %collective-permute-start.24 = (bf16[256,128]{1,0:T(8,128)(2,1)}, bf16[256,128]{1,0:T(8,128)(2,1)S(1)}, u32[]{:S(2)}, u32[]{:S(2)}) collective-permute-start(bf16[256,128]{1,0:T(8,128)(2,1)} %get-tuple-element.168), channel_id=1, source_target_pairs={{1,0},{2,1},{3,2},{4,3},{5,4},{6,5},{7,6},{8,7},{9,8},{10,9},{11,1... | collective-permute-start | bytes 196616 | tf_op jit(solution)/shard_map/ppermute | solution.py:558
  249.7 4.1 %copy-start.18 = (bf16[256,128]{1,0:T(8,128)(2,1)}, bf16[256,128]{1,0:T(8,128)(2,1)S(1)}, u32[]{:S(2)}) copy-start(bf16[256,128]{1,0:T(8,128)(2,1)S(1)} %collective-permute-done.23.refs_7_) | copy-start | bytes 196612
  249.7 4.1 %copy-start.20 = (bf16[256,128]{1,0:T(8,128)(2,1)}, bf16[256,128]{1,0:T(8,128)(2,1)S(1)}, u32[]{:S(2)}) copy-start(bf16[256,128]{1,0:T(8,128)(2,1)S(1)} %collective-permute-done.24.refs_8_) | copy-start | bytes 196612
  253.8 0.7 copy-start.4
